TPU v7x, 32 devices: a whole 2x2x4 slice. The times are simulated.
32 devices in a mesh: dp: 16 (over z, x, core), tensor: 2 (over y).
Axes of the slice: x: 2, y: 2, z: 4, core: 2. Of those that a mesh axis runs over, the one named last changes fastest.
Arguments:
- block_input: bfloat16 [32, 192, 2560], P(None, 'dp'), may hold values from -6 to 6
- cotangent: bfloat16 [32, 192, 2560], P(None, 'dp'), may hold values from -6 to 6
- seq_lengths: int32 [32], replicated, may hold values from 1 to 192, 4608 in all
- pre_gain: bfloat16 [2560], P('dp'), may hold values from -0.5 to 0.5
- w_branch: bfloat16 [2560, 2560], P('dp', 'tensor'), may hold values from -0.125 to 0.125
- b_branch: bfloat16 [10, 256], P('tensor', 'dp'), may hold values from -3 to 3
- w_recur: bfloat16 [2560, 2560], P('dp', 'tensor'), may hold values from -0.125 to 0.125
- b_recur: bfloat16 [10, 256], P('tensor', 'dp'), may hold values from -3 to 3
- conv_kernel: bfloat16 [4, 10, 256], P(None, 'tensor', 'dp'), may hold values from -3 to 3
- conv_bias: bfloat16 [10, 256], P('tensor', 'dp'), may hold values from -2 to 2
- input_gate_weight: bfloat16 [10, 256, 256], P('tensor', 'dp'), may hold values from -0.375 to 0.375
- input_gate_bias: bfloat16 [10, 256], P('tensor', 'dp'), may hold values from -3 to 3
- decay_gate_weight: bfloat16 [10, 256, 256], P('tensor', 'dp'), may hold values from -0.375 to 0.375
- decay_gate_bias: bfloat16 [10, 256], P('tensor', 'dp'), may hold values from -3 to 3
- decay_base: bfloat16 [10, 256], P('tensor', 'dp'), may hold values from -10 to -5
- w_output: bfloat16 [2560, 2560], P('dp', 'tensor'), may hold values from -0.5 to 0.5
- b_output: bfloat16 [2560], P('dp'), may hold values from -2 to 2
- ffn_gain: bfloat16 [2560], P('dp'), may hold values from -0.5 to 0.5
- w_expand: bfloat16 [2, 2560, 7680], P(None, 'dp', 'tensor'), may hold values from -0.125 to 0.125
- b_expand: bfloat16 [2, 30, 256], P(None, 'tensor', 'dp'), may hold values from -2 to 2
- w_shrink: bfloat16 [2560, 7680], P('dp', 'tensor'), may hold values from -0.125 to 0.125
- b_shrink: bfloat16 [2560], P('dp'), may hold values from -2 to 2
Outputs:
- block_output: bfloat16 [32, 192, 2560], P(None, 'dp')
- input_grad: bfloat16 [32, 192, 2560], P(None, 'dp')
- grad_pre_gain: float32 [2560], P('dp')
- grad_w_branch: float32 [2560, 2560], P('dp', 'tensor')
- grad_b_branch: float32 [10, 256], P('tensor', 'dp')
- grad_w_recur: float32 [2560, 2560], P('dp', 'tensor')
- grad_b_recur: float32 [10, 256], P('tensor', 'dp')
- grad_conv_kernel: float32 [4, 10, 256], P(None, 'tensor', 'dp')
- grad_conv_bias: float32 [10, 256], P('tensor', 'dp')
- grad_w_inlet: float32 [10, 256, 256], P('tensor', 'dp')
- grad_b_inlet: float32 [10, 256], P('tensor', 'dp')
- grad_w_decay: float32 [10, 256, 256], P('tensor', 'dp')
- grad_b_decay: float32 [10, 256], P('tensor', 'dp')
- grad_decay_base: float32 [10, 256], P('tensor', 'dp')
- grad_w_output: float32 [2560, 2560], P('dp', 'tensor')
- grad_b_output: float32 [2560], P('dp')
- grad_ffn_gain: float32 [2560], P('dp')
- grad_w_expand: float32 [2, 2560, 7680], P(None, 'dp', 'tensor')
- grad_b_expand: float32 [2, 30, 256], P(None, 'tensor', 'dp')
- grad_w_shrink: float32 [2560, 7680], P('dp', 'tensor')
- grad_b_shrink: float32 [2560], P('dp')
Inputs may be any that keep to these rules, and one draw needn't show every extreme that they name: `seq_lengths`: the longest sequence fills all 192 slots.
All inputs are finite; a program needn't handle non-finite values.
Results may differ from a plain program's by a relative error of at most 0.014.
Values may be sent and summed in bfloat16 or wider, within the bound.
No kernel may reach another device: no remote copies, remote signals or barrier semaphores. Data moves between devices by JAX's collectives and lax.ppermute only.
A program may use at most 576 MiB of HBM per device.

v0:
```python
import jax
import jax.numpy as jnp
from jax import lax
from jax.sharding import PartitionSpec as P


def rms_norm(values, gain_vec):
    return (
        values
        * lax.rsqrt(jnp.mean(values * values, axis=-1, keepdims=True) + 1e-06)
        * (1.0 + gain_vec)
    )


def causal_conv(values, kernel, offset_bias):
    taps = kernel.shape[0]
    length = values.shape[1]
    padded = jnp.pad(values, ((0, 0), (taps - 1, 0), (0, 0)))
    summed = offset_bias + jnp.zeros_like(values)
    for offset in range(taps):
        summed = summed + kernel[offset] * padded[:, taps - 1 - offset : taps - 1 - offset + length]
    return summed


def combine(earlier, later):
    return (earlier[0] * later[0], later[0] * earlier[1] + later[1])


def recurrence(decays, source):
    return lax.associative_scan(combine, (decays, source), axis=1)[1]


def lru_core(branch_pre, conv_out, input_preactivation, decay_preactivation, decay_vec):
    inlet_gate = jax.nn.sigmoid(input_preactivation)
    forget = jax.nn.sigmoid(decay_preactivation)
    log_decay = -8.0 * forget * jax.nn.softplus(decay_vec)
    decays = jnp.exp(log_decay)
    input_scale = jnp.sqrt(jnp.maximum(1.0 - jnp.exp(2.0 * log_decay), 0.001))
    first_row = lax.broadcasted_iota(jnp.int32, conv_out.shape, 1) == 0
    input_scale = jnp.where(first_row, 1.0, input_scale)
    states = recurrence(decays, conv_out * inlet_gate * input_scale)
    return jax.nn.gelu(branch_pre, approximate=True) * states


def glu_core(gate_pre, up_pre):
    return jax.nn.gelu(gate_pre, approximate=True) * up_pre


def matmul(left_op, right_op, formula):
    return jnp.einsum(formula, left_op, right_op, preferred_element_type=jnp.float32)


def row_total(values):
    return jnp.sum(values.astype(jnp.float32), axis=(0, 1))


def body(
    block_input,
    cotangent,
    seq_lengths,
    pre_gain,
    w_branch,
    b_branch,
    w_recur,
    b_recur,
    conv_kernel,
    conv_bias,
    input_gate_weight,
    input_gate_bias,
    decay_gate_weight,
    decay_gate_bias,
    decay_base,
    w_output,
    b_output,
    ffn_gain,
    w_expand,
    b_expand,
    w_shrink,
    b_shrink,
):
    groups = lax.axis_size("dp")
    group_index = lax.axis_index("dp")
    seq_count, piece_rows, model_width = block_input.shape
    batches = seq_count // groups
    length = piece_rows * groups
    shaped = (batches, groups, piece_rows, model_width)
    arrived, arrived_grad = (
        lax.all_to_all(block_input.reshape(shaped), "dp", split_axis=1, concat_axis=2, tiled=True),
        lax.all_to_all(cotangent.reshape(shaped), "dp", split_axis=1, concat_axis=2, tiled=True),
    )
    x_rows = arrived.reshape(batches, length, model_width).astype(jnp.float32)
    all_lengths = seq_lengths.reshape(batches, groups)
    own_length = lax.dynamic_slice_in_dim(all_lengths, group_index, 1, 1)
    row_mask = (lax.broadcasted_iota(jnp.int32, (batches, length), 1) < own_length).astype(
        jnp.float32
    )[..., None]
    (
        gain_one,
        branch_full,
        branch_offset,
        recur_full,
        recur_offset,
        kernel_full,
        conv_offset,
        inlet_full,
        inlet_offset,
        decay_full,
        decay_offset,
        base_full,
        output_full,
        output_offset,
    ) = (
        lax.all_gather(pre_gain, "dp", axis=0, tiled=True),
        lax.all_gather(w_branch, "dp", axis=0, tiled=True),
        lax.all_gather(b_branch, "dp", axis=1, tiled=True),
        lax.all_gather(w_recur, "dp", axis=0, tiled=True),
        lax.all_gather(b_recur, "dp", axis=1, tiled=True),
        lax.all_gather(conv_kernel, "dp", axis=2, tiled=True),
        lax.all_gather(conv_bias, "dp", axis=1, tiled=True),
        lax.all_gather(input_gate_weight, "dp", axis=1, tiled=True),
        lax.all_gather(input_gate_bias, "dp", axis=1, tiled=True),
        lax.all_gather(decay_gate_weight, "dp", axis=1, tiled=True),
        lax.all_gather(decay_gate_bias, "dp", axis=1, tiled=True),
        lax.all_gather(decay_base, "dp", axis=1, tiled=True),
        lax.all_gather(w_output, "dp", axis=0, tiled=True),
        lax.all_gather(b_output, "dp", axis=0, tiled=True),
    )
    head_count, head_size = inlet_offset.shape
    channels = head_count * head_size
    head_shape = (batches, length, channels)
    normed_f, pull_first = jax.vjp(rms_norm, x_rows, gain_one.astype(jnp.float32))
    normed = normed_f.astype(jnp.bfloat16)
    branch_pre = matmul(normed, branch_full, "bpd,dc->bpc") + branch_offset.astype(
        jnp.float32
    ).reshape(channels)
    recur_pre = matmul(normed, recur_full, "bpd,dc->bpc") + recur_offset.astype(
        jnp.float32
    ).reshape(channels)
    conv_out, pull_conv = jax.vjp(
        causal_conv,
        recur_pre,
        kernel_full.astype(jnp.float32).reshape(-1, channels),
        conv_offset.astype(jnp.float32).reshape(channels),
    )
    convolved_heads = conv_out.astype(jnp.bfloat16).reshape(batches, length, head_count, head_size)
    input_preactivation = (
        matmul(convolved_heads, inlet_full, "bphi,hio->bpho") + inlet_offset.astype(jnp.float32)
    ).reshape(head_shape)
    decay_preactivation = (
        matmul(convolved_heads, decay_full, "bphi,hio->bpho") + decay_offset.astype(jnp.float32)
    ).reshape(head_shape)
    mixed_f, pull_core = jax.vjp(
        lru_core,
        branch_pre,
        conv_out,
        input_preactivation,
        decay_preactivation,
        base_full.astype(jnp.float32).reshape(channels),
    )
    mixed = mixed_f.astype(jnp.bfloat16)
    branch_out = lax.psum(
        matmul(mixed, output_full, "bpc,dc->bpd"), "tensor"
    ) + output_offset.astype(jnp.float32)
    middle = x_rows + branch_out
    gain_two, expand_full, expand_offset, shrink_full, shrink_offset = (
        lax.all_gather(ffn_gain, "dp", axis=0, tiled=True),
        lax.all_gather(w_expand, "dp", axis=1, tiled=True),
        lax.all_gather(b_expand, "dp", axis=2, tiled=True),
        lax.all_gather(w_shrink, "dp", axis=0, tiled=True),
        lax.all_gather(b_shrink, "dp", axis=0, tiled=True),
    )
    second_f, pull_second = jax.vjp(rms_norm, middle, gain_two.astype(jnp.float32))
    second = second_f.astype(jnp.bfloat16)
    gate_pre = matmul(second, expand_full[0], "bpd,df->bpf") + expand_offset[0].astype(
        jnp.float32
    ).reshape(-1)
    up_pre = matmul(second, expand_full[1], "bpd,df->bpf") + expand_offset[1].astype(
        jnp.float32
    ).reshape(-1)
    hidden_f, pull_glu = jax.vjp(glu_core, gate_pre, up_pre)
    hidden = hidden_f.astype(jnp.bfloat16)
    ffn_out = lax.psum(
        matmul(hidden, shrink_full, "bpf,df->bpd").astype(jnp.bfloat16), "tensor"
    ).astype(jnp.float32) + shrink_offset.astype(jnp.float32)
    result = row_mask * (middle + ffn_out)
    upstream = arrived_grad.reshape(batches, length, model_width).astype(jnp.float32) * row_mask
    d_ffn = upstream.astype(jnp.bfloat16)
    expand_back, shrink_back = (
        lax.all_gather(w_expand, "dp", axis=1, tiled=True),
        lax.all_gather(w_shrink, "dp", axis=0, tiled=True),
    )
    grad_shrink_offset = row_total(d_ffn)
    grad_shrink = matmul(d_ffn, hidden, "bpd,bpf->df")
    d_hidden = matmul(d_ffn, shrink_back, "bpd,df->bpf")
    d_gate, d_up = pull_glu(d_hidden)
    d_gate_low = d_gate.astype(jnp.bfloat16)
    d_up_low = d_up.astype(jnp.bfloat16)
    grad_expand = jnp.stack(
        [matmul(second, d_gate_low, "bpd,bpf->df"), matmul(second, d_up_low, "bpd,bpf->df")]
    )
    grad_expand_offset = jnp.stack([row_total(d_gate_low), row_total(d_up_low)]).reshape(
        expand_offset.shape
    )
    d_second_part = matmul(d_gate_low, expand_back[0], "bpf,df->bpd") + matmul(
        d_up_low, expand_back[1], "bpf,df->bpd"
    )
    d_second = lax.psum(d_second_part, "tensor")
    d_middle_norm, grad_gain_two = pull_second(d_second)
    d_middle = upstream + d_middle_norm
    ffn_grads = (
        lax.psum_scatter(grad_gain_two, "dp", scatter_dimension=0, tiled=True),
        lax.psum_scatter(grad_expand, "dp", scatter_dimension=1, tiled=True),
        lax.psum_scatter(grad_expand_offset, "dp", scatter_dimension=2, tiled=True),
        lax.psum_scatter(grad_shrink, "dp", scatter_dimension=0, tiled=True),
        lax.psum_scatter(grad_shrink_offset, "dp", scatter_dimension=0, tiled=True),
    )
    d_branch = d_middle.astype(jnp.bfloat16)
    branch_back, recur_back, inlet_back, decay_back, output_back = (
        lax.all_gather(w_branch, "dp", axis=0, tiled=True),
        lax.all_gather(w_recur, "dp", axis=0, tiled=True),
        lax.all_gather(input_gate_weight, "dp", axis=1, tiled=True),
        lax.all_gather(decay_gate_weight, "dp", axis=1, tiled=True),
        lax.all_gather(w_output, "dp", axis=0, tiled=True),
    )
    grad_output_offset = row_total(d_branch)
    grad_output = matmul(d_branch, mixed, "bpd,bpc->dc")
    d_mixed = matmul(d_branch, output_back, "bpd,dc->bpc")
    d_branch_pre, d_conv_core, d_inlet, d_decay, grad_base = pull_core(d_mixed)
    head_form = (batches, length, head_count, head_size)
    d_inlet_low = d_inlet.astype(jnp.bfloat16).reshape(head_form)
    d_decay_low = d_decay.astype(jnp.bfloat16).reshape(head_form)
    grad_inlet = matmul(convolved_heads, d_inlet_low, "bphi,bpho->hio")
    grad_decay = matmul(convolved_heads, d_decay_low, "bphi,bpho->hio")
    grad_inlet_offset = row_total(d_inlet_low)
    grad_decay_offset = row_total(d_decay_low)
    d_conv_heads = matmul(d_inlet_low, inlet_back, "bpho,hio->bphi") + matmul(
        d_decay_low, decay_back, "bpho,hio->bphi"
    )
    d_conv = d_conv_core + d_conv_heads.reshape(head_shape)
    d_recur_pre, grad_kernel, grad_conv_offset = pull_conv(d_conv)
    d_branch_low = d_branch_pre.astype(jnp.bfloat16)
    d_recur_low = d_recur_pre.astype(jnp.bfloat16)
    grad_branch = matmul(normed, d_branch_low, "bpd,bpc->dc")
    grad_recur = matmul(normed, d_recur_low, "bpd,bpc->dc")
    d_first_part = matmul(d_branch_low, branch_back, "bpc,dc->bpd") + matmul(
        d_recur_low, recur_back, "bpc,dc->bpd"
    )
    d_first = lax.psum(d_first_part.astype(jnp.bfloat16), "tensor").astype(jnp.float32)
    d_input_norm, grad_gain_one = pull_first(d_first)
    d_input = d_middle + d_input_norm
    recur_grads = (
        lax.psum_scatter(grad_gain_one, "dp", scatter_dimension=0, tiled=True),
        lax.psum_scatter(grad_branch, "dp", scatter_dimension=0, tiled=True),
        lax.psum_scatter(
            row_total(d_branch_low).reshape(head_count, head_size),
            "dp",
            scatter_dimension=1,
            tiled=True,
        ),
        lax.psum_scatter(grad_recur, "dp", scatter_dimension=0, tiled=True),
        lax.psum_scatter(
            row_total(d_recur_low).reshape(head_count, head_size),
            "dp",
            scatter_dimension=1,
            tiled=True,
        ),
        lax.psum_scatter(
            grad_kernel.reshape(kernel_full.shape), "dp", scatter_dimension=2, tiled=True
        ),
        lax.psum_scatter(
            grad_conv_offset.reshape(head_count, head_size), "dp", scatter_dimension=1, tiled=True
        ),
        lax.psum_scatter(grad_inlet, "dp", scatter_dimension=1, tiled=True),
        lax.psum_scatter(grad_inlet_offset, "dp", scatter_dimension=1, tiled=True),
        lax.psum_scatter(grad_decay, "dp", scatter_dimension=1, tiled=True),
        lax.psum_scatter(grad_decay_offset, "dp", scatter_dimension=1, tiled=True),
        lax.psum_scatter(
            grad_base.reshape(head_count, head_size), "dp", scatter_dimension=1, tiled=True
        ),
        lax.psum_scatter(grad_output, "dp", scatter_dimension=0, tiled=True),
        lax.psum_scatter(grad_output_offset, "dp", scatter_dimension=0, tiled=True),
    )
    back_shape = (batches, 1, length, model_width)
    given_out, given_grad = (
        lax.all_to_all(
            result.astype(jnp.bfloat16).reshape(back_shape),
            "dp",
            split_axis=2,
            concat_axis=1,
            tiled=True,
        ),
        lax.all_to_all(
            d_input.astype(jnp.bfloat16).reshape(back_shape),
            "dp",
            split_axis=2,
            concat_axis=1,
            tiled=True,
        ),
    )
    given_out = given_out.reshape(seq_count, piece_rows, model_width)
    given_grad = given_grad.reshape(seq_count, piece_rows, model_width)
    return (given_out, given_grad) + tuple(recur_grads) + tuple(ffn_grads)


def solution(mesh):
    placed = (
        P(None, "dp", None),
        P(None, "dp", None),
        P(),
        P("dp"),
        P("dp", "tensor"),
        P("tensor", "dp"),
        P("dp", "tensor"),
        P("tensor", "dp"),
        P(None, "tensor", "dp"),
        P("tensor", "dp"),
        P("tensor", "dp", None),
        P("tensor", "dp"),
        P("tensor", "dp", None),
        P("tensor", "dp"),
        P("tensor", "dp"),
        P("dp", "tensor"),
        P("dp"),
        P("dp"),
        P(None, "dp", "tensor"),
        P(None, "tensor", "dp"),
        P("dp", "tensor"),
        P("dp"),
    )
    return jax.shard_map(
        body,
        mesh=mesh,
        in_specs=placed,
        out_specs=(
            P(None, "dp", None),
            P(None, "dp", None),
            P("dp"),
            P("dp", "tensor"),
            P("tensor", "dp"),
            P("dp", "tensor"),
            P("tensor", "dp"),
            P(None, "tensor", "dp"),
            P("tensor", "dp"),
            P("tensor", "dp", None),
            P("tensor", "dp"),
            P("tensor", "dp", None),
            P("tensor", "dp"),
            P("tensor", "dp"),
            P("dp", "tensor"),
            P("dp"),
            P("dp"),
            P(None, "dp", "tensor"),
            P(None, "tensor", "dp"),
            P("dp", "tensor"),
            P("dp"),
        ),
        check_vma=False,
    )
```

profile of v0, /device:TPU:9, one launch (start us, length us, event | category | flops | bytes accessed | tf_op | source)
XLA Modules:
  0.0 3374.0 jit_solution(2379951959126929002)
XLA Ops:
  8.7 4.8 copy.149
  13.6 6.7 all-to-all-start
  21.3 86.9 %all-gather = bf16[16,16,5]{1,2,0:T(8,128)(2,1)S(1)} all-gather(bf16[1,16,5]{1,2,0:T(8,128)(2,1)S(1)} %bitcast.233), channel_id=1, replica_groups=mesh['dp'=16,'tensor'=2] {'dp'}, dimensions={0}, use_global_device_ids=true | all-gather | bytes 2720 | tf_op jit(solution)/shard_map/all_gather | solution.py:115
  108.3 16.2 all-gather.2
  124.7 17.7 all-gather.1
  142.4 19.3 all-gather.3
  161.8 17.7 all-gather.4
  179.6 19.0 all-gather.5
  199.3 19.3 all_gather.68
  221.6 49.2 %all-reduce.86 = (bf16[2560]{0:T(1024)(128)(2,1)S(1)}, bf16[2560]{0:T(1024)(128)(2,1)S(1)}, bf16[2560]{0:T(1024)(128)(2,1)S(1)}, bf16[2560]{0:T(1024)(128)(2,1)}) all-reduce(bf16[2560]{0:T(1024)(128)(2,1)S(1)} %dynamic-update-slice, bf16[2560]{0:T(1024)(128)(2,1)S(1)} %dynamic-update-slice.1, ...), channel_id=1, replica_groups=mesh['dp'=16,'tensor'=2] {'dp'}, use_global_device_ids=true, to_apply=%add.77 | all-reduce | flops 10240 | bytes 40960
  271.5 30.7 all_gather.71
  302.2 22.4 all_gather.73
  332.4 5.6 fusion.50
  358.4 5.8 fusion.74
  364.1 4.1 slice.268
  368.3 5.8 slice.272
  374.0 5.4 slice.267
  411.7 9.6 multiply_convert_fusion.6
  421.3 7.9 fusion.10
  434.0 6.7 all-to-all-start.2
  441.0 55.2 %all_gather.80 = bf16[2,15,256]{1,0,2:T(2,128)(2,1)S(1)} all-gather(bf16[2,15,16]{1,0,2:T(2,128)(2,1)S(1)} %copy.172), channel_id=1, replica_groups=mesh['dp'=16,'tensor'=2] {'dp'}, dimensions={2}, use_global_device_ids=true | all-gather | bytes 16320 | tf_op jit(solution)/shard_map/all_gather | solution.py:168
  500.4 31.3 all-reduce.92.cloned.1.call-done
  531.7 4.2 multiply_reduce_fusion.2
  538.2 190.6 %all-gather.18.cloned.1.call-done = bf16[2,2560,3840]{2,1,0:T(8,128)(2,1)} async-done(((bf16[2,160,3840]{2,1,0:T(8,128)(2,1)}), bf16[2,2560,3840]{2,1,0:T(8,128)(2,1)}) %all-gather.18.cloned.1.call-update) | async-done | bytes 39321616 | tf_op jit(solution)/shard_map/all_gather | solution.py:167
  728.8 14.1 fusion.27
  742.9 14.1 fusion.28
  757.0 76.1 %all-gather.20.cloned.1.call-done = bf16[2560,3840]{1,0:T(8,128)(2,1)} async-done(((bf16[160,3840]{1,0:T(8,128)(2,1)}), bf16[2560,3840]{1,0:T(8,128)(2,1)}) %all-gather.20.cloned.1.call-update) | async-done | bytes 19660816 | tf_op jit(solution)/shard_map/all_gather | solution.py:169
  833.1 21.6 convert_reduce_fusion
  854.7 14.2 fusion.4
  868.8 14.5 fusion.34
  883.4 14.2 fusion.35
  897.6 88.4 %all-reduce.94.cloned.1.call-done = f32[2,192,2560]{2,1,0:T(8,128)} async-done(((f32[2,192,2560]{2,1,0:T(8,128)}), f32[2,192,2560]{2,1,0:T(8,128)}) %all-reduce.94.cloned.1.call-update) | async-done | bytes 3932176 | tf_op jit(solution)/shard_map/psum | solution.py:207
  986.0 5.1 multiply_reduce_fusion
  991.6 4.3 convert_reduce_fusion.3
  996.0 4.8 convert_reduce_fusion.7
  1003.0 5.5 slice.323
  1012.4 4.1 slice.324
  1055.1 4.5 multiply_add_fusion.3
  1078.1 6.4 multiply_reduce_fusion.4
  1100.0 6.8 multiply_reduce_fusion.8
  1130.2 10.7 convolution_bitcast_fusion.3
  1142.8 6.6 convolution_bitcast_fusion.5
  1150.6 6.7 convolution_bitcast_fusion.4
  1159.1 20.3 convolution_bitcast_fusion
  1181.0 18.0 convolution_bitcast_fusion.1
  1199.1 16.8 convolution_bitcast_fusion.2
  1215.9 51.6 %pad_maximum_fusion = f32[2,2560,3840]{2,1,0:T(8,128)} fusion(f32[1,2560,3840]{2,1,0:T(8,128)} %convolution_bitcast_fusion.1, f32[1,2560,3840]{2,1,0:T(8,128)} %convolution_bitcast_fusion.2), kind=kLoop, calls=%fused_computation | loop fusion | flops 19660800 | bytes 157286400 | tf_op jit(solution)/shard_map/stack | solution.py:198
  1268.2 4.4 fusion.42
  1279.9 6.8 all-to-all-start.3
  1292.9 37.6 %all-to-all-done.3 = bf16[2,1,192,2560]{3,0,1,2:T(2,128)(2,1)} async-done(((bf16[2,1,192,2560]{3,0,1,2:T(2,128)(2,1)}), bf16[2,1,192,2560]{3,0,1,2:T(2,128)(2,1)}, u32[]{:S(2)}, u32[]{:S(2)}) %all-to-all-start.3) | async-done | bytes 1966112 | tf_op jit(solution)/shard_map/all_to_all | solution.py:292
  1330.6 6.2 all-to-all-start.1
  1343.4 66.7 %reduce-scatter.54.cloned.1.call-done = f32[16,5]{1,0:T(8,128)} async-done(((f32[256,5]{1,0:T(8,128)}), f32[16,5]{1,0:T(8,128)}) %reduce-scatter.54.cloned.1.call-update) | async-done | bytes 336
  1411.4 56.5 %reduce-scatter.56.cloned.1.call-done = f32[16,5]{1,0:T(8,128)} async-done(((f32[256,5]{1,0:T(8,128)}), f32[16,5]{1,0:T(8,128)}) %reduce-scatter.56.cloned.1.call-update) | async-done | bytes 336
  1469.3 56.7 %reduce-scatter.58.cloned.1.call-done = f32[16,5]{1,0:T(8,128)} async-done(((f32[256,5]{1,0:T(8,128)}), f32[16,5]{1,0:T(8,128)}) %reduce-scatter.58.cloned.1.call-update) | async-done | bytes 336
  1527.3 56.5 %reduce-scatter.52.cloned.1.call-done = f32[16,5]{1,0:T(8,128)} async-done(((f32[256,5]{1,0:T(8,128)}), f32[16,5]{1,0:T(8,128)}) %reduce-scatter.52.cloned.1.call-update) | async-done | bytes 336
  1585.2 56.5 %reduce-scatter.48.cloned.1.call-done = f32[16,5]{1,0:T(8,128)} async-done(((f32[256,5]{1,0:T(8,128)}), f32[16,5]{1,0:T(8,128)}) %reduce-scatter.48.cloned.1.call-update) | async-done | bytes 336
  1643.1 56.5 %reduce-scatter.50.cloned.1.call-done = f32[16,20]{1,0:T(8,128)} async-done(((f32[256,20]{1,0:T(8,128)}), f32[16,20]{1,0:T(8,128)}) %reduce-scatter.50.cloned.1.call-update) | async-done | bytes 1296
  1701.1 48.4 %all-reduce.85 = (f32[2560]{0:T(1024)S(1)}, f32[2560]{0:T(1024)S(1)}, f32[2560]{0:T(1024)S(1)}, f32[2560]{0:T(1024)S(1)}) all-reduce(f32[2560]{0:T(1024)S(1)} %get-tuple-element.107, f32[2560]{0:T(1024)S(1)} %copy-done.128, f32[2560]{0:T(1024)S(1)} %copy-done.127, ...), channel_id=2, replica_groups=mesh['dp'=16,'tensor'=2] {'dp'}, use_global_device_ids=true, to_apply=%region_9.10.clone | all-reduce | flops 10240 | bytes 81920
  1767.8 55.4 %reduce-scatter.36.cloned.1.call-done = f32[5,16,256]{2,1,0:T(8,128)} async-done(((f32[5,256,256]{2,1,0:T(8,128)}), f32[5,16,256]{2,1,0:T(8,128)}) %reduce-scatter.36.cloned.1.call-update) | async-done | bytes 81936 | tf_op jit(solution)/shard_map/reduce_scatter | solution.py:273
  1823.2 143.7 %reduce-scatter.40.cloned.1.call-done = f32[160,1280]{1,0:T(8,128)} async-done(((f32[2560,1280]{1,0:T(8,128)}), f32[160,1280]{1,0:T(8,128)}) %reduce-scatter.40.cloned.1.call-update) | async-done | bytes 819216 | tf_op jit(solution)/shard_map/reduce_scatter | solution.py:280
  1966.9 142.1 %reduce-scatter.32.cloned.1.call-done = f32[160,1280]{1,0:T(8,128)} async-done(((f32[2560,1280]{1,0:T(8,128)}), f32[160,1280]{1,0:T(8,128)}) %reduce-scatter.32.cloned.1.call-update) | async-done | bytes 819216 | tf_op jit(solution)/shard_map/reduce_scatter | solution.py:253
  2109.0 142.8 %reduce-scatter.34.cloned.1.call-done = f32[160,1280]{1,0:T(8,128)} async-done(((f32[2560,1280]{1,0:T(8,128)}), f32[160,1280]{1,0:T(8,128)}) %reduce-scatter.34.cloned.1.call-update) | async-done | bytes 819216 | tf_op jit(solution)/shard_map/reduce_scatter | solution.py:260
  2251.8 383.2 %reduce-scatter.44.cloned.1.call-done = f32[160,3840]{1,0:T(8,128)} async-done(((f32[2560,3840]{1,0:T(8,128)}), f32[160,3840]{1,0:T(8,128)}) %reduce-scatter.44.cloned.1.call-update) | async-done | bytes 2457616 | tf_op jit(solution)/shard_map/reduce_scatter | solution.py:214
  2635.0 732.2 %reduce-scatter.42.cloned.1.call-done = f32[2,160,3840]{2,1,0:T(8,128)} async-done(((f32[2,2560,3840]{2,1,0:T(8,128)}), f32[2,160,3840]{2,1,0:T(8,128)}) %reduce-scatter.42.cloned.1.call-update) | async-done | bytes 4915216 | tf_op jit(solution)/shard_map/reduce_scatter | solution.py:212
  (696 shorter events, 231.8 us)
Async XLA Ops:
  7.2 323.9 %all-gather.14.cloned.1.call-start = ((), (), s32[]{:S(2)}) async-start(), calls=%async_computation.20 | async-start | bytes 6963200 | tf_op jit(solution)/shard_map/all_gather | solution.py:116
  7.9 403.7 %all-gather.12.cloned.1.call-start = ((), (), s32[]{:S(2)}) async-start(), calls=%async_computation.19 | async-start | bytes 6963200 | tf_op jit(solution)/shard_map/all_gather | solution.py:114
  13.5 94.8 %copy-start.144 = (bf16[5,16]{1,0:T(8,128)(2,1)S(1)}, bf16[5,16]{1,0:T(8,128)(2,1)}, u32[]{:S(2)}) copy-start(bf16[5,16]{1,0:T(8,128)(2,1)} %param.29) | copy-start | bytes 484
  13.5 111.1 %copy-start.145 = (bf16[5,16]{1,0:T(8,128)(2,1)S(1)}, bf16[5,16]{1,0:T(8,128)(2,1)}, u32[]{:S(2)}) copy-start(bf16[5,16]{1,0:T(8,128)(2,1)} %param.31) | copy-start | bytes 484
  13.5 128.9 %copy-start.146 = (bf16[5,16]{1,0:T(8,128)(2,1)S(1)}, bf16[5,16]{1,0:T(8,128)(2,1)}, u32[]{:S(2)}) copy-start(bf16[5,16]{1,0:T(8,128)(2,1)} %param.33) | copy-start | bytes 484
  13.5 148.2 %copy-start.147 = (bf16[5,16]{1,0:T(8,128)(2,1)S(1)}, bf16[5,16]{1,0:T(8,128)(2,1)}, u32[]{:S(2)}) copy-start(bf16[5,16]{1,0:T(8,128)(2,1)} %param.35) | copy-start | bytes 484
  13.5 166.1 %copy-start.148 = (bf16[5,16]{1,0:T(8,128)(2,1)S(1)}, bf16[5,16]{1,0:T(8,128)(2,1)}, u32[]{:S(2)}) copy-start(bf16[5,16]{1,0:T(8,128)(2,1)} %param.36) | copy-start | bytes 484
  13.6 311.0 %all-to-all-start = ((bf16[2,16,12,2560]{3,0,2,1:T(2,128)(2,1)}), bf16[2,16,12,2560]{3,0,2,1:T(2,128)(2,1)S(1)}, u32[]{:S(2)}, u32[]{:S(2)}) async-start(bf16[2,16,12,2560]{3,0,2,1:T(2,128)(2,1)} %copy.149), calls=%async_computation | async-start | bytes 3932160 | tf_op jit(solution)/shard_map/all_to_all | solution.py:88
  20.3 199.0 %copy-start.149 = (u32[32]{0:T(128)S(1)}, u32[32]{0:T(128)}, u32[]{:S(2)}) copy-start(u32[32]{0:T(128)} %constant.230) | copy-start | bytes 388
  20.3 200.3 %copy-start.150 = (bf16[160]{0:T(256)(128)(2,1)S(1)}, bf16[160]{0:T(256)(128)(2,1)}, u32[]{:S(2)}) copy-start(bf16[160]{0:T(256)(128)(2,1)} %param.39) | copy-start | bytes 964
  20.3 200.6 %copy-start.151 = (bf16[160]{0:T(256)(128)(2,1)S(1)}, bf16[160]{0:T(256)(128)(2,1)}, u32[]{:S(2)}) copy-start(bf16[160]{0:T(256)(128)(2,1)} %param.38) | copy-start | bytes 964
  20.3 200.8 %copy-start.152 = (bf16[160]{0:T(256)(128)(2,1)S(1)}, bf16[160]{0:T(256)(128)(2,1)}, u32[]{:S(2)}) copy-start(bf16[160]{0:T(256)(128)(2,1)} %param.25) | copy-start | bytes 964
  20.3 201.0 %copy-start.153 = (bf16[160]{0:T(256)(128)(2,1)S(1)}, bf16[160]{0:T(256)(128)(2,1)}, u32[]{:S(2)}) copy-start(bf16[160]{0:T(256)(128)(2,1)} %param.43) | copy-start | bytes 964
  20.3 251.1 %copy-start.129 = (bf16[5,16,256]{2,1,0:T(8,128)(2,1)S(1)}, bf16[5,16,256]{2,1,0:T(8,128)(2,1)}, u32[]{:S(2)}) copy-start(bf16[5,16,256]{2,1,0:T(8,128)(2,1)} %param.32) | copy-start | bytes 122884
  20.4 400.9 %all-gather.16.cloned.1.call-start = ((), (), s32[]{:S(2)}) async-start(), calls=%async_computation.21 | async-start | bytes 6963200 | tf_op jit(solution)/shard_map/all_gather | solution.py:125
  21.1 281.1 %copy-start.130 = (bf16[5,16,256]{2,1,0:T(8,128)(2,1)S(1)}, bf16[5,16,256]{2,1,0:T(8,128)(2,1)}, u32[]{:S(2)}) copy-start(bf16[5,16,256]{2,1,0:T(8,128)(2,1)} %param.34) | copy-start | bytes 122884
  21.1 510.6 %all-reduce.92.cloned.1.call-start = ((), (), s32[]{:S(2)}) async-start(), calls=%async_computation.22 | async-start | bytes 7864320 | tf_op jit(solution)/shard_map/psum | solution.py:161
  219.0 118.9 %copy-start.117 = (f32[1280]{0:T(1024)}, f32[1280]{0:T(1024)S(1)}, u32[]{:S(2)}) copy-start(f32[1280]{0:T(1024)S(1)} %mul.582) | copy-start | bytes 15364
  219.1 118.9 %copy-start.119 = (f32[1280]{0:T(1024)}, f32[1280]{0:T(1024)S(1)}, u32[]{:S(2)}) copy-start(f32[1280]{0:T(1024)S(1)} %mul.585) | copy-start | bytes 15364
  219.2 118.8 %copy-start.121 = (f32[1280]{0:T(1024)}, f32[1280]{0:T(1024)S(1)}, u32[]{:S(2)}) copy-start(f32[1280]{0:T(1024)S(1)} %mul.588) | copy-start | bytes 15364
  219.3 118.7 %copy-start.123 = (f32[1280]{0:T(1024)}, f32[1280]{0:T(1024)S(1)}, u32[]{:S(2)}) copy-start(f32[1280]{0:T(1024)S(1)} %mul.591) | copy-start | bytes 15364
  270.8 87.5 %copy-start.136 = (pred[192]{0:T(512)(128)(4,1)}, pred[192]{0:T(512)(128)(4,1)S(1)}, u32[]{:S(2)}) copy-start(pred[192]{0:T(512)(128)(4,1)S(1)} %iota_compare_fusion) | copy-start | bytes 580
  270.8 57.6 %copy-start.110 = (f32[2560]{0:T(1024)}, f32[2560]{0:T(1024)S(1)}, u32[]{:S(2)}) copy-start(f32[2560]{0:T(1024)S(1)} %convert_add_fusion.1) | copy-start | bytes 30724
  271.5 86.9 %copy-start.108 = (f32[1280]{0:T(1024)}, f32[1280]{0:T(1024)S(1)}, u32[]{:S(2)}) copy-start(f32[1280]{0:T(1024)S(1)} %get-tuple-element.237) | copy-start | bytes 15364
  348.6 9.8 copy-start.4
  368.2 19.8 copy-start.15
  368.2 11.2 copy-start.17
  391.0 11.1 copy-start.34
  429.2 299.7 %all-gather.18.cloned.1.call-start = ((), (), s32[]{:S(2)}) async-start(), calls=%async_computation.23 | async-start | bytes 41779200 | tf_op jit(solution)/shard_map/all_gather | solution.py:167
  429.8 403.3 %all-gather.20.cloned.1.call-start = ((), (), s32[]{:S(2)}) async-start(), calls=%async_computation.24 | async-start | bytes 20889600 | tf_op jit(solution)/shard_map/all_gather | solution.py:169
  434.0 63.0 %all-to-all-start.2 = ((bf16[2,16,12,2560]{3,0,2,1:T(2,128)(2,1)}), bf16[2,16,12,2560]{3,0,2,1:T(2,128)(2,1)S(1)}, u32[]{:S(2)}, u32[]{:S(2)}) async-start(bf16[2,16,12,2560]{3,0,2,1:T(2,128)(2,1)} %copy.177), calls=%async_computation.2 | async-start | bytes 3932160 | tf_op jit(solution)/shard_map/all_to_all | solution.py:89
  440.8 545.2 %all-reduce.94.cloned.1.call-start = ((), (), s32[]{:S(2)}) async-start(), calls=%async_computation.25 | async-start | bytes 7864320 | tf_op jit(solution)/shard_map/psum | solution.py:207
  538.2 204.7 %copy-start.71 = (bf16[2,192,2560]{2,1,0:T(8,128)(2,1)}, bf16[2,192,2560]{2,1,0:T(8,128)(2,1)S(1)}, u32[]{:S(2)}) copy-start(bf16[2,192,2560]{2,1,0:T(8,128)(2,1)S(1)} %multiply_convert_fusion.4) | copy-start | bytes 5898244
  854.7 14.2 copy-start.161
  883.4 384.2 %all-reduce.96.cloned.1.call-start = ((), (), s32[]{:S(2)}) async-start(), calls=%async_computation.41 | async-start | bytes 7864320 | tf_op jit(solution)/shard_map/psum | solution.py:182
  986.0 9.9 slice-start.4
  1044.8 8.2 copy-start.74
  1046.9 8.2 copy-start.16
  1046.9 8.2 copy-start.23
  1046.9 8.2 copy-start.24
  1100.0 8.3 slice-start
  1115.4 224.3 %reduce-scatter.60.cloned.1.call-start = ((), (), s32[]{:S(2)}) async-start(), calls=%async_computation.40 | async-start | bytes 139264
  1116.5 225.5 %reduce-scatter.46.cloned.1.call-start = ((), (), s32[]{:S(2)}) async-start(), calls=%async_computation.33 | async-start | bytes 139264
  1117.4 292.7 %reduce-scatter.54.cloned.1.call-start = ((), (), s32[]{:S(2)}) async-start(), calls=%async_computation.37 | async-start | bytes 139264
  1117.4 8.1 copy-start.19
  1118.3 349.7 %reduce-scatter.56.cloned.1.call-start = ((), (), s32[]{:S(2)}) async-start(), calls=%async_computation.38 | async-start | bytes 139264
  1119.2 406.8 %reduce-scatter.58.cloned.1.call-start = ((), (), s32[]{:S(2)}) async-start(), calls=%async_computation.39 | async-start | bytes 139264
  1120.1 463.8 %reduce-scatter.52.cloned.1.call-start = ((), (), s32[]{:S(2)}) async-start(), calls=%async_computation.36 | async-start | bytes 139264
  1121.0 520.8 %reduce-scatter.48.cloned.1.call-start = ((), (), s32[]{:S(2)}) async-start(), calls=%async_computation.34 | async-start | bytes 139264
  1121.9 577.7 %reduce-scatter.50.cloned.1.call-start = ((), (), s32[]{:S(2)}) async-start(), calls=%async_computation.35 | async-start | bytes 139264
  1125.4 642.3 %reduce-scatter.38.cloned.1.call-start = ((), (), s32[]{:S(2)}) async-start(), calls=%async_computation.29 | async-start | bytes 1392640 | tf_op jit(solution)/shard_map/reduce_scatter | solution.py:275
  1128.5 694.7 %reduce-scatter.36.cloned.1.call-start = ((), (), s32[]{:S(2)}) async-start(), calls=%async_computation.28 | async-start | bytes 1392640 | tf_op jit(solution)/shard_map/reduce_scatter | solution.py:273
  1130.2 836.7 %reduce-scatter.40.cloned.1.call-start = ((), (), s32[]{:S(2)}) async-start(), calls=%async_computation.30 | async-start | bytes 13926400 | tf_op jit(solution)/shard_map/reduce_scatter | solution.py:280
  1141.0 968.0 %reduce-scatter.32.cloned.1.call-start = ((), (), s32[]{:S(2)}) async-start(), calls=%async_computation.26 | async-start | bytes 13926400 | tf_op jit(solution)/shard_map/reduce_scatter | solution.py:253
  1149.4 1102.4 %reduce-scatter.34.cloned.1.call-start = ((), (), s32[]{:S(2)}) async-start(), calls=%async_computation.27 | async-start | bytes 13926400 | tf_op jit(solution)/shard_map/reduce_scatter | solution.py:260
  1157.3 1477.7 %reduce-scatter.44.cloned.1.call-start = ((), (), s32[]{:S(2)}) async-start(), calls=%async_computation.32 | async-start | bytes 41779200 | tf_op jit(solution)/shard_map/reduce_scatter | solution.py:214
  1179.5 2187.7 %reduce-scatter.42.cloned.1.call-start = ((), (), s32[]{:S(2)}) async-start(), calls=%async_computation.31 | async-start | bytes 83558400 | tf_op jit(solution)/shard_map/reduce_scatter | solution.py:212
  1181.0 18.0 copy-start.162
  1279.9 50.7 %all-to-all-start.3 = ((bf16[2,1,192,2560]{3,0,1,2:T(2,128)(2,1)}), bf16[2,1,192,2560]{3,0,1,2:T(2,128)(2,1)}, u32[]{:S(2)}, u32[]{:S(2)}) async-start(bf16[2,1,192,2560]{3,0,1,2:T(2,128)(2,1)} %copy.192), calls=%async_computation.3 | async-start | bytes 3932160 | tf_op jit(solution)/shard_map/all_to_all | solution.py:292
  1292.9 44.5 %copy-start.142 = (s32[2]{0:T(128)S(1)}, s32[2]{0:T(128)}, u32[]{:S(2)}) copy-start(s32[2]{0:T(128)} %copy-done.141) | copy-start | bytes 28
  1292.9 44.6 %copy-start.9 = (bf16[2,16,12,2560]{3,0,2,1:T(2,128)(2,1)S(1)}, bf16[2,16,12,2560]{3,0,2,1:T(2,128)(2,1)}, u32[]{:S(2)}) copy-start(bf16[2,16,12,2560]{3,0,2,1:T(2,128)(2,1)} %copy-done.8) | copy-start | bytes 5898244
  1330.6 429.3 %all-to-all-start.1 = ((bf16[2,1,192,2560]{3,0,1,2:T(2,128)(2,1)}), bf16[2,1,192,2560]{3,0,1,2:T(2,128)(2,1)}, u32[]{:S(2)}, u32[]{:S(2)}) async-start(bf16[2,1,192,2560]{3,0,1,2:T(2,128)(2,1)} %copy.175), calls=%async_computation.1 | async-start | bytes 3932160 | tf_op jit(solution)/shard_map/all_to_all | solution.py:285
  1336.7 364.4 %copy-start.127 = (f32[2560]{0:T(1024)S(1)}, f32[2560]{0:T(1024)}, u32[]{:S(2)}) copy-start(f32[2560]{0:T(1024)} %get-tuple-element.105) | copy-start | bytes 30724
  1336.7 364.4 %copy-start.128 = (f32[2560]{0:T(1024)S(1)}, f32[2560]{0:T(1024)}, u32[]{:S(2)}) copy-start(f32[2560]{0:T(1024)} %get-tuple-element.140) | copy-start | bytes 30724
  (132 other events, 367.1 us)
Sparse Core Ops, SparseCore 0:
  10.3 94.2 all-gather.13
  106.9 65.5 all-gather.11
  174.8 64.0 all-gather.15
  429.3 102.3 all-reduce.91
  533.1 195.6 all-gather.17
  730.4 102.6 all-gather.19
  883.5 102.4 all-reduce.93
  1115.5 103.0 all-reduce.95
  1222.5 52.9 reduce-scatter.59
  1279.2 62.8 reduce-scatter.45
  1345.9 64.1 reduce-scatter.53
  1413.7 54.1 reduce-scatter.55
  1471.8 54.1 reduce-scatter.57
  1529.7 54.1 reduce-scatter.51
  1587.6 54.1 reduce-scatter.47
  1645.4 54.1 reduce-scatter.49
  1704.1 57.6 reduce-scatter.37
  1765.8 57.3 reduce-scatter.35
  1828.4 138.4 reduce-scatter.39
  1971.4 137.4 reduce-scatter.31
  2114.2 137.5 reduce-scatter.33
  2256.6 378.3 reduce-scatter.43
  2639.8 727.3 reduce-scatter.41
where the time goes:
time: 3390 us; the launch traced here: 3370 us
  waiting for transfers between devices  2380 us (70%)
  blocking collectives  402 us (12%)
  matrix products  220 us (6%)
  local copies, waits for them, and re-layouts  193 us (6%)
  other arithmetic  136 us (4%)
    reduce_scatter x1, waiting for transfers between devices, body(): lax.psum_scatter(grad_expand, 'dp', scatter_dimension=1, tiled=True)  732 us
    reduce_scatter x1, waiting for transfers between devices, body(): lax.psum_scatter(grad_shrink, 'dp', scatter_dimension=0, tiled=True)  383 us
    unnamed x31, waiting for transfers between devices  354 us
    dot_general x24, matrix products, matmul(): jnp.einsum(formula, left_op, right_op, preferred_element_type=jnp.float32)  220 us
    all_gather x1, waiting for transfers between devices, body(): lax.all_gather(w_expand, 'dp', axis=1, tiled=True)  191 us
    reduce_scatter x1, waiting for transfers between devices, body(): lax.psum_scatter(grad_output, 'dp', scatter_dimension=0, tiled=True)  144 us
    reduce_scatter x1, waiting for transfers between devices, body(): lax.psum_scatter(grad_recur, 'dp', scatter_dimension=0, tiled=True)  143 us
    reduce_scatter x1, waiting for transfers between devices, body(): lax.psum_scatter(grad_branch, 'dp', scatter_dimension=0, tiled=True)  142 us
  transfers between devices with their start and end apart: 27, of which 18 were waited for; matrix products, arithmetic and copies ran while one was open for 10% of the time, Pallas kernels for 0%

commit v1 on v0

v1 whole, which is shorter than its diff:
```python
import functools

import jax
import jax.numpy as jnp
from jax import lax
from jax.experimental import pallas as pl
from jax.experimental.pallas import tpu as pltpu
from jax.sharding import Mesh, PartitionSpec as P

F32, BF16 = jnp.float32, jnp.bfloat16
LANES = 128
PLANES = 4
CORES = 2
CHUNKS = 4
DP = ("z", "x", "c")
GELU_A, GELU_B = 0.7978845608028654, 0.044715


def gelu_parts(v):
    square = v * v
    bent = jnp.tanh(GELU_A * v * (1.0 + GELU_B * square))
    half = 0.5 * (1.0 + bent)
    slope = half + 0.5 * v * (1.0 - bent * bent) * (GELU_A * (1.0 + 3.0 * GELU_B * square))
    return v * half, slope


def gelu(v):
    return v * (0.5 * (1.0 + jnp.tanh(GELU_A * v * (1.0 + GELU_B * v * v))))


def dot(a, b, dims=((1,), (0,))):
    return lax.dot_general(a, b, (dims, ((), ())), preferred_element_type=F32)


def logistic(v):
    return 1.0 / (1.0 + jnp.exp(-v))


def input_scale(decay, at_start):
    spare = 1.0 - decay * decay
    scale = jnp.sqrt(jnp.maximum(spare, 0.001))
    return jnp.where(at_start, 1.0, scale), spare


def start_rows(first_ref, rows, seqs, width):
    row = lax.broadcasted_iota(jnp.int32, (rows, width), 0)
    return jnp.logical_and(row < seqs, first_ref[0] == 1)


def gates_kernel(first_ref, r_ref, v_ref, wi_ref, wd_ref, c_ref, si_ref, sd_ref, e_ref, p_ref, *, seqs, taps):
    rows, width = c_ref.shape
    halo = r_ref.shape[0] - rows
    conv = v_ref[taps : taps + 1, :] + v_ref[0:1, :] * r_ref[pl.ds(halo, rows), :]
    for k in range(1, taps):
        conv = conv + v_ref[k : k + 1, :] * r_ref[pl.ds(halo - k * seqs, rows), :]
    c_ref[...] = conv
    low = conv.astype(BF16)
    si = logistic(dot(low, wi_ref[0]) + v_ref[taps + 1 : taps + 2, :])
    sd = logistic(dot(low, wd_ref[0]) + v_ref[taps + 2 : taps + 3, :])
    si_ref[...] = si
    sd_ref[...] = sd
    decay = jnp.exp(sd * v_ref[taps + 3 : taps + 4, :])
    scale, _ = input_scale(decay, start_rows(first_ref, rows, seqs, width))
    source = conv * si * scale
    state, total = source[:seqs], decay[:seqs]
    for p in range(1, rows // seqs):
        a = decay[p * seqs : (p + 1) * seqs]
        state = a * state + source[p * seqs : (p + 1) * seqs]
        total = total * a
    e_ref[...] = state
    p_ref[...] = total


def states_kernel(first_ref, c_ref, si_ref, sd_ref, b_ref, v_ref, carry_ref, s_ref, m_ref, *, seqs, taps):
    rows, width = c_ref.shape
    decay = jnp.exp(sd_ref[...] * v_ref[taps + 3 : taps + 4, :])
    scale, _ = input_scale(decay, start_rows(first_ref, rows, seqs, width))
    source = c_ref[...] * si_ref[...] * scale
    state = carry_ref[...]
    for p in range(rows // seqs):
        at = slice(p * seqs, (p + 1) * seqs)
        state = decay[at] * state + source[at]
        s_ref[pl.ds(p * seqs, seqs), :] = state
    m_ref[...] = (gelu(b_ref[...]) * s_ref[...]).astype(BF16)


def branch_kernel(dm_ref, b_ref, s_ref, sd_ref, v_ref, t_ref, db_ref, e_ref, sum_ref, *, seqs, taps):
    rows, _ = t_ref.shape
    value, slope = gelu_parts(b_ref[...])
    dm = dm_ref[...]
    t = dm * value
    t_ref[...] = t
    db = (dm * s_ref[...] * slope).astype(BF16)
    db_ref[...] = db
    sum_ref[...] = jnp.broadcast_to(jnp.sum(db.astype(F32), axis=0, keepdims=True), sum_ref.shape)
    decay = jnp.exp(sd_ref[...] * v_ref[taps + 3 : taps + 4, :])
    count = rows // seqs
    grad = t[(count - 1) * seqs :]
    for p in range(count - 2, -1, -1):
        grad = t[p * seqs : (p + 1) * seqs] + decay[(p + 1) * seqs : (p + 2) * seqs] * grad
    e_ref[...] = decay[:seqs] * grad


def core_kernel(
    first_ref, t_ref, c_ref, si_ref, sd_ref, s_ref, r_ref, v_ref, carry_ref, late_ref, wi_ref, wd_ref,
    dc_ref, gi_ref, gd_ref, sum_ref, ds_ref, *, seqs, taps,
):
    rows, width = c_ref.shape
    halo = r_ref.shape[0] - rows
    count = rows // seqs
    si, sd, conv = si_ref[...], sd_ref[...], c_ref[...]
    rate = v_ref[taps + 3 : taps + 4, :]
    decay = jnp.exp(sd * rate)
    at_start = start_rows(first_ref, rows, seqs, width)
    scale, spare = input_scale(decay, at_start)
    grad = late_ref[...]
    for p in range(count - 1, -1, -1):
        grad = t_ref[pl.ds(p * seqs, seqs), :] + grad
        ds_ref[pl.ds(p * seqs, seqs), :] = grad
        grad = decay[p * seqs : (p + 1) * seqs] * grad
    ds = ds_ref[...]
    before = carry_ref[...] if count == 1 else jnp.concatenate([carry_ref[...], s_ref[pl.ds(0, rows - seqs), :]], axis=0)
    bends = jnp.logical_and(spare > 0.001, jnp.logical_not(at_start))
    d_scale = jnp.where(bends, -(decay * decay) / scale, 0.0)
    gated = ds * conv
    d_log = ds * before * decay + gated * si * d_scale
    d_in = (gated * scale * si * (1.0 - si)).astype(BF16)
    d_dec = (d_log * rate * sd * (1.0 - sd)).astype(BF16)
    low = conv.astype(BF16)
    gi_ref[0] = dot(low, d_in, ((0,), (0,))).astype(gi_ref.dtype)
    gd_ref[0] = dot(low, d_dec, ((0,), (0,))).astype(gd_ref.dtype)
    dc = ds * si * scale + dot(d_in, wi_ref[0], ((1,), (1,))) + dot(d_dec, wd_ref[0], ((1,), (1,)))
    dc_ref[...] = dc

    def total(values):
        return jnp.sum(values, axis=0, keepdims=True)

    parts = [
        total(d_in.astype(F32)),
        total(d_dec.astype(F32)),
        total(d_log * sd) * v_ref[taps + 4 : taps + 5, :],
        total(dc),
    ]
    for k in range(taps):
        parts.append(total(r_ref[pl.ds(halo - k * seqs, rows), :] * dc))
    sum_ref[...] = jnp.concatenate(parts, axis=0)


def head_calls(heads, width, rows, halo_rows, seqs, taps):
    def cols(n):
        return pl.BlockSpec((n, width), lambda h: (0, h))

    flag = pl.BlockSpec(memory_space=pltpu.SMEM)
    mats = pl.BlockSpec((1, width, width), lambda h: (h, 0, 0))
    full = heads * width
    params = pltpu.CompilerParams(vmem_limit_bytes=48 * 1024 * 1024)
    vec_rows = 16

    def shape(n, kind=F32):
        return jax.ShapeDtypeStruct((n, full), kind)

    def call(kernel, ins, outs, shapes, scratch=(), flops=0):
        return pl.pallas_call(
            functools.partial(kernel, seqs=seqs, taps=taps),
            grid=(heads,),
            in_specs=ins,
            out_specs=outs,
            out_shape=shapes,
            scratch_shapes=list(scratch),
            compiler_params=params,
            cost_estimate=pl.CostEstimate(flops=flops, bytes_accessed=rows * full * 4 * len(ins), transcendentals=4 * rows * full),
        )

    unit = 2 * rows * full * width
    return (
        call(
            gates_kernel,
            [flag, cols(halo_rows), cols(vec_rows), mats, mats],
            [cols(rows), cols(rows), cols(rows), cols(seqs), cols(seqs)],
            [shape(rows), shape(rows), shape(rows), shape(seqs), shape(seqs)],
            flops=2 * unit,
        ),
        call(
            states_kernel,
            [flag, cols(rows), cols(rows), cols(rows), cols(rows), cols(vec_rows), cols(seqs)],
            [cols(rows), cols(rows)],
            [shape(rows), shape(rows, BF16)],
        ),
        call(
            branch_kernel,
            [cols(rows), cols(rows), cols(rows), cols(rows), cols(vec_rows)],
            [cols(rows), cols(rows), cols(seqs), cols(8)],
            [shape(rows), shape(rows, BF16), shape(seqs), shape(8)],
        ),
        call(
            core_kernel,
            [flag, cols(rows), cols(rows), cols(rows), cols(rows), cols(rows), cols(halo_rows), cols(vec_rows),
             cols(seqs), cols(seqs), mats, mats],
            [cols(rows), mats, mats, cols(4 + taps)],
            [shape(rows), jax.ShapeDtypeStruct((heads, width, width), BF16),
             jax.ShapeDtypeStruct((heads, width, width), BF16), shape(4 + taps)],
            scratch=[pltpu.VMEM((rows, width), F32)],
            flops=4 * unit,
        ),
    )


def swap(v, axis):
    return lax.ppermute(v, axis, [(0, 1), (1, 0)])


def gather_rows(v, axis):
    if lax.axis_size(axis) == 2:
        return jnp.concatenate([v, swap(v, axis)], axis=0)
    return lax.all_gather(v, axis, axis=0, tiled=True)


def scatter_rows(v, axis):
    count = lax.axis_size(axis)
    if count == 2:
        half = v.shape[0] // 2
        return v[:half].astype(F32) + swap(v[half:].astype(BF16), axis).astype(F32)
    return lax.psum_scatter(v.astype(BF16), axis, scatter_dimension=0, tiled=True).astype(F32)


def halves(v, axis):
    half = v.shape[0] // 2
    at = lax.axis_index(axis)
    own = lax.dynamic_slice_in_dim(v, at * half, half, 0)
    return own, lax.dynamic_slice_in_dim(v, (1 - at) * half, half, 0)


def whole_rows(own, axis):
    other = swap(own, axis)
    low = lax.axis_index(axis) == 0
    return jnp.concatenate([jnp.where(low, own, other), jnp.where(low, other, own)], axis=0)


def ranks(value, axis):
    count = lax.axis_size(axis)
    if count == 2:
        other = swap(value, axis)
        low = lax.axis_index(axis) == 0
        return [jnp.where(low, value, other), jnp.where(low, other, value)]
    every = lax.all_gather(value, axis)
    return [every[j] for j in range(count)]


def carry_in(state, total, backward):
    pair = jnp.stack([state, total])
    inner = []
    for axis, kind in (("c", F32), ("x", BF16)):
        parts = [part.astype(F32) for part in ranks(pair.astype(kind), axis)]
        order = range(len(parts))
        at = lax.axis_index(axis)
        if backward:
            order, at = [len(parts) - 1 - j for j in order], len(parts) - 1 - at
        gone = jnp.stack([jnp.zeros_like(state), jnp.ones_like(total)])
        mine = gone
        for place, j in enumerate(order):
            mine = jnp.where(at == place, gone, mine)
            gone = jnp.stack([parts[j][0] + parts[j][1] * gone[0], parts[j][1] * gone[1]])
        inner.append(mine)
        pair = gone
    planes = lax.axis_size("z")
    sent = pair.astype(BF16)
    entering = jnp.zeros_like(state)
    steps = []
    for far in range(1, planes):
        if backward:
            route = [(j + far, j) for j in range(planes - far)]
        else:
            route = [(j, j + far) for j in range(planes - far)]
        steps.append(lax.ppermute(sent if far < planes - 1 else sent[:1], "z", route).astype(F32))
    for step in reversed(steps):
        entering = step[0] + (step[1] * entering if step.shape[0] == 2 else 0.0)
    for mine in reversed(inner):
        entering = mine[0] + mine[1] * entering
    return entering


def norm(v, gain):
    scale = lax.rsqrt(jnp.mean(v * v, axis=-1, keepdims=True) + 1e-6)
    return v * scale * gain, scale


def norm_back(v, scale, gain, d_out):
    scaled = gain * d_out
    mean = jnp.mean(v * scaled, axis=-1, keepdims=True)
    return scale * scaled - v * (scale * scale * scale * mean), jnp.sum(v * scale * d_out, axis=0)


def body(
    block_input, cotangent, seq_lengths, pre_gain, w_branch, b_branch, w_recur, b_recur, conv_kernel, conv_bias,
    input_gate_weight, input_gate_bias, decay_gate_weight, decay_gate_bias, decay_base, w_output, b_output,
    ffn_gain, w_expand, b_expand, w_shrink, b_shrink,
):
    mid = lax.axis_size("x")
    groups = PLANES * mid * CORES
    place = lax.axis_index(DP)
    side = lax.axis_index("y")
    seqs, pieces, width = block_input.shape
    rows = seqs * pieces
    taps, heads, head_part = conv_kernel.shape
    head_size = head_part * groups
    channels = heads * head_size
    part = w_recur.shape[0]
    units = w_shrink.shape[1]
    halo = (taps - 1) * seqs

    x_low = block_input.transpose(1, 0, 2).reshape(rows, width)
    positions = place * pieces + lax.broadcasted_iota(jnp.int32, (pieces, seqs), 0)
    mask = (positions < seq_lengths[None, :]).reshape(rows, 1)
    d_out = jnp.where(mask, cotangent.transpose(1, 0, 2).reshape(rows, width), 0).astype(BF16)
    early = lax.ppermute(x_low[rows - halo :], DP, [(j, j + 1) for j in range(groups - 1)])

    vectors = [b_branch, b_recur, *[conv_kernel[k] for k in range(taps)], conv_bias, input_gate_bias,
               decay_gate_bias, decay_base]
    flat = jnp.concatenate([v.reshape(-1) for v in vectors] + [pre_gain, b_output, ffn_gain, b_shrink, b_expand.reshape(-1)])
    small_rows = -(-flat.size // channels)
    pad_rows = -(-small_rows // 16) * 16
    flat = jnp.pad(flat, (0, pad_rows * channels - flat.size)).reshape(pad_rows, channels)
    gate_rows = input_gate_weight.transpose(1, 0, 2).reshape(head_part, channels)
    decay_rows = decay_gate_weight.transpose(1, 0, 2).reshape(head_part, channels)
    packed = jnp.concatenate([w_recur, w_branch, w_output, gate_rows, decay_rows, flat], axis=0)
    gathered = lax.all_gather(packed, DP, axis=0, tiled=False)
    recur_full = gathered[:, :part].reshape(width, channels)
    branch_full = gathered[:, part : 2 * part].reshape(width, channels)
    output_full = gathered[:, 2 * part : 3 * part].reshape(width, channels)

    def gate_full(at):
        return (
            gathered[:, at : at + head_part].reshape(groups, head_part, heads, head_size)
            .transpose(2, 0, 1, 3).reshape(heads, head_size, head_size)
        )

    inlet_full, decay_full = gate_full(3 * part), gate_full(3 * part + head_part)
    every = gathered[:, 3 * part + 2 * head_part :].reshape(groups, -1)[:, : small_rows * channels].astype(F32)
    taken = 0

    def take(count):
        nonlocal taken
        taken += count
        return every[:, taken - count : taken]

    def by_head():
        return take(heads * head_part).reshape(groups, heads, head_part).transpose(1, 0, 2).reshape(channels)

    vec_branch, vec_recur = by_head(), by_head()
    vec_taps = [by_head() for _ in range(taps)]
    vec_conv, vec_inlet, vec_decay, vec_base = by_head(), by_head(), by_head(), by_head()
    gain_one, vec_output, gain_two, vec_shrink = [take(part).reshape(width) for _ in range(4)]
    blocks = b_expand.shape[1]
    vec_expand = take(2 * blocks * head_part).reshape(groups, 2, blocks, head_part).transpose(1, 2, 0, 3).reshape(2, units)
    gain_one, gain_two = 1.0 + gain_one, 1.0 + gain_two
    coefs = jnp.stack(
        vec_taps + [vec_conv, vec_inlet, vec_decay, -8.0 * jax.nn.softplus(vec_base), -8.0 * jax.nn.sigmoid(vec_base)]
    )
    coefs = jnp.pad(coefs, ((0, 16 - coefs.shape[0]), (0, 0)))

    slices = mid * CORES
    tiles = units // LANES
    wide_tiles = -(-tiles // slices)
    wide = wide_tiles * LANES
    starts = [j * (tiles - wide_tiles) // (slices - 1) for j in range(slices)]
    owned = [(starts[j + 1] if j + 1 < slices else tiles) - starts[j] for j in range(slices)]
    chunks = CHUNKS if wide % (CHUNKS * LANES) == 0 else 1
    step = wide // chunks
    sent = []
    for k in range(chunks):
        for j in range(slices):
            at = starts[j] * LANES + k * step
            sent.append(jnp.concatenate([w_expand[0, :, at : at + step], w_expand[1, :, at : at + step], w_shrink[:, at : at + step]], axis=1))
    sent = jnp.stack(sent).reshape(chunks, slices, part, 3 * step)
    held = lax.all_to_all(sent, ("x", "c"), split_axis=1, concat_axis=1, tiled=True)
    held = held.reshape(chunks, slices * part, 3 * step)
    my_slice = lax.axis_index(("x", "c"))
    my_start = jnp.array(starts, jnp.int32)[my_slice] * LANES
    my_owned = jnp.array(owned, jnp.int32)[my_slice] * LANES
    held, gathered_after = lax.optimization_barrier((held, output_full))
    output_full = gathered_after
    ffn_full = [lax.all_gather(held[k], "z", axis=0, tiled=True) for k in range(chunks)]
    my_bias = lax.dynamic_slice_in_dim(vec_expand, my_start, wide, 1)

    d_first, d_second = halves(d_out, "y")
    d_plane = gather_rows(gather_rows(jnp.concatenate([d_first, d_second], axis=0), "x"), "c")

    gates, states, branch_back, core_back = head_calls(heads, head_size, rows, rows + halo, seqs, taps)
    first = (place == 0).astype(jnp.int32).reshape(1)
    x_ext = jnp.concatenate([early, x_low], axis=0).astype(F32)
    normed_f, _ = norm(x_ext, gain_one)
    normed_ext = normed_f.astype(BF16)
    normed = normed_ext[halo:]
    recur = dot(normed_ext, recur_full) + vec_recur
    ext_row = lax.broadcasted_iota(jnp.int32, (rows + halo, 1), 0)
    recur = jnp.where(jnp.logical_and(ext_row < halo, place == 0), 0.0, recur)
    conv, sig_in, sig_dec, end, total = gates(first, recur, coefs, inlet_full, decay_full)
    carry = carry_in(end, total, False)
    branch = dot(normed, branch_full) + vec_branch
    state, mixed = states(first, conv, sig_in, sig_dec, branch, coefs, carry)
    out_own, out_other = halves(dot(mixed, output_full, ((1,), (1,))), "y")
    x_own, _ = halves(x_low, "y")
    x_own = x_own.astype(F32)
    middle = x_own + out_own + swap(out_other.astype(BF16), "y").astype(F32) + vec_output
    second_f, scale_two = norm(middle, gain_two)
    second = second_f.astype(BF16)

    plane = gather_rows(gather_rows(gather_rows(second, "y"), "x"), "c")
    ffn_out = 0.0
    d_second_part = 0.0
    ffn_grads, bias_grads = [], []
    for k in range(chunks):
        weights = ffn_full[k]
        pre = dot(plane, weights[:, : 2 * step])
        gate = pre[:, :step] + my_bias[0, k * step : (k + 1) * step]
        up = pre[:, step:] + my_bias[1, k * step : (k + 1) * step]
        d_hidden = dot(d_plane, weights[:, 2 * step :])
        mine = k * step + lax.broadcasted_iota(jnp.int32, (1, step), 1) < my_owned
        value, slope = gelu_parts(gate)
        hidden = jnp.where(mine, value * up, 0.0).astype(BF16)
        d_gate = jnp.where(mine, d_hidden * up * slope, 0.0).astype(BF16)
        d_up = jnp.where(mine, d_hidden * value, 0.0).astype(BF16)
        d_pre = jnp.concatenate([d_gate, d_up], axis=1)
        d_second_part = d_second_part + dot(d_pre, weights[:, : 2 * step], ((1,), (1,)))
        ffn_out = ffn_out + dot(hidden, weights[:, 2 * step :], ((1,), (1,)))
        grads = jnp.concatenate(
            [dot(plane, d_pre, ((0,), (0,))).astype(BF16), dot(d_plane, hidden, ((0,), (0,))).astype(BF16)], axis=1
        )
        ffn_grads.append(lax.psum_scatter(grads, "z", scatter_dimension=0, tiled=True))
        bias_grads.append(jnp.sum(d_pre.astype(F32), axis=0).reshape(2, step))

    def to_owner(values):
        values = values.astype(BF16)
        return scatter_rows(scatter_rows(scatter_rows(values, "c").astype(BF16), "x").astype(BF16), "y")

    d_second_own = to_owner(d_second_part)
    d_middle, grad_gain_two = norm_back(middle, scale_two, gain_two, d_second_own)
    d_middle = d_middle + d_first.astype(F32)
    d_low_own = d_middle.astype(BF16)
    mask_own, _ = halves(mask, "y")
    result = jnp.where(mask_own, middle + to_owner(ffn_out) + vec_shrink, 0.0).astype(BF16)
    result = whole_rows(result, "y")

    d_low = whole_rows(d_low_own, "y")
    d_mixed = dot(d_low, output_full)
    pulled, d_branch, end_back, branch_sum = branch_back(d_mixed, branch, state, sig_dec, coefs)
    late = carry_in(end_back, total, True)
    grad_output = dot(d_low, mixed, ((0,), (0,))).astype(BF16)
    grad_branch = dot(normed, d_branch, ((0,), (0,))).astype(BF16)
    d_conv, grad_inlet, grad_decay, core_sums = core_back(
        first, pulled, conv, sig_in, sig_dec, state, recur, coefs, carry, late, inlet_full, decay_full
    )
    after = lax.ppermute(d_conv[:halo].astype(BF16), DP, [(j + 1, j) for j in range(groups - 1)])
    d_ext = jnp.concatenate([d_conv, after.astype(F32)], axis=0)
    d_recur = vec_taps[0] * d_ext[:rows]
    for k in range(1, taps):
        d_recur = d_recur + vec_taps[k] * d_ext[k * seqs : k * seqs + rows]
    d_recur = d_recur.astype(BF16)
    grad_recur = dot(normed, d_recur, ((0,), (0,))).astype(BF16)
    d_normed = dot(d_branch, branch_full, ((1,), (1,))) + dot(d_recur, recur_full, ((1,), (1,)))
    dn_own, dn_other = halves(d_normed, "y")
    dn_own = dn_own + swap(dn_other.astype(BF16), "y").astype(F32)
    scale_one = lax.rsqrt(jnp.mean(x_own * x_own, axis=-1, keepdims=True) + 1e-6)
    d_input, grad_gain_one = norm_back(x_own, scale_one, gain_one, dn_own)
    d_input = whole_rows((d_middle + d_input).astype(BF16), "y")

    shared = jnp.stack([grad_gain_one, jnp.sum(d_low_own.astype(F32), axis=0), grad_gain_two])
    shared = shared + swap(shared, "y")
    shared = jnp.concatenate([shared, jnp.sum(d_out.astype(F32), axis=0)[None]], axis=0)
    recur_sum = jnp.sum(d_recur.astype(F32), axis=0)
    by_channel = jnp.concatenate(
        [branch_sum[:1], recur_sum[None], core_sums[4:], core_sums[3:4], core_sums[:3]], axis=0
    )
    by_channel = by_channel.reshape(-1, heads, groups, head_part).transpose(2, 0, 1, 3).reshape(groups, -1)
    by_feature = shared.reshape(4, groups, part).transpose(1, 0, 2).reshape(groups, -1)
    by_unit = lax.dynamic_update_slice_in_dim(jnp.zeros((2, units), F32), jnp.concatenate(bias_grads, axis=1), my_start, 1)
    by_unit = by_unit.reshape(2, blocks, groups, head_part).transpose(2, 0, 1, 3).reshape(groups, -1)
    small = jnp.concatenate([by_channel, by_feature, by_unit], axis=1)
    small_count = small.shape[1]
    small = jnp.pad(small, ((0, 0), (0, pad_rows * channels - small_count))).reshape(groups, pad_rows, channels)

    def gate_pack(grad):
        return grad.reshape(heads, groups, head_part, head_size).transpose(1, 2, 0, 3).reshape(groups, head_part, channels)

    pack_a = jnp.concatenate(
        [grad_output.reshape(groups, part, channels), grad_branch.reshape(groups, part, channels)], axis=1
    )
    pack_b = jnp.concatenate(
        [grad_recur.reshape(groups, part, channels), gate_pack(grad_inlet), gate_pack(grad_decay), small.astype(BF16)], axis=1
    )
    sum_a = lax.psum_scatter(pack_a, DP, scatter_dimension=0, tiled=False).astype(F32)
    sum_b = lax.psum_scatter(pack_b, DP, scatter_dimension=0, tiled=False).astype(F32)

    ffn_sum = jnp.stack(ffn_grads).reshape(chunks, slices, part, 3 * step)
    ffn_sum = lax.all_to_all(ffn_sum, ("x", "c"), split_axis=1, concat_axis=1, tiled=True)
    grads_out = []
    for kind in range(3):
        pieces_out = []
        for j in range(slices):
            for k in range(chunks):
                keep = min(step, owned[j] * LANES - k * step)
                if keep > 0:
                    pieces_out.append(ffn_sum[k, j, :, kind * step : kind * step + keep])
        grads_out.append(jnp.concatenate(pieces_out, axis=1).astype(F32))
    grad_expand = jnp.stack(grads_out[:2])
    grad_shrink = grads_out[2]

    given = sum_b[part + 2 * head_part :].reshape(-1)[:small_count]
    taken = 0

    def give(*dims):
        nonlocal taken
        count = 1
        for n in dims:
            count *= n
        taken += count
        return given[taken - count : taken].reshape(dims)

    head_dims = (heads, head_part)
    g_b_branch, g_b_recur, g_kernel = give(*head_dims), give(*head_dims), give(taps, *head_dims)
    g_conv_bias, g_b_inlet, g_b_decay, g_base = give(*head_dims), give(*head_dims), give(*head_dims), give(*head_dims)
    g_pre_gain, g_b_output, g_ffn_gain, g_b_shrink = give(part), give(part), give(part), give(part)
    g_b_expand = give(2, blocks, head_part)

    def gate_out(at):
        return sum_b[at : at + head_part].reshape(head_part, heads, head_size).transpose(1, 0, 2)

    def rows_out(v):
        return v.reshape(pieces, seqs, width).transpose(1, 0, 2)

    return (
        rows_out(result), rows_out(d_input), g_pre_gain, sum_a[part:], g_b_branch, sum_b[:part], g_b_recur,
        g_kernel, g_conv_bias, gate_out(part), g_b_inlet, gate_out(part + head_part), g_b_decay, g_base,
        sum_a[:part], g_b_output, g_ffn_gain, grad_expand, g_b_expand, grad_shrink, g_b_shrink,
    )


def solution(mesh):
    groups, sides = mesh.shape["dp"], mesh.shape["tensor"]
    mid = groups // (PLANES * CORES)
    grid = Mesh(mesh.devices.reshape(PLANES, mid, CORES, sides), ("z", "x", "c", "y"))
    rows, vec = P(None, DP, None), P(DP)
    mat, head, tap, gate = P(DP, "y"), P("y", DP), P(None, "y", DP), P("y", DP, None)
    wide = P(None, DP, "y")
    return jax.shard_map(
        body,
        mesh=grid,
        in_specs=(
            rows, rows, P(), vec, mat, head, mat, head, tap, head, gate, head, gate, head, head, mat, vec, vec,
            wide, tap, mat, vec,
        ),
        out_specs=(
            rows, rows, vec, mat, head, mat, head, tap, head, gate, head, gate, head, head, mat, vec, vec,
            wide, tap, mat, vec,
        ),
        check_vma=False,
    )
```

time: 3390 us -> 1170 us (0.35)
  waiting for transfers between devices: 2380 us -> 386 us
  blocking collectives: 402 us -> 48 us
  starting transfers between devices: 27.4 us -> 107 us
  matrix products: 220 us -> 262 us
  other arithmetic: 136 us -> 94.7 us
    reduce_scatter x7 -> x6, waiting for transfers between devices: 1600 us -> 0.01 us  [the longest x4 0.01 us: body(): lax.psum_scatter(grads, 'z', scatter_dimension=0, tiled=True)]
    unnamed x31 -> x11, waiting for transfers between devices: 354 us -> 0.18 us
    all_gather x10 -> x0, blocking collectives: 304 us -> none  [the longest x1 86.9 us: body(): lax.all_gather(b_branch, 'dp', axis=1, tiled=True)]
    ppermute x0 -> x29, waiting for transfers between devices: none -> 260 us  [the longest x21 222 us: swap(): return lax.ppermute(v, axis, [(0, 1), (1, 0)])]
    all_gather x5, waiting for transfers between devices: 267 us -> 92.3 us  [the longest x1 92.3 us: body(): gathered = lax.all_gather(packed, DP, axis=0, tiled=False)]
    psum x3 -> x0, waiting for transfers between devices: 120 us -> none  [the longest x1 88.4 us: body(): d_second = lax.psum(d_second_part, 'tensor')]
    ppermute x0 -> x29, starting transfers between devices: none -> 98.4 us  [the longest x21 75.3 us: swap(): return lax.ppermute(v, axis, [(0, 1), (1, 0)])]
    unnamed x2 -> x0, blocking collectives: 97.6 us -> none
  transfers between devices with their start and end apart: 27 -> 41, of which waited for: 18 -> 22; matrix products, arithmetic and copies ran while one was open for 10% -> 44% of each run, Pallas kernels for 0% -> 2%
where the time goes in v1:
time: 1170 us; the launch traced here: 1150 us
  waiting for transfers between devices  386 us (33%)
  matrix products  262 us (22%)
  local copies, waits for them, and re-layouts  209 us (18%)
  starting transfers between devices  107 us (9%)
  other arithmetic  94.7 us (8%)
  blocking collectives  48 us (4%)
  Pallas kernels  24.9 us (2%)
  between operations  18.4 us (2%)
    dot_general x33, matrix products, dot(): return lax.dot_general(a, b, (dims, ((), ())), preferred_element_type=F32)  262 us
    ppermute x21, waiting for transfers between devices, swap(): return lax.ppermute(v, axis, [(0, 1), (1, 0)])  222 us
    all_gather x1, waiting for transfers between devices, body(): gathered = lax.all_gather(packed, DP, axis=0, tiled=False)  92.3 us
    unnamed x373, local copies, waits for them, and re-layouts  88.4 us
    ppermute x21, starting transfers between devices, swap(): return lax.ppermute(v, axis, [(0, 1), (1, 0)])  75.3 us
    all_to_all x1, blocking collectives, body(): lax.all_to_all(sent, ('x', 'c'), split_axis=1, concat_axis=1, tiled=True)  48 us
    ppermute x6, waiting for transfers between devices, carry_in(): lax.ppermute(sent if far < planes - 1 else sent[:1], 'z', route).astype(F32)  34.2 us
    all_to_all x1, waiting for transfers between devices, body(): lax.all_to_all(ffn_sum, ('x', 'c'), split_axis=1, concat_axis=1, tiled=True)  33.4 us
  transfers between devices with their start and end apart: 41, of which 22 were waited for; matrix products, arithmetic and copies ran while one was open for 44% of the time, Pallas kernels for 2%

profile of v1, /device:TPU:9, one launch (start us, length us, event | category | flops | bytes accessed | tf_op | source)
XLA Modules:
  0.0 1149.7 jit_solution(17169264787705797972)
XLA Ops:
  27.0 48.0 %all_to_all.10 = bf16[4,4,160,768]{3,2,0,1:T(8,128)(2,1)S(1)} all-to-all(bf16[4,4,160,768]{3,2,0,1:T(8,128)(2,1)S(1)} %copy.221), channel_id=1, replica_groups=mesh['z'=4,'x'=2,'c'=2,'y'=2] {'x','c'}, dimensions={1} | all-to-all | bytes 7864320 | tf_op jit(solution)/shard_map/all_to_all | solution.py:375
  77.2 92.3 %all-gather.11.cloned.1.call-done = bf16[8448,1280]{1,0:T(8,128)(2,1)} async-done(((bf16[528,1280]{1,0:T(8,128)(2,1)}), bf16[8448,1280]{1,0:T(8,128)(2,1)}) %all-gather.11.cloned.1.call-update) | async-done | bytes 21626896 | tf_op jit(solution)/shard_map/all_gather | solution.py:326
  169.5 13.8 %fusion.118 = (bf16[16,160,1280]{2,1,0:T(8,128)(2,1)}, bf16[16,160,1280]{2,1,0:T(8,128)(2,1)}, bf16[16,160,1280]{2,1,0:T(8,128)(2,1)}) fusion(bf16[16,528,1280]{2,1,0:T(8,128)(2,1)} %bitcast.556), kind=kLoop, calls=%fused_computation.447 | loop fusion | bytes 39321600 | tf_op jit(solution)/shard_map/slice | solution.py:329
  238.9 8.5 fusion.3.r_ref
  247.4 6.0 shard_map.391
  256.1 9.9 collective-permute-start.1
  269.1 7.5 convolution_add_fusion.2.b_ref
  277.9 5.8 collective-permute-done.2
  288.4 5.3 collective-permute-start.4
  295.0 17.5 %collective-permute-done.4 = bf16[2,32,1280]{2,1,0:T(8,128)(2,1)S(1)} collective-permute-done((bf16[2,32,1280]{2,1,0:T(8,128)(2,1)S(1)}, bf16[2,32,1280]{2,1,0:T(8,128)(2,1)S(1)}, u32[]{:S(2)}, u32[]{:S(2)}) %collective-permute-start.4) | collective-permute-done | bytes 163872 | tf_op jit(solution)/shard_map/ppermute | solution.py:274
  312.6 5.6 shard_map.392
  326.1 10.2 collective-permute-done.6
  349.8 6.7 collective-permute-done.7
  358.1 5.6 collective-permute-start.8
  363.7 20.8 %collective-permute-done.14 = bf16[384,2560]{1,0:T(8,128)(2,1)} collective-permute-done((bf16[384,2560]{1,0:T(8,128)(2,1)}, bf16[384,2560]{1,0:T(8,128)(2,1)}, u32[]{:S(2)}, u32[]{:S(2)}) %collective-permute-start.14) | collective-permute-done | bytes 1966112 | tf_op jit(solution)/shard_map/ppermute | solution.py:209
  387.8 18.3 %collective-permute-start.15 = (bf16[768,2560]{1,0:T(8,128)(2,1)}, bf16[768,2560]{1,0:T(8,128)(2,1)}, u32[]{:S(2)}, u32[]{:S(2)}) collective-permute-start(bf16[768,2560]{1,0:T(8,128)(2,1)} %pad_maximum_fusion.5), channel_id=1, source_target_pairs={{0,2},{2,0},{1,3},{3,1},{4,6},{6,4},{5,7},{7,5},{8,10},{10,8},{9,1... | collective-permute-start | bytes 11796488 | tf_op jit(solution)/shard_map/ppermute | solution.py:209
  406.1 20.4 %collective-permute-done.8 = bf16[384,2560]{1,0:T(8,128)(2,1)S(1)} collective-permute-done((bf16[384,2560]{1,0:T(8,128)(2,1)S(1)}, bf16[384,2560]{1,0:T(8,128)(2,1)S(1)}, u32[]{:S(2)}, u32[]{:S(2)}) %collective-permute-start.8) | collective-permute-done | bytes 1966112 | tf_op jit(solution)/shard_map/ppermute | solution.py:209
  430.4 9.4 collective-permute-start.9
  442.4 6.3 pad_maximum_fusion.3
  450.7 11.0 fusion.17
  471.3 6.8 convolution_convert_fusion.6
  480.2 6.5 copy.292
  486.8 7.8 fusion.13
  494.7 7.1 convolution_convert_fusion.9
  501.8 6.8 select_convert_fusion.6
  508.7 6.8 convolution_convert_fusion.5
  517.7 6.3 copy.294
  523.9 12.1 %fusion.11 = f32[1536,2560]{1,0:T(8,128)} fusion(bf16[2560,768]{1,0:T(8,128)(2,1)} %bitcast.604, bf16[1536,256]{0,1:T(8,128)(2,1)} %copy-done.68, bf16[1536,256]{0,1:T(8,128)(2,1)} %copy-done.67), kind=kOutput, calls=%fused_computation.59 | convolution fusion | flops 4029677568 | bytes 19922944 | tf_op jit(solution)/shard_map/dot_general | solution.py:32
  536.5 7.8 fusion.9
  546.0 8.1 select_convert_fusion.4
  554.1 7.9 fusion.5
  562.1 9.2 fusion.15
  571.4 7.9 fusion.7
  584.0 21.3 %add_convert_fusion = bf16[1536,2560]{1,0:T(8,128)(2,1)} fusion(f32[1536,2560]{1,0:T(8,128)} %fusion.7, f32[1536,2560]{1,0:T(8,128)} %fusion.15, f32[1536,2560]{1,0:T(8,128)} %fusion.11, bf16[2560,768]{1,0:T(8,128)(2,1)} %bitcast.581, bf16[1536,256]{0,1:T(8,128)(2,1)S(1)} %get-tuple-element.168, bf16[1536,256]{0,1:T(8,128)(2,1)S(1)} %get-tuple-element.167), kind=kOutput, calls=%fused_computation | convolution fusion | flops 4045406208 | bytes 59244544 | tf_op jit(solution)/shard_map/dot_general | solution.py:32
  610.0 6.1 convolution_convert_fusion.8
  616.2 6.7 convolution_convert_fusion.4
  625.1 6.3 copy.296
  647.7 36.1 %collective-permute-done.17 = bf16[384,2560]{1,0:T(8,128)(2,1)} collective-permute-done((bf16[384,2560]{1,0:T(8,128)(2,1)}, bf16[384,2560]{1,0:T(8,128)(2,1)}, u32[]{:S(2)}, u32[]{:S(2)}) %collective-permute-start.17) | collective-permute-done | bytes 1966112 | tf_op jit(solution)/shard_map/ppermute | solution.py:209
  686.8 7.0 convolution_convert_fusion.3
  693.8 15.3 %collective-permute-done.18 = bf16[192,2560]{1,0:T(8,128)(2,1)S(1)} collective-permute-done((bf16[192,2560]{1,0:T(8,128)(2,1)S(1)}, bf16[192,2560]{1,0:T(8,128)(2,1)S(1)}, u32[]{:S(2)}, u32[]{:S(2)}) %collective-permute-start.18) | collective-permute-done | bytes 983072 | tf_op jit(solution)/shard_map/ppermute | solution.py:209
  717.0 6.3 copy.298
  733.9 6.3 fusion.46.dm_ref
  740.2 5.3 shard_map.393
  748.5 7.5 fusion.128
  765.9 10.2 collective-permute-done.22
  776.2 6.4 collective-permute-done.23
  782.8 7.9 shard_map.394
  792.4 5.6 collective-permute-start.25
  812.0 5.1 convolution_add_fusion
  824.4 7.0 convolution_convert_fusion.2
  838.7 6.6 pad_maximum_fusion.1
  845.9 11.1 fusion.56
  857.0 9.9 fusion.60
  867.0 11.0 fusion.52
  878.1 20.2 %add_convert_fusion.1 = bf16[1536,2560]{1,0:T(8,128)(2,1)S(1)} fusion(f32[1536,2560]{1,0:T(8,128)} %fusion.52, f32[1536,2560]{1,0:T(8,128)} %fusion.60, f32[1536,2560]{1,0:T(8,128)} %fusion.56, bf16[2560,768]{1,0:T(8,128)(2,1)} %bitcast.582, f32[1536,512]{0,1:T(8,128)} %copy-done.73, f32[256]{0:T(256)S(1)} %bitcast.648, pred[256]{0:T(512)(128)(4,1)S(1)} %copy-done.149, ...), kind=kOutput, calls=%fused_computation.1 | convolution fusion | flops 2034106368 | bytes 59508992 | tf_op jit(solution)/shard_map/dot_general | solution.py:32
  903.1 14.9 %collective-permute-start.10 = (bf16[768,2560]{1,0:T(8,128)(2,1)}, bf16[768,2560]{1,0:T(8,128)(2,1)}, u32[]{:S(2)}, u32[]{:S(2)}) collective-permute-start(bf16[768,2560]{1,0:T(8,128)(2,1)} %slice.1018), channel_id=1, source_target_pairs={{0,2},{2,0},{1,3},{3,1},{4,6},{6,4},{5,7},{7,5},{8,10},{10,8},{9,1... | collective-permute-start | bytes 11796488 | tf_op jit(solution)/shard_map/ppermute | solution.py:209
  925.8 8.6 pad_maximum_fusion
  939.0 50.1 %collective-permute-done.11 = bf16[384,2560]{1,0:T(8,128)(2,1)S(1)} collective-permute-done((bf16[384,2560]{1,0:T(8,128)(2,1)S(1)}, bf16[384,2560]{1,0:T(8,128)(2,1)S(1)}, u32[]{:S(2)}, u32[]{:S(2)}) %collective-permute-start.11) | collective-permute-done | bytes 1966112 | tf_op jit(solution)/shard_map/ppermute | solution.py:209
  993.2 21.4 %collective-permute-done.12 = bf16[192,2560]{1,0:T(8,128)(2,1)} collective-permute-done((bf16[192,2560]{1,0:T(8,128)(2,1)}, bf16[192,2560]{1,0:T(8,128)(2,1)}, u32[]{:S(2)}, u32[]{:S(2)}) %collective-permute-start.12) | collective-permute-done | bytes 983072 | tf_op jit(solution)/shard_map/ppermute | solution.py:209
  1014.7 5.1 fusion.33
  1025.4 7.7 all-to-all-start.1
  1033.7 7.2 collective-permute-done.27
  1043.7 18.3 %collective-permute-done.13 = bf16[192,2560]{1,0:T(8,128)(2,1)S(1)} collective-permute-done((bf16[192,2560]{1,0:T(8,128)(2,1)S(1)}, bf16[192,2560]{1,0:T(8,128)(2,1)S(1)}, u32[]{:S(2)}, u32[]{:S(2)}) %collective-permute-start.13) | collective-permute-done | bytes 983072 | tf_op jit(solution)/shard_map/ppermute | solution.py:209
  1063.7 33.4 %all-to-all-done.1 = bf16[4,4,160,768]{3,2,0,1:T(8,128)(2,1)} async-done(((bf16[4,4,160,768]{3,2,0,1:T(8,128)(2,1)}), bf16[4,4,160,768]{3,2,0,1:T(8,128)(2,1)}, u32[]{:S(2)}, u32[]{:S(2)}) %all-to-all-start.1) | async-done | bytes 3932192 | tf_op jit(solution)/shard_map/all_to_all | solution.py:495
  (683 shorter events, 309.7 us)
Async XLA Ops:
  7.2 162.3 %all-gather.11.cloned.1.call-start = ((), (), s32[]{:S(2)}) async-start(), calls=%async_computation.10 | async-start | bytes 22978560 | tf_op jit(solution)/shard_map/all_gather | solution.py:326
  24.7 426.0 %all-gather.13.cloned.1.call-start = ((), (), s32[]{:S(2)}) async-start(), calls=%async_computation.11 | async-start | bytes 4915200 | tf_op jit(solution)/shard_map/all_gather | solution.py:382
  185.8 301.1 %all-gather.15.cloned.1.call-start = ((), (), s32[]{:S(2)}) async-start(), calls=%async_computation.12 | async-start | bytes 4915200 | tf_op jit(solution)/shard_map/all_gather | solution.py:382
  186.6 8.1 collective-permute-start
  197.9 34.4 %copy-start.75 = (f32[16,2560]{1,0:T(8,128)}, f32[16,2560]{1,0:T(8,128)S(1)}, u32[]{:S(2)}) copy-start(f32[16,2560]{1,0:T(8,128)S(1)} %slice_convert_fusion.1) | copy-start | bytes 491524
  203.1 30.7 %copy-start.80 = (f32[5,16,16]{2,1,0:T(8,128)}, f32[5,16,16]{2,1,0:T(8,128)S(1)}, u32[]{:S(2)}) copy-start(f32[5,16,16]{2,1,0:T(8,128)S(1)} %copy.210) | copy-start | bytes 15364
  205.3 28.4 %copy-start.81 = (f32[5,16,16]{2,1,0:T(8,128)}, f32[5,16,16]{2,1,0:T(8,128)S(1)}, u32[]{:S(2)}) copy-start(f32[5,16,16]{2,1,0:T(8,128)S(1)} %copy.211) | copy-start | bytes 15364
  254.6 57.9 %copy-start = (f32[384,1280]{1,0:T(8,128)}, f32[384,1280]{1,0:T(8,128)S(1)}, u32[]{:S(2)}) copy-start(f32[384,1280]{1,0:T(8,128)S(1)} %get-tuple-element.38.c_ref) | copy-start | bytes 5898244
  256.1 20.5 %collective-permute-start.1 = (f32[2,32,1280]{2,1,0:T(8,128)}, f32[2,32,1280]{2,1,0:T(8,128)}, u32[]{:S(2)}, u32[]{:S(2)}) collective-permute-start(f32[2,32,1280]{2,1,0:T(8,128)} %pad_maximum_fusion.33), channel_id=1, source_target_pairs={{0,2},{2,0},{1,3},{3,1},{4,6},{6,4},{5,7},{7,5},{8,10},{10,8},{9,1... | collective-permute-start | bytes 983048 | tf_op jit(solution)/shard_map/ppermute | solution.py:209
  276.6 259.9 %all-gather.17.cloned.1.call-start = ((), (), s32[]{:S(2)}) async-start(), calls=%async_computation.13 | async-start | bytes 4915200 | tf_op jit(solution)/shard_map/all_gather | solution.py:382
  277.8 5.9 collective-permute-start.2
  283.7 34.5 %slice-start.4 = ((s8[6553600]{0:T(1024)(128)(4,1)}), s8[4194304]{0:T(1024)(128)(4,1)S(1)}, s32[]{:S(2)}) async-start(s8[6553600]{0:T(1024)(128)(4,1)} %bitcast.568), calls=%async_computation.23 | async-start | bytes 8388608
  283.8 11.1 collective-permute-start.3
  288.4 24.1 %collective-permute-start.4 = (bf16[2,32,1280]{2,1,0:T(8,128)(2,1)S(1)}, bf16[2,32,1280]{2,1,0:T(8,128)(2,1)S(1)}, u32[]{:S(2)}, u32[]{:S(2)}) collective-permute-start(bf16[2,32,1280]{2,1,0:T(8,128)(2,1)S(1)} %pad_maximum_fusion.35), channel_id=1, source_target_pairs={{0,16},{8,24},{1,17},{9,25},{2,18},{10,26},{3,19},{11,27},{4,20},{... | collective-permute-start | bytes 491528 | tf_op jit(solution)/shard_map/ppermute | solution.py:274
  293.7 18.8 %collective-permute-start.5 = (bf16[1,32,1280]{2,1,0:T(8,128)(2,1)S(1)}, bf16[1,32,1280]{2,1,0:T(8,128)(2,1)S(1)}, u32[]{:S(2)}, u32[]{:S(2)}) collective-permute-start(bf16[1,32,1280]{2,1,0:T(8,128)(2,1)S(1)} %get-tuple-element.157), channel_id=1, source_target_pairs={{0,24},{1,25},{2,26},{3,27},{4,28},{5,29},{6,30},{7,31}} | collective-permute-start | bytes 245768 | tf_op jit(solution)/shard_map/ppermute | solution.py:274
  322.1 14.2 %collective-permute-start.6 = (bf16[192,2560]{1,0:T(8,128)(2,1)}, bf16[192,2560]{1,0:T(8,128)(2,1)}, u32[]{:S(2)}, u32[]{:S(2)}) collective-permute-start(bf16[192,2560]{1,0:T(8,128)(2,1)} %dynamic-slice_convert_fusion.1), channel_id=1, source_target_pairs={{0,1},{1,0},{2,3},{3,2},{4,5},{5,4},{6,7},{7,6},{8,9},{9,8},{10,11... | collective-permute-start | bytes 2949128 | tf_op jit(solution)/shard_map/ppermute | solution.py:209
  324.6 117.8 %copy-start.17 = (bf16[192,2560]{1,0:T(8,128)(2,1)}, bf16[192,2560]{1,0:T(8,128)(2,1)S(1)}, u32[]{:S(2)}) copy-start(bf16[192,2560]{1,0:T(8,128)(2,1)S(1)} %get-tuple-element.242) | copy-start | bytes 2949124
  342.2 14.3 %collective-permute-start.7 = (bf16[192,2560]{1,0:T(8,128)(2,1)}, bf16[192,2560]{1,0:T(8,128)(2,1)}, u32[]{:S(2)}, u32[]{:S(2)}) collective-permute-start(bf16[192,2560]{1,0:T(8,128)(2,1)} %multiply_convert_fusion), channel_id=1, source_target_pairs={{0,1},{1,0},{2,3},{3,2},{4,5},{5,4},{6,7},{7,6},{8,9},{9,8},{10,11... | collective-permute-start | bytes 2949128 | tf_op jit(solution)/shard_map/ppermute | solution.py:209
  344.7 39.7 %collective-permute-start.14 = (bf16[384,2560]{1,0:T(8,128)(2,1)}, bf16[384,2560]{1,0:T(8,128)(2,1)}, u32[]{:S(2)}, u32[]{:S(2)}) collective-permute-start(bf16[384,2560]{1,0:T(8,128)(2,1)} %pad_maximum_fusion.15), channel_id=1, source_target_pairs={{0,4},{4,0},{1,5},{5,1},{2,6},{6,2},{3,7},{7,3},{8,12},{12,8},{9,1... | collective-permute-start | bytes 5898248 | tf_op jit(solution)/shard_map/ppermute | solution.py:209
  349.7 204.4 %all-gather.19.cloned.1.call-start = ((), (), s32[]{:S(2)}) async-start(), calls=%async_computation.14 | async-start | bytes 4915200 | tf_op jit(solution)/shard_map/all_gather | solution.py:382
  358.1 68.4 %collective-permute-start.8 = (bf16[384,2560]{1,0:T(8,128)(2,1)S(1)}, bf16[384,2560]{1,0:T(8,128)(2,1)S(1)}, u32[]{:S(2)}, u32[]{:S(2)}) collective-permute-start(bf16[384,2560]{1,0:T(8,128)(2,1)S(1)} %pad_maximum_fusion.13), channel_id=1, source_target_pairs={{0,4},{4,0},{1,5},{5,1},{2,6},{6,2},{3,7},{7,3},{8,12},{12,8},{9,1... | collective-permute-start | bytes 5898248 | tf_op jit(solution)/shard_map/ppermute | solution.py:209
  387.8 52.0 %copy-start.151 = (s32[4]{0:T(128)S(1)}, s32[4]{0:T(128)}, u32[]{:S(2)}) copy-start(s32[4]{0:T(128)} %constant.85.clone) | copy-start | bytes 52
  387.8 53.3 %copy-start.150 = (s32[4]{0:T(128)S(1)}, s32[4]{0:T(128)}, u32[]{:S(2)}) copy-start(s32[4]{0:T(128)} %constant.86.clone) | copy-start | bytes 52
  387.8 54.6 %collective-permute-start.15 = (bf16[768,2560]{1,0:T(8,128)(2,1)}, bf16[768,2560]{1,0:T(8,128)(2,1)}, u32[]{:S(2)}, u32[]{:S(2)}) collective-permute-start(bf16[768,2560]{1,0:T(8,128)(2,1)} %pad_maximum_fusion.5), channel_id=1, source_target_pairs={{0,2},{2,0},{1,3},{3,1},{4,6},{6,4},{5,7},{7,5},{8,10},{10,8},{9,1... | collective-permute-start | bytes 11796488 | tf_op jit(solution)/shard_map/ppermute | solution.py:209
  430.4 20.3 %collective-permute-start.9 = (bf16[768,2560]{1,0:T(8,128)(2,1)}, bf16[768,2560]{1,0:T(8,128)(2,1)}, u32[]{:S(2)}, u32[]{:S(2)}) collective-permute-start(bf16[768,2560]{1,0:T(8,128)(2,1)} %pad_maximum_fusion.4), channel_id=1, source_target_pairs={{0,2},{2,0},{1,3},{3,1},{4,6},{6,4},{5,7},{7,5},{8,10},{10,8},{9,1... | collective-permute-start | bytes 11796488 | tf_op jit(solution)/shard_map/ppermute | solution.py:209
  442.3 578.5 %reduce-scatter.19.cloned.1.call-start = ((), (), s32[]{:S(2)}) async-start(), calls=%async_computation.15 | async-start | bytes 4915200 | tf_op jit(solution)/shard_map/reduce_scatter | solution.py:429
  442.4 24.1 %copy-start.139 = (pred[256]{0:T(512)(128)(4,1)}, pred[256]{0:T(512)(128)(4,1)S(1)}, u32[]{:S(2)}) copy-start(pred[256]{0:T(512)(128)(4,1)S(1)} %get-tuple-element.320) | copy-start | bytes 772
  442.4 59.4 %copy-start.141 = (pred[256]{0:T(512)(128)(4,1)}, pred[256]{0:T(512)(128)(4,1)S(1)}, u32[]{:S(2)}) copy-start(pred[256]{0:T(512)(128)(4,1)S(1)} %get-tuple-element.319) | copy-start | bytes 772
  450.7 51.1 %copy-start.120 = (f32[1,256]{1,0:T(1,128)}, f32[1,256]{1,0:T(1,128)S(1)}, u32[]{:S(2)}) copy-start(f32[1,256]{1,0:T(1,128)S(1)} %get-tuple-element.310) | copy-start | bytes 3076
  450.7 51.1 %copy-start.122 = (f32[1,256]{1,0:T(1,128)}, f32[1,256]{1,0:T(1,128)S(1)}, u32[]{:S(2)}) copy-start(f32[1,256]{1,0:T(1,128)S(1)} %get-tuple-element.311) | copy-start | bytes 3076
  486.7 534.1 %reduce-scatter.21.cloned.1.call-start = ((), (), s32[]{:S(2)}) async-start(), calls=%async_computation.16 | async-start | bytes 4915200 | tf_op jit(solution)/shard_map/reduce_scatter | solution.py:429
  486.8 92.5 %copy-start.147 = (pred[256]{0:T(512)(128)(4,1)}, pred[256]{0:T(512)(128)(4,1)S(1)}, u32[]{:S(2)}) copy-start(pred[256]{0:T(512)(128)(4,1)S(1)} %get-tuple-element.317) | copy-start | bytes 772
  486.8 123.2 %copy-start.143 = (pred[256]{0:T(512)(128)(4,1)}, pred[256]{0:T(512)(128)(4,1)S(1)}, u32[]{:S(2)}) copy-start(pred[256]{0:T(512)(128)(4,1)S(1)} %get-tuple-element.318) | copy-start | bytes 772
  536.0 484.8 %reduce-scatter.23.cloned.1.call-start = ((), (), s32[]{:S(2)}) async-start(), calls=%async_computation.17 | async-start | bytes 4915200 | tf_op jit(solution)/shard_map/reduce_scatter | solution.py:429
  609.8 21.7 %collective-permute-start.16 = (bf16[768,2560]{1,0:T(8,128)(2,1)}, bf16[768,2560]{1,0:T(8,128)(2,1)}, u32[]{:S(2)}, u32[]{:S(2)}) collective-permute-start(bf16[768,2560]{1,0:T(8,128)(2,1)} %slice.1025), channel_id=1, source_target_pairs={{0,2},{2,0},{1,3},{3,1},{4,6},{6,4},{5,7},{7,5},{8,10},{10,8},{9,1... | collective-permute-start | bytes 11796488 | tf_op jit(solution)/shard_map/ppermute | solution.py:209
  631.4 389.4 %reduce-scatter.25.cloned.1.call-start = ((), (), s32[]{:S(2)}) async-start(), calls=%async_computation.18 | async-start | bytes 4915200 | tf_op jit(solution)/shard_map/reduce_scatter | solution.py:429
  639.3 44.5 %collective-permute-start.17 = (bf16[384,2560]{1,0:T(8,128)(2,1)}, bf16[384,2560]{1,0:T(8,128)(2,1)}, u32[]{:S(2)}, u32[]{:S(2)}) collective-permute-start(bf16[384,2560]{1,0:T(8,128)(2,1)} %slice.1027), channel_id=1, source_target_pairs={{0,4},{4,0},{1,5},{5,1},{2,6},{6,2},{3,7},{7,3},{8,12},{12,8},{9,1... | collective-permute-start | bytes 5898248 | tf_op jit(solution)/shard_map/ppermute | solution.py:209
  647.7 39.0 %copy-start.36 = (bf16[1536,256]{0,1:T(8,128)(2,1)S(1)}, bf16[1536,256]{0,1:T(8,128)(2,1)}, u32[]{:S(2)}) copy-start(bf16[1536,256]{0,1:T(8,128)(2,1)} %copy-done.35) | copy-start | bytes 2359300
  647.7 39.1 %copy-start.38 = (bf16[1536,256]{0,1:T(8,128)(2,1)S(1)}, bf16[1536,256]{0,1:T(8,128)(2,1)}, u32[]{:S(2)}) copy-start(bf16[1536,256]{0,1:T(8,128)(2,1)} %copy-done.37) | copy-start | bytes 2359300
  647.7 39.1 %copy-start.48 = (bf16[384,2560]{1,0:T(8,128)(2,1)S(1)}, bf16[384,2560]{1,0:T(8,128)(2,1)}, u32[]{:S(2)}) copy-start(bf16[384,2560]{1,0:T(8,128)(2,1)} %copy-done.46) | copy-start | bytes 5898244
  683.8 27.5 %slice-start.2 = ((s8[7864320]{0:T(1024)(128)(4,1)}), s8[4194304]{0:T(1024)(128)(4,1)S(1)}, s32[]{:S(2)}) async-start(s8[7864320]{0:T(1024)(128)(4,1)} %bitcast.561), calls=%async_computation.21 | async-start | bytes 8388608
  686.7 24.7 %slice-start.3 = ((s8[7864320]{0:T(1024)(128)(4,1)}), s8[3670016]{0:T(1024)(128)(4,1)S(1)}, s32[]{:S(2)}) async-start(s8[7864320]{0:T(1024)(128)(4,1)} %bitcast.561), calls=%async_computation.22 | async-start | bytes 7340032
  686.7 22.4 %collective-permute-start.18 = (bf16[192,2560]{1,0:T(8,128)(2,1)S(1)}, bf16[192,2560]{1,0:T(8,128)(2,1)S(1)}, u32[]{:S(2)}, u32[]{:S(2)}) collective-permute-start(bf16[192,2560]{1,0:T(8,128)(2,1)S(1)} %slice.1029), channel_id=1, source_target_pairs={{0,1},{1,0},{2,3},{3,2},{4,5},{5,4},{6,7},{7,6},{8,9},{9,8},{10,11... | collective-permute-start | bytes 2949128 | tf_op jit(solution)/shard_map/ppermute | solution.py:209
  710.9 21.6 %collective-permute-start.19 = (bf16[192,2560]{1,0:T(8,128)(2,1)S(1)}, bf16[192,2560]{1,0:T(8,128)(2,1)}, u32[]{:S(2)}, u32[]{:S(2)}) collective-permute-start(bf16[192,2560]{1,0:T(8,128)(2,1)S(1)} %get-tuple-element.148), channel_id=1, source_target_pairs={{0,1},{1,0},{2,3},{3,2},{4,5},{5,4},{6,7},{7,6},{8,9},{9,8},{10,11... | collective-permute-start | bytes 2949128 | tf_op jit(solution)/shard_map/ppermute | solution.py:209
  730.8 402.8 %reduce-scatter.15.cloned.1.call-start = ((), (), s32[]{:S(2)}) async-start(), calls=%async_computation.8 | async-start | bytes 9052160 | tf_op jit(solution)/shard_map/reduce_scatter | solution.py:492
  745.6 11.1 collective-permute-start.20
  756.8 5.0 collective-permute-start.21
  762.0 14.2 %collective-permute-start.22 = (bf16[2,32,1280]{2,1,0:T(8,128)(2,1)S(1)}, bf16[2,32,1280]{2,1,0:T(8,128)(2,1)S(1)}, u32[]{:S(2)}, u32[]{:S(2)}) collective-permute-start(bf16[2,32,1280]{2,1,0:T(8,128)(2,1)S(1)} %pad_maximum_fusion.37), channel_id=1, source_target_pairs={{8,0},{16,8},{24,16},{9,1},{17,9},{25,17},{10,2},{18,10},{26,18},{... | collective-permute-start | bytes 491528 | tf_op jit(solution)/shard_map/ppermute | solution.py:274
  763.9 18.7 %collective-permute-start.23 = (bf16[2,32,1280]{2,1,0:T(8,128)(2,1)S(1)}, bf16[2,32,1280]{2,1,0:T(8,128)(2,1)S(1)}, u32[]{:S(2)}, u32[]{:S(2)}) collective-permute-start(bf16[2,32,1280]{2,1,0:T(8,128)(2,1)S(1)} %pad_maximum_fusion.37), channel_id=1, source_target_pairs={{16,0},{24,8},{17,1},{25,9},{18,2},{26,10},{19,3},{27,11},{20,4},{... | collective-permute-start | bytes 491528 | tf_op jit(solution)/shard_map/ppermute | solution.py:274
  765.2 17.4 %collective-permute-start.24 = (bf16[1,32,1280]{2,1,0:T(8,128)(2,1)S(1)}, bf16[1,32,1280]{2,1,0:T(8,128)(2,1)S(1)}, u32[]{:S(2)}, u32[]{:S(2)}) collective-permute-start(bf16[1,32,1280]{2,1,0:T(8,128)(2,1)S(1)} %get-tuple-element.151), channel_id=1, source_target_pairs={{24,0},{25,1},{26,2},{27,3},{28,4},{29,5},{30,6},{31,7}} | collective-permute-start | bytes 245768 | tf_op jit(solution)/shard_map/ppermute | solution.py:274
  792.4 17.5 %collective-permute-start.25 = (bf16[96,1280]{1,0:T(8,128)(2,1)S(1)}, bf16[96,1280]{1,0:T(8,128)(2,1)S(1)}, u32[]{:S(2)}, u32[]{:S(2)}) collective-permute-start(bf16[96,1280]{1,0:T(8,128)(2,1)S(1)} %slice.1542), channel_id=1, source_target_pairs={{2,0},{4,2},{6,4},{8,6},{10,8},{12,10},{14,12},{16,14},{18,16},{20... | collective-permute-start | bytes 737288 | tf_op jit(solution)/shard_map/ppermute | solution.py:453
  820.1 13.6 %collective-permute-start.26 = (bf16[192,2560]{1,0:T(8,128)(2,1)}, bf16[192,2560]{1,0:T(8,128)(2,1)S(1)}, u32[]{:S(2)}, u32[]{:S(2)}) collective-permute-start(bf16[192,2560]{1,0:T(8,128)(2,1)} %dynamic-slice_convert_fusion), channel_id=1, source_target_pairs={{0,1},{1,0},{2,3},{3,2},{4,5},{5,4},{6,7},{7,6},{8,9},{9,8},{10,11... | collective-permute-start | bytes 2949128 | tf_op jit(solution)/shard_map/ppermute | solution.py:209
  834.8 3.3 collective-permute-start.28
  845.3 294.8 %reduce-scatter.17.cloned.1.call-start = ((), (), s32[]{:S(2)}) async-start(), calls=%async_computation.9 | async-start | bytes 13926400 | tf_op jit(solution)/shard_map/reduce_scatter | solution.py:491
  903.1 31.3 %collective-permute-start.10 = (bf16[768,2560]{1,0:T(8,128)(2,1)}, bf16[768,2560]{1,0:T(8,128)(2,1)}, u32[]{:S(2)}, u32[]{:S(2)}) collective-permute-start(bf16[768,2560]{1,0:T(8,128)(2,1)} %slice.1018), channel_id=1, source_target_pairs={{0,2},{2,0},{1,3},{3,1},{4,6},{6,4},{5,7},{7,5},{8,10},{10,8},{9,1... | collective-permute-start | bytes 11796488 | tf_op jit(solution)/shard_map/ppermute | solution.py:209
  939.0 50.2 %collective-permute-start.11 = (bf16[384,2560]{1,0:T(8,128)(2,1)S(1)}, bf16[384,2560]{1,0:T(8,128)(2,1)S(1)}, u32[]{:S(2)}, u32[]{:S(2)}) collective-permute-start(bf16[384,2560]{1,0:T(8,128)(2,1)S(1)} %slice.1020), channel_id=1, source_target_pairs={{0,4},{4,0},{1,5},{5,1},{2,6},{6,2},{3,7},{7,3},{8,12},{12,8},{9,1... | collective-permute-start | bytes 5898248 | tf_op jit(solution)/shard_map/ppermute | solution.py:209
  989.1 25.5 %copy-start.19 = (bf16[192,2560]{1,0:T(8,128)(2,1)S(1)}, bf16[192,2560]{1,0:T(8,128)(2,1)}, u32[]{:S(2)}) copy-start(bf16[192,2560]{1,0:T(8,128)(2,1)} %copy-done.17) | copy-start | bytes 2949124
  990.9 23.8 %copy-start.16 = (f32[192,2560]{1,0:T(8,128)S(1)}, f32[192,2560]{1,0:T(8,128)}, u32[]{:S(2)}) copy-start(f32[192,2560]{1,0:T(8,128)} %copy-done.14) | copy-start | bytes 5898244
  990.9 23.8 %copy-start.102 = (f32[192]{0:T(256)S(1)}, f32[192]{0:T(256)}, u32[]{:S(2)}) copy-start(f32[192]{0:T(256)} %copy-done.100) | copy-start | bytes 2308
  990.9 23.8 %copy-start.129 = (f32[192]{0:T(256)S(1)}, f32[192]{0:T(256)}, u32[]{:S(2)}) copy-start(f32[192]{0:T(256)} %copy-done.128) | copy-start | bytes 2308
  991.9 22.7 %collective-permute-start.12 = (bf16[192,2560]{1,0:T(8,128)(2,1)}, bf16[192,2560]{1,0:T(8,128)(2,1)}, u32[]{:S(2)}, u32[]{:S(2)}) collective-permute-start(bf16[192,2560]{1,0:T(8,128)(2,1)} %slice.1022), channel_id=1, source_target_pairs={{0,1},{1,0},{2,3},{3,2},{4,5},{5,4},{6,7},{7,6},{8,9},{9,8},{10,11... | collective-permute-start | bytes 2949128 | tf_op jit(solution)/shard_map/ppermute | solution.py:209
  1019.8 21.2 %collective-permute-start.27 = (bf16[192,2560]{1,0:T(8,128)(2,1)}, bf16[192,2560]{1,0:T(8,128)(2,1)S(1)}, u32[]{:S(2)}, u32[]{:S(2)}) collective-permute-start(bf16[192,2560]{1,0:T(8,128)(2,1)} %get-tuple-element.237), channel_id=1, source_target_pairs={{0,1},{1,0},{2,3},{3,2},{4,5},{5,4},{6,7},{7,6},{8,9},{9,8},{10,11... | collective-permute-start | bytes 2949128 | tf_op jit(solution)/shard_map/ppermute | solution.py:209
  1025.4 71.7 %all-to-all-start.1 = ((bf16[4,4,160,768]{3,2,0,1:T(8,128)(2,1)}), bf16[4,4,160,768]{3,2,0,1:T(8,128)(2,1)}, u32[]{:S(2)}, u32[]{:S(2)}) async-start(bf16[4,4,160,768]{3,2,0,1:T(8,128)(2,1)} %copy.241), calls=%async_computation.3 | async-start | bytes 7864320 | tf_op jit(solution)/shard_map/all_to_all | solution.py:495
  1033.1 28.9 %collective-permute-start.13 = (bf16[192,2560]{1,0:T(8,128)(2,1)S(1)}, bf16[192,2560]{1,0:T(8,128)(2,1)S(1)}, u32[]{:S(2)}, u32[]{:S(2)}) collective-permute-start(bf16[192,2560]{1,0:T(8,128)(2,1)S(1)} %copy-done.34), channel_id=1, source_target_pairs={{0,1},{1,0},{2,3},{3,2},{4,5},{5,4},{6,7},{7,6},{8,9},{9,8},{10,11... | collective-permute-start | bytes 2949128 | tf_op jit(solution)/shard_map/ppermute | solution.py:209
  (137 other events, 1044.0 us)
Sparse Core Ops, SparseCore 0:
  24.8 144.6 all-gather.10
  185.9 83.0 all-gather.12
  276.7 87.9 all-gather.14
  366.1 75.9 all-gather.16
  443.5 74.9 all-gather.18
  520.7 73.6 reduce-scatter.18
  596.7 73.0 reduce-scatter.20
  672.1 73.0 reduce-scatter.22
  747.5 87.9 reduce-scatter.24
  845.4 134.4 reduce-scatter.14
  983.9 154.3 reduce-scatter.16

commit v2 on v1

v2 whole, which is shorter than its diff:
```python
import functools

import jax
import jax.numpy as jnp
from jax import lax
from jax.experimental import pallas as pl
from jax.experimental.pallas import tpu as pltpu
from jax.sharding import Mesh, PartitionSpec as P

F32, BF16 = jnp.float32, jnp.bfloat16
LANES = 128
PLANES = 4
CORES = 2
CHUNKS = 2
VMEM_BYTES = 56 * 1024 * 1024
SMALL = pl.CostEstimate(flops=1, bytes_accessed=1, transcendentals=0)
DP = ("z", "x", "c")
GELU_A, GELU_B = 0.7978845608028654, 0.044715


def gelu_parts(v):
    square = v * v
    bent = jnp.tanh(GELU_A * v * (1.0 + GELU_B * square))
    half = 0.5 * (1.0 + bent)
    slope = half + 0.5 * v * (1.0 - bent * bent) * (GELU_A * (1.0 + 3.0 * GELU_B * square))
    return v * half, slope


def gelu(v):
    return v * (0.5 * (1.0 + jnp.tanh(GELU_A * v * (1.0 + GELU_B * v * v))))


def dot(a, b, dims=((1,), (0,))):
    return lax.dot_general(a, b, (dims, ((), ())), preferred_element_type=F32)


def tie(*values):
    return lax.optimization_barrier(values)


def input_scale(decay, at_start):
    spare = 1.0 - decay * decay
    scale = jnp.sqrt(jnp.maximum(spare, 0.001))
    return jnp.where(at_start, 1.0, scale), spare


def start_rows(first_ref, rows, seqs, width):
    row = lax.broadcasted_iota(jnp.int32, (rows, width), 0)
    return jnp.logical_and(row < seqs, first_ref[0] == 1)


def gates_kernel(first_ref, r_ref, v_ref, wi_ref, wd_ref, c_ref, si_ref, sd_ref, e_ref, p_ref, *, seqs, taps):
    rows, width = c_ref.shape
    halo = r_ref.shape[0] - rows
    conv = v_ref[taps : taps + 1, :] + v_ref[0:1, :] * r_ref[pl.ds(halo, rows), :]
    for k in range(1, taps):
        conv = conv + v_ref[k : k + 1, :] * r_ref[pl.ds(halo - k * seqs, rows), :]
    c_ref[...] = conv
    low = conv.astype(BF16)
    si = jax.nn.sigmoid(dot(low, wi_ref[...]) + v_ref[taps + 1 : taps + 2, :])
    sd = jax.nn.sigmoid(dot(low, wd_ref[...]) + v_ref[taps + 2 : taps + 3, :])
    si_ref[...] = si
    sd_ref[...] = sd
    decay = jnp.exp(sd * v_ref[taps + 3 : taps + 4, :])
    scale, _ = input_scale(decay, start_rows(first_ref, rows, seqs, width))
    source = conv * si * scale
    state, total = source[:seqs], decay[:seqs]
    for p in range(1, rows // seqs):
        a = decay[p * seqs : (p + 1) * seqs]
        state = a * state + source[p * seqs : (p + 1) * seqs]
        total = total * a
    e_ref[...] = state
    p_ref[...] = total


def states_kernel(first_ref, c_ref, si_ref, sd_ref, b_ref, v_ref, carry_ref, s_ref, m_ref, *, seqs, taps):
    rows, width = c_ref.shape
    decay = jnp.exp(sd_ref[...] * v_ref[taps + 3 : taps + 4, :])
    scale, _ = input_scale(decay, start_rows(first_ref, rows, seqs, width))
    source = c_ref[...] * si_ref[...] * scale
    state = carry_ref[...]
    for p in range(rows // seqs):
        at = slice(p * seqs, (p + 1) * seqs)
        state = decay[at] * state + source[at]
        s_ref[pl.ds(p * seqs, seqs), :] = state
    m_ref[...] = (gelu(b_ref[...]) * s_ref[...]).astype(BF16)


def branch_kernel(dm_ref, b_ref, s_ref, sd_ref, v_ref, t_ref, db_ref, e_ref, sum_ref, *, seqs, taps):
    rows, _ = t_ref.shape
    value, slope = gelu_parts(b_ref[...])
    dm = dm_ref[...]
    t = dm * value
    t_ref[...] = t
    db = (dm * s_ref[...] * slope).astype(BF16)
    db_ref[...] = db
    sum_ref[...] = jnp.broadcast_to(jnp.sum(db.astype(F32), axis=0, keepdims=True), sum_ref.shape)
    decay = jnp.exp(sd_ref[...] * v_ref[taps + 3 : taps + 4, :])
    count = rows // seqs
    grad = t[(count - 1) * seqs :]
    for p in range(count - 2, -1, -1):
        grad = t[p * seqs : (p + 1) * seqs] + decay[(p + 1) * seqs : (p + 2) * seqs] * grad
    e_ref[...] = decay[:seqs] * grad


def core_kernel(
    first_ref, t_ref, c_ref, si_ref, sd_ref, s_ref, r_ref, v_ref, carry_ref, late_ref, wi_ref, wd_ref,
    dc_ref, gi_ref, gd_ref, sum_ref, ds_ref, *, seqs, taps,
):
    rows, width = c_ref.shape
    halo = r_ref.shape[0] - rows
    count = rows // seqs
    si, sd, conv = si_ref[...], sd_ref[...], c_ref[...]
    rate = v_ref[taps + 3 : taps + 4, :]
    decay = jnp.exp(sd * rate)
    at_start = start_rows(first_ref, rows, seqs, width)
    scale, spare = input_scale(decay, at_start)
    grad = late_ref[...]
    for p in range(count - 1, -1, -1):
        grad = t_ref[pl.ds(p * seqs, seqs), :] + grad
        ds_ref[pl.ds(p * seqs, seqs), :] = grad
        grad = decay[p * seqs : (p + 1) * seqs] * grad
    ds = ds_ref[...]
    before = carry_ref[...] if count == 1 else jnp.concatenate([carry_ref[...], s_ref[pl.ds(0, rows - seqs), :]], axis=0)
    bends = jnp.logical_and(spare > 0.001, jnp.logical_not(at_start))
    d_scale = jnp.where(bends, -(decay * decay) / scale, 0.0)
    gated = ds * conv
    d_log = ds * before * decay + gated * si * d_scale
    d_in = (gated * scale * si * (1.0 - si)).astype(BF16)
    d_dec = (d_log * rate * sd * (1.0 - sd)).astype(BF16)
    low = conv.astype(BF16)
    gi_ref[...] = dot(low, d_in, ((0,), (0,))).astype(gi_ref.dtype)
    gd_ref[...] = dot(low, d_dec, ((0,), (0,))).astype(gd_ref.dtype)
    dc = ds * si * scale + dot(d_in, wi_ref[...], ((1,), (1,))) + dot(d_dec, wd_ref[...], ((1,), (1,)))
    dc_ref[...] = dc

    def total(values):
        return jnp.sum(values, axis=0, keepdims=True)

    parts = [
        total(d_in.astype(F32)),
        total(d_dec.astype(F32)),
        total(d_log * sd) * v_ref[taps + 4 : taps + 5, :],
        total(dc),
    ]
    for k in range(taps):
        parts.append(total(r_ref[pl.ds(halo - k * seqs, rows), :] * dc))
    sum_ref[...] = jnp.concatenate(parts, axis=0)


def head_calls(heads, width, rows, halo_rows, seqs, taps):
    def cols(n):
        return pl.BlockSpec((n, width), lambda h: (0, h))

    flag = pl.BlockSpec(memory_space=pltpu.SMEM)
    full = heads * width
    params = pltpu.CompilerParams(vmem_limit_bytes=48 * 1024 * 1024)
    vec_rows = 16

    def shape(n, kind=F32):
        return jax.ShapeDtypeStruct((n, full), kind)

    def call(kernel, ins, outs, shapes, scratch=(), flops=0):
        return pl.pallas_call(
            functools.partial(kernel, seqs=seqs, taps=taps),
            grid=(heads,),
            in_specs=ins,
            out_specs=outs,
            out_shape=shapes,
            scratch_shapes=list(scratch),
            compiler_params=params,
            cost_estimate=SMALL,
        )

    unit = 2 * rows * full * width
    return (
        call(
            gates_kernel,
            [flag, cols(halo_rows), cols(vec_rows), cols(width), cols(width)],
            [cols(rows), cols(rows), cols(rows), cols(seqs), cols(seqs)],
            [shape(rows), shape(rows), shape(rows), shape(seqs), shape(seqs)],
            flops=2 * unit,
        ),
        call(
            states_kernel,
            [flag, cols(rows), cols(rows), cols(rows), cols(rows), cols(vec_rows), cols(seqs)],
            [cols(rows), cols(rows)],
            [shape(rows), shape(rows, BF16)],
        ),
        call(
            branch_kernel,
            [cols(rows), cols(rows), cols(rows), cols(rows), cols(vec_rows)],
            [cols(rows), cols(rows), cols(seqs), cols(8)],
            [shape(rows), shape(rows, BF16), shape(seqs), shape(8)],
        ),
        call(
            core_kernel,
            [flag, cols(rows), cols(rows), cols(rows), cols(rows), cols(rows), cols(halo_rows), cols(vec_rows),
             cols(seqs), cols(seqs), cols(width), cols(width)],
            [cols(rows), cols(width), cols(width), cols(4 + taps)],
            [shape(rows), shape(width, BF16), shape(width, BF16), shape(4 + taps)],
            scratch=[pltpu.VMEM((rows, width), F32)],
            flops=4 * unit,
        ),
    )


def row_tile(rows):
    return max(n for n in (512, 256, 128, 64, 32, 16) if rows % n == 0)


def feed_kernel(at_ref, x_ref, d_ref, w_ref, b_ref, h_ref, g_ref, *, first_unit):
    step = h_ref.shape[1]
    pre = dot(x_ref[...], w_ref[:, : 2 * step]) + b_ref[...]
    d_hidden = dot(d_ref[...], w_ref[:, 2 * step :])
    gate, up = pre[:, :step], pre[:, step:]
    mine = lax.broadcasted_iota(jnp.int32, gate.shape, 1) + first_unit < at_ref[0]
    value, slope = gelu_parts(gate)
    h_ref[...] = jnp.where(mine, value * up, 0.0).astype(BF16)
    g_ref[:, :step] = jnp.where(mine, d_hidden * up * slope, 0.0).astype(BF16)
    g_ref[:, step:] = jnp.where(mine, d_hidden * value, 0.0).astype(BF16)


def feed(owned, x, d, weights, bias, first_unit):
    rows, width = x.shape
    step = weights.shape[1] // 3
    tile = row_tile(rows)
    return pl.pallas_call(
        functools.partial(feed_kernel, first_unit=first_unit),
        grid=(rows // tile,),
        in_specs=[
            pl.BlockSpec(memory_space=pltpu.SMEM),
            pl.BlockSpec((tile, width), lambda i: (i, 0)),
            pl.BlockSpec((tile, width), lambda i: (i, 0)),
            pl.BlockSpec((width, 3 * step), lambda i: (0, 0)),
            pl.BlockSpec((1, 2 * step), lambda i: (0, 0)),
        ],
        out_specs=[
            pl.BlockSpec((tile, step), lambda i: (i, 0)),
            pl.BlockSpec((tile, 2 * step), lambda i: (i, 0)),
        ],
        out_shape=[
            jax.ShapeDtypeStruct((rows, step), BF16),
            jax.ShapeDtypeStruct((rows, 2 * step), BF16),
        ],
        compiler_params=pltpu.CompilerParams(vmem_limit_bytes=VMEM_BYTES),
        cost_estimate=SMALL,
    )(owned, x, d, weights, bias)


def grad_kernel(x_ref, d_ref, g_ref, h_ref, o_ref, sum_ref):
    step = h_ref.shape[1]

    @pl.when(pl.program_id(0) == 0)
    def _():
        total = jnp.sum(g_ref[...].astype(F32), axis=0, keepdims=True)
        sum_ref[...] = jnp.broadcast_to(total, sum_ref.shape)

    o_ref[:, : 2 * step] = dot(x_ref[...], g_ref[...], ((0,), (0,))).astype(BF16)
    o_ref[:, 2 * step :] = dot(d_ref[...], h_ref[...], ((0,), (0,))).astype(BF16)


def feed_grads(x, d, d_pre, hidden):
    rows, width = x.shape
    step = hidden.shape[1]
    tile = 512 if width % 512 == 0 else width
    return pl.pallas_call(
        grad_kernel,
        grid=(width // tile,),
        in_specs=[
            pl.BlockSpec((rows, tile), lambda i: (0, i)),
            pl.BlockSpec((rows, tile), lambda i: (0, i)),
            pl.BlockSpec((rows, 2 * step), lambda i: (0, 0)),
            pl.BlockSpec((rows, step), lambda i: (0, 0)),
        ],
        out_specs=[pl.BlockSpec((tile, 3 * step), lambda i: (i, 0)), pl.BlockSpec((8, 2 * step), lambda i: (0, 0))],
        out_shape=[jax.ShapeDtypeStruct((width, 3 * step), BF16), jax.ShapeDtypeStruct((8, 2 * step), F32)],
        compiler_params=pltpu.CompilerParams(vmem_limit_bytes=VMEM_BYTES),
        cost_estimate=SMALL,
    )(x, d, d_pre, hidden)


def back_kernel(*refs):
    count = (len(refs) - 1) // 2
    out = dot(refs[0][...], refs[count][...], ((1,), (1,)))
    for k in range(1, count):
        out = out + dot(refs[k][...], refs[count + k][...], ((1,), (1,)))
    refs[-1][...] = out.astype(BF16)


def feed_back(values, weights, part, block, blocks):
    rows, cols = values[0].shape
    rows = rows // blocks
    width = weights[0].shape[0]
    tile = 512 if width % 512 == 0 else width
    return pl.pallas_call(
        back_kernel,
        grid=(width // tile,),
        in_specs=[pl.BlockSpec((rows, cols), lambda i: (part, 0)) for _ in values]
        + [pl.BlockSpec((tile, cols), lambda i: (i, block)) for _ in weights],
        out_specs=pl.BlockSpec((rows, tile), lambda i: (0, i)),
        out_shape=jax.ShapeDtypeStruct((rows, width), BF16),
        compiler_params=pltpu.CompilerParams(vmem_limit_bytes=VMEM_BYTES),
        cost_estimate=SMALL,
    )(*values, *weights)


def swap(v, axis):
    return lax.ppermute(v, axis, [(0, 1), (1, 0)])


def gather_rows(v, axis):
    if lax.axis_size(axis) == 2:
        return jnp.concatenate([v, swap(v, axis)], axis=0)
    return lax.all_gather(v, axis, axis=0, tiled=True)


def scatter_rows(v, axis):
    if lax.axis_size(axis) == 2:
        half = v.shape[0] // 2
        return (v[:half].astype(F32) + swap(v[half:], axis).astype(F32)).astype(BF16)
    return lax.psum_scatter(v, axis, scatter_dimension=0, tiled=True)


def gather_plane(v):
    if lax.axis_size("x") != 2:
        return gather_rows(gather_rows(v, "x"), "y")
    half = v.shape[0] // 2
    a, b = v[:half], v[half:]
    ax, by = swap(a, "x"), swap(b, "y")
    a, b = jnp.concatenate([a, ax], axis=0), jnp.concatenate([b, by], axis=0)
    return jnp.concatenate([a, swap(a, "y"), b, swap(b, "x")], axis=0)


def replicated_plane(own, side):
    if lax.axis_size("x") != 2:
        return gather_plane(own)
    half = own.shape[0] // 2
    near = swap(own, "x")
    far = swap(near, "y")
    return jnp.concatenate(
        [own[:half], near[:half], side[:half], far[:half], own[half:], side[half:], near[half:], far[half:]], axis=0
    )


def scatter_plane(v, *beside):
    if lax.axis_size("x") != 2:
        return (scatter_rows(scatter_rows(v, "y"), "x").astype(F32), *beside)
    half = v.shape[0] // 2
    quarter = half // 2
    a = v[:half].reshape(2, 2, quarter // 2, -1).swapaxes(0, 1).reshape(half, -1)
    b = v[half:].reshape(2, 2, quarter // 2, -1).swapaxes(0, 1).reshape(half, -1)
    got_a, got_b, *beside = tie(swap(a[quarter:], "x"), swap(b[quarter:], "y"), *beside)

    def fold(rows, got):
        return rows.astype(F32) + got.astype(F32)

    a, b = fold(a[:quarter], got_a).astype(BF16), fold(b[:quarter], got_b).astype(BF16)
    keep = quarter // 2
    a, b = fold(a[:keep], swap(a[keep:], "y")), fold(b[:keep], swap(b[keep:], "x"))
    return (jnp.concatenate([a, b], axis=0), *beside)


def scatter_side(v):
    if lax.axis_size("x") != 2:
        return scatter_rows(v, "y")
    count = v.shape[0] // 8
    a, b = v[: 4 * count].reshape(4, count, -1), v[4 * count :].reshape(4, count, -1)
    keep = jnp.concatenate([a[0], b[0], a[1], b[2]], axis=0)
    send = jnp.concatenate([a[2], b[1], a[3], b[3]], axis=0)
    return keep, swap(send, "y")


def gather_group(v):
    return gather_rows(gather_rows(v, "x"), "c")


def deal_group(v):
    mid, count = lax.axis_size("x"), v.shape[1]
    v = v.reshape(PLANES, mid * CORES, -1, count)
    if mid != 2:
        got = lax.all_gather(v, "x", axis=3, tiled=True)
        got = gather_cols(got)
        return lax.dynamic_index_in_dim(got, lax.axis_index(("x", "c")), 1, keepdims=False).reshape(-1, got.shape[-1])
    me = lax.axis_index(("x", "c"))
    parts = []
    for flip in (0, 2, 1, 3):
        part = lax.dynamic_index_in_dim(v, jnp.bitwise_xor(me, flip), 1, keepdims=False)
        parts.append(lax.ppermute(part, ("x", "c"), [(j, j ^ flip) for j in range(4)]) if flip else part)
    return jnp.concatenate(parts, axis=-1).reshape(-1, 4 * count)


def gather_cols(v):
    return jnp.concatenate([v, swap(v, "c")], axis=-1)


def fold_cores(v):
    v = v.reshape(lax.axis_size("z"), lax.axis_size("x"), CORES, *v.shape[1:])
    at = lax.axis_index("c")
    own = lax.dynamic_index_in_dim(v, at, 2, keepdims=False)
    return (own.astype(F32) + swap(lax.dynamic_index_in_dim(v, 1 - at, 2, keepdims=False), "c").astype(F32)).astype(BF16)


def fold_mid(v):
    if lax.axis_size("x") != 2:
        return lax.psum_scatter(v, "x", scatter_dimension=1, tiled=False)
    at = lax.axis_index("x")
    own = lax.dynamic_index_in_dim(v, at, 1, keepdims=False)
    return (own.astype(F32) + swap(lax.dynamic_index_in_dim(v, 1 - at, 1, keepdims=False), "x").astype(F32)).astype(BF16)


def fold_planes(v):
    return lax.psum_scatter(v, "z", scatter_dimension=0, tiled=False).astype(F32)


def sum_plane(v):
    v = v + swap(v, "c")
    return v + swap(v, "x") if lax.axis_size("x") == 2 else lax.psum(v, "x")


def sum_planes(v):
    count = lax.axis_size("z")
    return sum([lax.ppermute(v, "z", [(j, (j + far) % count) for j in range(count)]) for far in range(1, count)], v)


def to_slices(v):
    if lax.axis_size("x") != 2:
        return lax.all_to_all(v, ("x", "c"), split_axis=0, concat_axis=0, tiled=True)
    me = lax.axis_index(("x", "c"))
    pick = functools.partial(lax.dynamic_slice_in_dim, slice_size=1, axis=0)
    out = lax.dynamic_update_slice_in_dim(jnp.zeros_like(v), pick(v, me), me, 0)
    for flip in (1, 2, 3):
        other = jnp.bitwise_xor(me, flip)
        got = lax.ppermute(pick(v, other), ("x", "c"), [(j, j ^ flip) for j in range(4)])
        out = lax.dynamic_update_slice_in_dim(out, got, other, 0)
    return out


def halves(v, axis):
    half = v.shape[0] // 2
    at = lax.axis_index(axis)
    own = lax.dynamic_slice_in_dim(v, at * half, half, 0)
    return own, lax.dynamic_slice_in_dim(v, (1 - at) * half, half, 0)


def whole_rows(own, axis):
    other = swap(own, axis)
    low = lax.axis_index(axis) == 0
    return jnp.concatenate([jnp.where(low, own, other), jnp.where(low, other, own)], axis=0)


def ranks(value, axis):
    count = lax.axis_size(axis)
    if count == 2:
        other = swap(value, axis)
        low = lax.axis_index(axis) == 0
        return [jnp.where(low, value, other), jnp.where(low, other, value)]
    every = lax.all_gather(value, axis)
    return [every[j] for j in range(count)]


def carry_in(state, total, backward):
    pair = jnp.stack([state, total])
    inner = []
    for axis, kind in (("c", F32), ("x", BF16)):
        parts = [part.astype(F32) for part in ranks(pair.astype(kind), axis)]
        order = range(len(parts))
        at = lax.axis_index(axis)
        if backward:
            order, at = [len(parts) - 1 - j for j in order], len(parts) - 1 - at
        gone = jnp.stack([jnp.zeros_like(state), jnp.ones_like(total)])
        mine = gone
        for place, j in enumerate(order):
            mine = jnp.where(at == place, gone, mine)
            gone = jnp.stack([parts[j][0] + parts[j][1] * gone[0], parts[j][1] * gone[1]])
        inner.append(mine)
        pair = gone
    planes = lax.axis_size("z")
    sent = pair.astype(BF16)
    entering = jnp.zeros_like(state)
    steps = []
    for far in range(1, planes):
        if backward:
            route = [(j + far, j) for j in range(planes - far)]
        else:
            route = [(j, j + far) for j in range(planes - far)]
        steps.append(lax.ppermute(sent if far < planes - 1 else sent[:1], "z", route).astype(F32))
    for step in reversed(steps):
        entering = step[0] + (step[1] * entering if step.shape[0] == 2 else 0.0)
    for mine in reversed(inner):
        entering = mine[0] + mine[1] * entering
    return entering


def norm(v, gain):
    scale = lax.rsqrt(jnp.mean(v * v, axis=-1, keepdims=True) + 1e-6)
    return v * scale * gain, scale


def norm_back(v, scale, gain, d_out):
    scaled = gain * d_out
    mean = jnp.mean(v * scaled, axis=-1, keepdims=True)
    return scale * scaled - v * (scale * scale * scale * mean), jnp.sum(v * scale * d_out, axis=0)


def body(
    block_input, cotangent, seq_lengths, pre_gain, w_branch, b_branch, w_recur, b_recur, conv_kernel, conv_bias,
    input_gate_weight, input_gate_bias, decay_gate_weight, decay_gate_bias, decay_base, w_output, b_output,
    ffn_gain, w_expand, b_expand, w_shrink, b_shrink,
):
    mid = lax.axis_size("x")
    groups = PLANES * mid * CORES
    place = lax.axis_index(DP)
    side = lax.axis_index("y")
    seqs, pieces, width = block_input.shape
    rows = seqs * pieces
    taps, heads, head_part = conv_kernel.shape
    head_size = head_part * groups
    channels = heads * head_size
    part = w_recur.shape[0]
    units = w_shrink.shape[1]
    halo = (taps - 1) * seqs

    x_low = block_input.transpose(1, 0, 2).reshape(rows, width)
    positions = place * pieces + lax.broadcasted_iota(jnp.int32, (pieces, seqs), 0)
    mask = (positions < seq_lengths[None, :]).reshape(rows, 1)
    d_out = jnp.where(mask, cotangent.transpose(1, 0, 2).reshape(rows, width), 0).astype(BF16)
    early = lax.ppermute(x_low[rows - halo :], DP, [(j, j + 1) for j in range(groups - 1)])

    recur_stack = lax.all_gather(jnp.stack([w_recur, w_branch, w_output]), DP, axis=1, tiled=True)
    inlet_full = lax.all_gather(input_gate_weight.transpose(1, 0, 2).reshape(head_part, channels), DP, axis=0, tiled=True)
    decay_full = lax.all_gather(decay_gate_weight.transpose(1, 0, 2).reshape(head_part, channels), DP, axis=0, tiled=True)
    vectors = jnp.stack([b_branch, b_recur, *[conv_kernel[k] for k in range(taps)], conv_bias, input_gate_bias,
                         decay_gate_bias, decay_base])
    flat = jnp.concatenate([vectors.reshape(-1), pre_gain, b_output, ffn_gain, b_shrink, b_expand.reshape(-1)])
    every = lax.all_gather(flat, DP, axis=0, tiled=False).astype(F32)
    taken = 0

    def take(count):
        nonlocal taken
        taken += count
        return every[:, taken - count : taken]

    by_head = take(vectors.size).reshape(groups, -1, head_part).transpose(1, 0, 2).reshape(-1, channels)
    vec_branch, vec_recur, vec_taps = by_head[0], by_head[1], by_head[2 : 2 + taps]
    vec_base = by_head[5 + taps]
    gain_one, vec_output, gain_two, vec_shrink = [take(part).reshape(width) for _ in range(4)]
    blocks = b_expand.shape[1]
    vec_expand = take(2 * blocks * head_part).reshape(groups, 2, blocks, head_part).transpose(1, 2, 0, 3).reshape(2, units)
    gain_one, gain_two = 1.0 + gain_one, 1.0 + gain_two
    rates = jnp.stack([-8.0 * jax.nn.softplus(vec_base), -8.0 * jax.nn.sigmoid(vec_base)])
    coefs = jnp.concatenate([by_head[2 : 5 + taps], rates], axis=0)
    coefs = jnp.pad(coefs, ((0, 16 - coefs.shape[0]), (0, 0)))

    first = (place == 0).astype(jnp.int32).reshape(1)
    x_ext = jnp.concatenate([early, x_low], axis=0).astype(F32)
    normed_f, _ = norm(x_ext, gain_one)
    normed_ext = normed_f.astype(BF16)
    d_own, d_side = halves(d_out, "y")

    slices = mid * CORES
    tiles = units // LANES
    wide_tiles = -(-tiles // slices)
    wide = wide_tiles * LANES
    starts = [j * (tiles - wide_tiles) // (slices - 1) for j in range(slices)]
    owned = [(starts[j + 1] if j + 1 < slices else tiles) - starts[j] for j in range(slices)]
    chunks = CHUNKS if wide % (CHUNKS * LANES) == 0 else 1
    step = wide // chunks
    sent = []
    for j in range(slices):
        for k in range(chunks):
            at = starts[j] * LANES + k * step
            sent += [w_expand[0, :, at : at + step], w_expand[1, :, at : at + step], w_shrink[:, at : at + step]]
    per = 3 * chunks

    def to_send(low, high):
        mine = [jnp.concatenate(sent[j * per + 3 * k : j * per + 3 * k + 3], axis=1) for j in range(slices) for k in range(low, high)]
        return jnp.stack(mine).reshape(slices, high - low, part, 3 * step)

    def to_plane(mine):
        got = to_slices(mine)
        return [got[:, k].reshape(slices * part, 3 * step) for k in range(got.shape[1])]

    early_chunks = 1
    held = to_plane(to_send(0, early_chunks))
    later = to_send(early_chunks, chunks) if early_chunks < chunks else held[0]
    my_slice = lax.axis_index(("x", "c"))
    my_start = jnp.array(starts, jnp.int32)[my_slice] * LANES
    my_owned = jnp.array(owned, jnp.int32)[my_slice] * LANES
    my_bias = lax.dynamic_slice_in_dim(vec_expand, my_start, wide, 1)
    recur_stack, normed_ext, coefs, inlet_full, decay_full, my_bias, d_out, d_own, d_side, later, *held = tie(
        recur_stack, normed_ext, coefs, inlet_full, decay_full, my_bias, d_out, d_own, d_side, later, *held
    )
    recur_full, branch_full, output_full = recur_stack[0], recur_stack[1], recur_stack[2]
    if early_chunks < chunks:
        held += to_plane(later)
    ffn_full = [lax.all_gather(weights, "z", axis=0, tiled=True) for weights in held]

    d_plane = gather_rows(replicated_plane(d_own, d_side), "c")

    gates, states, branch_back, core_back = head_calls(heads, head_size, rows, rows + halo, seqs, taps)
    normed = normed_ext[halo:]
    recur = dot(normed_ext, recur_full) + vec_recur
    ext_row = lax.broadcasted_iota(jnp.int32, (rows + halo, 1), 0)
    recur = jnp.where(jnp.logical_and(ext_row < halo, place == 0), 0.0, recur)
    conv, sig_in, sig_dec, end, total = gates(first, recur, coefs, inlet_full, decay_full)
    carry = carry_in(end, total, False)
    branch = dot(normed, branch_full) + vec_branch
    state, mixed = states(first, conv, sig_in, sig_dec, branch, coefs, carry)
    mixed_own, mixed_other = halves(mixed, "y")
    out_other = dot(mixed_other, output_full, ((1,), (1,))).astype(BF16)
    got = swap(out_other, "y")
    out_own = dot(mixed_own, output_full, ((1,), (1,)))
    x_own, _ = halves(x_low, "y")
    x_own = x_own.astype(F32)
    middle = x_own + out_own + got.astype(F32) + vec_output
    second_f, scale_two = norm(middle, gain_two)
    second = second_f.astype(BF16)

    pair = gather_plane(second)
    plane = gather_rows(pair, "c")
    hidden, d_pre, ffn_grads, bias_grads = [], [], [], []
    owned_units = my_owned.reshape(1)
    mixed, normed, plane = tie(mixed, normed, plane)
    normed_dealt, mixed_group = deal_group(normed.T), gather_group(mixed)
    for k in range(chunks):
        bias = my_bias[:, k * step : (k + 1) * step].reshape(1, 2 * step)
        if k == chunks - 1:
            ffn_full[k], normed_dealt, mixed_group, *bias_grads = tie(ffn_full[k], normed_dealt, mixed_group, *bias_grads)
        hid, pre = feed(owned_units, plane, d_plane, ffn_full[k], bias, k * step)
        hidden.append(hid)
        d_pre.append(pre)
        if k + 1 < chunks:
            grads, sums = feed_grads(plane, d_plane, pre, hid)
            ffn_grads.append(grads)
            bias_grads.append(sums)

    def pair_sum(values, block):
        other = feed_back(values, ffn_full, 1, block, CORES)
        own = feed_back(values, ffn_full, 0, block, CORES)
        arrived, own = tie(swap(other, "c"), own)
        return (own.astype(F32) + arrived.astype(F32)).astype(BF16)

    d_pair = pair_sum(d_pre, 0)
    d_pair, *hidden = tie(d_pair, *hidden)
    last_grads, last_sums = feed_grads(plane, d_plane, d_pre[-1], hidden[-1])
    d_second_own, last_sums = scatter_plane(d_pair, last_sums)
    bias_grads = [sums[0].reshape(2, step) for sums in [*bias_grads, last_sums]]
    ffn_grads = [lax.psum_scatter(grad, "z", scatter_dimension=0, tiled=True) for grad in ffn_grads + [last_grads]]
    d_middle, grad_gain_two = norm_back(middle, scale_two, gain_two, d_second_own)
    d_middle = d_middle + d_own.astype(F32)
    d_low_own = d_middle.astype(BF16)
    d_low_own, *hidden = tie(d_low_own, *hidden)
    low_other, out_pair = tie(swap(d_low_own, "y"), pair_sum(hidden, 2))
    out_side = scatter_side(out_pair)
    is_low = side == 0
    d_low = jnp.concatenate([jnp.where(is_low, d_low_own, low_other), jnp.where(is_low, low_other, d_low_own)], axis=0)
    d_mixed = dot(d_low, output_full)
    pulled, d_branch, end_back, branch_sum = branch_back(d_mixed, branch, state, sig_dec, coefs)
    low_dealt = deal_group(d_low.T)
    end_back, low_dealt = tie(end_back, low_dealt)
    late = carry_in(end_back, total, True)

    def by_plane(grad):
        return grad.astype(BF16).reshape(PLANES, part, channels)

    def by_owner(grad):
        return grad.reshape(groups, -1, channels)

    d_normed_first = dot(d_branch, branch_full, ((1,), (1,)))
    late, d_normed_first, *out_side = tie(late, d_normed_first, *(out_side if mid == 2 else [out_side]))
    if mid == 2:
        out_side = ((out_side[0].astype(F32) + out_side[1].astype(F32)).astype(BF16),)
    out_side = out_side[0]
    d_conv, grad_inlet, grad_decay, core_sums = core_back(
        first, pulled, conv, sig_in, sig_dec, state, recur, coefs, carry, late, inlet_full, decay_full
    )
    branch_group = gather_group(d_branch)
    d_conv, branch_group = tie(d_conv, branch_group)
    behind = lax.ppermute(d_conv[:halo].astype(BF16), DP, [(j + 1, j) for j in range(groups - 1)])
    d_ext = jnp.concatenate([d_conv, behind.astype(F32)], axis=0)
    d_recur = vec_taps[0] * d_ext[:rows]
    for k in range(1, taps):
        d_recur = d_recur + vec_taps[k] * d_ext[k * seqs : k * seqs + rows]
    d_recur = d_recur.astype(BF16)
    recur_near = swap(d_recur, "x") if mid == 2 else lax.all_gather(d_recur, "x", axis=0, tiled=True)
    gates_b = fold_mid(fold_cores(jnp.concatenate([by_owner(grad_inlet), by_owner(grad_decay)], axis=1)))
    grad_output, grad_branch = dot(low_dealt, mixed_group), dot(normed_dealt, branch_group)
    packed = [by_plane(grad_output), by_plane(grad_branch)]
    recur_near, gates_b, *packed = tie(recur_near, gates_b, *packed)
    recur_near = jnp.concatenate([d_recur, recur_near], axis=0) if mid == 2 else recur_near
    packed += [by_plane(dot(normed_dealt, gather_rows(recur_near, "c"))), gates_b]
    packed = jnp.concatenate(packed, axis=1)
    packed, d_recur = tie(packed, d_recur)
    d_normed = d_normed_first + dot(d_recur, recur_full, ((1,), (1,)))
    dn_own, dn_other = halves(d_normed, "y")
    dn_got = swap(dn_other.astype(BF16), "y")
    packed, dn_got, out_side, *ffn_grads = tie(packed, dn_got, out_side, *ffn_grads)
    sums = fold_planes(packed)
    dn_own = dn_own + dn_got.astype(F32)
    scale_one = lax.rsqrt(jnp.mean(x_own * x_own, axis=-1, keepdims=True) + 1e-6)
    d_input, grad_gain_one = norm_back(x_own, scale_one, gain_one, dn_own)
    d_input = whole_rows((d_middle + d_input).astype(BF16), "y")

    shared = jnp.stack([grad_gain_one, jnp.sum(d_low_own.astype(F32), axis=0), grad_gain_two])
    shared = shared + swap(shared, "y")
    recur_sum = jnp.sum(d_recur.astype(F32), axis=0)
    by_unit = lax.dynamic_update_slice_in_dim(jnp.zeros((2, units), F32), jnp.concatenate(bias_grads, axis=1), my_start, 1)
    small = jnp.concatenate(
        [
            jnp.concatenate([branch_sum[:1], recur_sum[None], core_sums[4:], core_sums[3:4], core_sums[:3]], axis=0),
            shared.reshape(-1, channels),
            jnp.sum(d_out.astype(F32), axis=0).reshape(-1, channels),
            by_unit.reshape(-1, channels),
        ],
        axis=0,
    )
    small = sum_plane(small)
    returned = jnp.stack([grad.reshape(slices, part, 3 * step) for grad in ffn_grads], axis=1)
    small, out_side, returned = tie(small, out_side, returned)

    mask_own, _ = halves(mask, "y")
    result = jnp.where(mask_own, middle + scatter_rows(out_side, "x").astype(F32) + vec_shrink, 0.0).astype(BF16)
    result = whole_rows(result, "y")
    small = sum_planes(small)
    count = 6 + taps
    head_sums = lax.dynamic_slice_in_dim(small[:count].reshape(count, heads, head_size), place * head_part, head_part, 2)
    features = 4 * (width // channels)
    feature_sums = lax.dynamic_slice_in_dim(small[count : count + features].reshape(4, width), place * part, part, 1)
    unit_sums = small[count + features :].reshape(2, blocks, head_size)
    g_b_expand = lax.dynamic_slice_in_dim(unit_sums, place * head_part, head_part, 2)
    g_b_branch, g_b_recur, g_kernel = head_sums[0], head_sums[1], head_sums[2 : 2 + taps]
    g_conv_bias, g_b_inlet, g_b_decay, g_base = [head_sums[2 + taps + j] for j in range(4)]
    g_pre_gain, g_b_output, g_ffn_gain, g_b_shrink = [feature_sums[j] for j in range(4)]

    ffn_sum = to_slices(returned)
    grads_out = []
    for kind in range(3):
        pieces_out = []
        for j in range(slices):
            for k in range(chunks):
                keep = min(step, owned[j] * LANES - k * step)
                if keep > 0:
                    pieces_out.append(ffn_sum[j, k, :, kind * step : kind * step + keep])
        grads_out.append(jnp.concatenate(pieces_out, axis=1).astype(F32))
    grad_expand = jnp.stack(grads_out[:2])
    grad_shrink = grads_out[2]

    def gate_out(at):
        return sums[at : at + head_part].reshape(head_part, heads, head_size).transpose(1, 0, 2)

    def rows_out(v):
        return v.reshape(pieces, seqs, width).transpose(1, 0, 2)

    return (
        rows_out(result), rows_out(d_input), g_pre_gain, sums[part : 2 * part], g_b_branch, sums[2 * part : 3 * part], g_b_recur,
        g_kernel, g_conv_bias, gate_out(3 * part), g_b_inlet, gate_out(3 * part + head_part), g_b_decay, g_base,
        sums[:part], g_b_output, g_ffn_gain, grad_expand, g_b_expand, grad_shrink, g_b_shrink,
    )


def solution(mesh):
    groups, sides = mesh.shape["dp"], mesh.shape["tensor"]
    mid = groups // (PLANES * CORES)
    grid = Mesh(mesh.devices.reshape(PLANES, mid, CORES, sides), ("z", "x", "c", "y"))
    rows, vec = P(None, DP, None), P(DP)
    mat, head, tap, gate = P(DP, "y"), P("y", DP), P(None, "y", DP), P("y", DP, None)
    wide = P(None, DP, "y")
    return jax.shard_map(
        body,
        mesh=grid,
        in_specs=(
            rows, rows, P(), vec, mat, head, mat, head, tap, head, gate, head, gate, head, head, mat, vec, vec,
            wide, tap, mat, vec,
        ),
        out_specs=(
            rows, rows, vec, mat, head, mat, head, tap, head, gate, head, gate, head, head, mat, vec, vec,
            wide, tap, mat, vec,
        ),
        check_vma=False,
    )
```

time: 1170 us -> 909 us (0.78); the launches traced: 1150 us -> 901 us
  matrix products: 262 us -> 59.5 us
  Pallas kernels: 24.9 us -> 144 us
  local copies, waits for them, and re-layouts: 209 us -> 96.9 us
  waiting for transfers between devices: 386 us -> 325 us
  blocking collectives: 48 us -> 101 us
  starting transfers between devices: 107 us -> 82.9 us
  other arithmetic: 94.7 us -> 74.8 us
    dot_general x33 -> x10, matrix products: 262 us -> 59.5 us  [dot(): return lax.dot_general(a, b, (dims, ((), ())), preferred_element_type=F32)]
    pallas_call x0 -> x8, Pallas kernels: none -> 119 us  [the longest x4 44.4 us: feed_back(): pl.pallas_call(back_kernel, grid=(width // tile,), in_specs=[pl.BlockSpec...]
    all_gather x0 -> x3, blocking collectives: none -> 101 us  [the longest x1 54.1 us: body(): every = lax.all_gather(flat, DP, axis=0, tiled=False).astype(F32)]
    all_gather x5 -> x3, waiting for transfers between devices: 92.3 us -> 0.02 us  [the longest x1 0.02 us: body(): lax.all_gather(jnp.stack([w_recur, w_branch, w_output]), DP, axis=1, tile...]
    ppermute x0 -> x18, waiting for transfers between devices: none -> 83.9 us  [the longest x6 39.6 us: deal_group(): lax.ppermute(part, ('x', 'c'), [(j, j ^ flip) for j in range(4)])]
    unnamed x373 -> x241, local copies, waits for them, and re-layouts: 88.4 us -> 29 us
    ppermute x21 -> x36, waiting for transfers between devices: 222 us -> 165 us  [swap(): return lax.ppermute(v, axis, [(0, 1), (1, 0)])]
    all_to_all x1 -> x0, blocking collectives: 48 us -> none  [body(): lax.all_to_all(sent, ('x', 'c'), split_axis=1, concat_axis=1, tiled=True)]
  transfers between devices with their start and end apart: 41 -> 68, of which waited for: 22 -> 30; matrix products, arithmetic and copies ran while one was open for 44% -> 23% of each run, Pallas kernels for 2% -> 12%
where the time goes in v2:
time: 909 us; the launch traced here: 901 us
  waiting for transfers between devices  325 us (36%)
  Pallas kernels  144 us (16%)
  blocking collectives  101 us (11%)
  local copies, waits for them, and re-layouts  96.9 us (11%)
  starting transfers between devices  82.9 us (9%)
  other arithmetic  74.8 us (8%)
  matrix products  59.5 us (7%)
  between operations  18 us (2%)
    ppermute x36, waiting for transfers between devices, swap(): return lax.ppermute(v, axis, [(0, 1), (1, 0)])  165 us
    dot_general x10, matrix products, dot(): return lax.dot_general(a, b, (dims, ((), ())), preferred_element_type=F32)  59.5 us
    ppermute x6, waiting for transfers between devices, carry_in(): lax.ppermute(sent if far < planes - 1 else sent[:1], 'z', route).astype(F32)  55 us
    all_gather x1, blocking collectives, body(): every = lax.all_gather(flat, DP, axis=0, tiled=False).astype(F32)  54.1 us
    ppermute x36, starting transfers between devices, swap(): return lax.ppermute(v, axis, [(0, 1), (1, 0)])  49.1 us
    pallas_call x4, Pallas kernels, feed_back(): pl.pallas_call(back_kernel, grid=(width // tile,), in_specs=[pl.BlockSpec...  44.4 us
    ppermute x6, waiting for transfers between devices, deal_group(): lax.ppermute(part, ('x', 'c'), [(j, j ^ flip) for j in range(4)])  39.6 us
    pallas_call x2, Pallas kernels, feed(): pl.pallas_call(functools.partial(feed_kernel, first_unit=first_unit), gri...  37.9 us
  transfers between devices with their start and end apart: 68, of which 30 were waited for; matrix products, arithmetic and copies ran while one was open for 23% of the time, Pallas kernels for 12%

profile of v2, /device:TPU:9, one launch (start us, length us, event | category | flops | bytes accessed | tf_op | source)
XLA Modules:
  0.0 901.4 jit_solution(17892667982558130390)
XLA Ops:
  10.7 3.7 collective-permute-start
  24.9 54.1 %all-gather.1 = bf16[16,1,1920]{2,1,0:T(2,128)(2,1)S(1)} all-gather(bf16[1,1,1920]{2,1,0:T(2,128)(2,1)S(1)} %reshape.682), channel_id=2, replica_groups=mesh['z'=4,'x'=2,'c'=2,'y'=2] {'z','x','c'}, dimensions={0}, use_global_device_ids=true | all-gather | bytes 65280 | tf_op jit(solution)/shard_map/all_gather | solution.py:536
  87.8 22.0 %all_gather.25.wd_ref = bf16[256,1280]{1,0:T(8,128)(2,1)S(1)} all-gather(bf16[16,1280]{1,0:T(8,128)(2,1)S(1)} %bitcast.390), channel_id=1, replica_groups=mesh['z'=4,'x'=2,'c'=2,'y'=2] {'z','x','c'}, dimensions={0}, use_global_device_ids=true | all-gather | bytes 696320 | tf_op jit(solution)/shard_map/all_gather | solution.py:532
  109.8 24.5 %all_gather.24.wi_ref = bf16[256,1280]{1,0:T(8,128)(2,1)S(1)} all-gather(bf16[16,1280]{1,0:T(8,128)(2,1)S(1)} %bitcast.389), channel_id=1, replica_groups=mesh['z'=4,'x'=2,'c'=2,'y'=2] {'z','x','c'}, dimensions={0}, use_global_device_ids=true | all-gather | bytes 696320 | tf_op jit(solution)/shard_map/all_gather | solution.py:531
  151.0 3.1 fusion.23
  160.1 8.5 fusion.38.r_ref
  168.6 5.7 shard_map.391
  174.4 8.2 fusion.44.b_ref
  183.3 10.0 %collective-permute-done.5 = bf16[2,32,1280]{2,1,0:T(8,128)(2,1)S(1)} collective-permute-done((bf16[2,32,1280]{2,1,0:T(8,128)(2,1)S(1)}, bf16[2,32,1280]{2,1,0:T(8,128)(2,1)S(1)}, u32[]{:S(2)}, u32[]{:S(2)}) %collective-permute-start.5) | collective-permute-done | bytes 163872 | tf_op jit(solution)/shard_map/ppermute | solution.py:309
  194.0 3.4 collective-permute-start.7
  199.4 13.8 %collective-permute-done.7 = bf16[2,32,1280]{2,1,0:T(8,128)(2,1)S(1)} collective-permute-done((bf16[2,32,1280]{2,1,0:T(8,128)(2,1)S(1)}, bf16[2,32,1280]{2,1,0:T(8,128)(2,1)S(1)}, u32[]{:S(2)}, u32[]{:S(2)}) %collective-permute-start.7) | collective-permute-done | bytes 163872 | tf_op jit(solution)/shard_map/ppermute | solution.py:487
  214.7 10.8 %collective-permute-done.6 = bf16[2,32,1280]{2,1,0:T(8,128)(2,1)S(1)} collective-permute-done((bf16[2,32,1280]{2,1,0:T(8,128)(2,1)S(1)}, bf16[2,32,1280]{2,1,0:T(8,128)(2,1)S(1)}, u32[]{:S(2)}, u32[]{:S(2)}) %collective-permute-start.6) | collective-permute-done | bytes 163872 | tf_op jit(solution)/shard_map/ppermute | solution.py:487
  226.1 5.5 shard_map.392
  231.7 7.2 fusion.32
  243.8 18.8 %collective-permute-done.9 = bf16[192,2560]{1,0:T(8,128)(2,1)} collective-permute-done((bf16[192,2560]{1,0:T(8,128)(2,1)}, bf16[192,2560]{1,0:T(8,128)(2,1)}, u32[]{:S(2)}, u32[]{:S(2)}) %collective-permute-start.9) | collective-permute-done | bytes 983072 | tf_op jit(solution)/shard_map/ppermute | solution.py:309
  262.6 5.8 multiply_reduce_fusion.2
  272.7 8.5 collective-permute-done.10
  283.0 19.5 %collective-permute-done.11 = bf16[192,2560]{1,0:T(8,128)(2,1)S(1)} collective-permute-done((bf16[192,2560]{1,0:T(8,128)(2,1)S(1)}, bf16[192,2560]{1,0:T(8,128)(2,1)S(1)}, u32[]{:S(2)}, u32[]{:S(2)}) %collective-permute-start.11) | collective-permute-done | bytes 983072 | tf_op jit(solution)/shard_map/ppermute | solution.py:309
  304.0 8.5 collective-permute-done.12
  313.8 18.2 %collective-permute-done.13 = bf16[192,2560]{1,0:T(8,128)(2,1)S(1)} collective-permute-done((bf16[192,2560]{1,0:T(8,128)(2,1)S(1)}, bf16[192,2560]{1,0:T(8,128)(2,1)S(1)}, u32[]{:S(2)}, u32[]{:S(2)}) %collective-permute-start.13) | collective-permute-done | bytes 983072 | tf_op jit(solution)/shard_map/ppermute | solution.py:309
  332.2 4.8 collective-permute-start.14
  351.3 19.6 %collective-permute-done.24 = bf16[384,1280]{1,0:T(8,128)(2,1)S(1)} collective-permute-done((bf16[384,1280]{1,0:T(8,128)(2,1)S(1)}, bf16[384,1280]{1,0:T(8,128)(2,1)S(1)}, u32[]{:S(2)}, u32[]{:S(2)}) %collective-permute-start.24) | collective-permute-done | bytes 983072 | tf_op jit(solution)/shard_map/ppermute | solution.py:309
  375.6 4.2 copy.132
  384.3 4.3 constant_dynamic-update-slice_fusion.13.d_ref
  388.6 6.9 collective-permute-done.23
  395.5 9.2 %collective-permute-done.21 = bf16[4,160,384]{2,1,0:T(8,128)(2,1)S(1)} collective-permute-done((bf16[4,160,384]{2,1,0:T(8,128)(2,1)S(1)}, bf16[4,160,384]{2,1,0:T(8,128)(2,1)S(1)}, u32[]{:S(2)}, u32[]{:S(2)}) %collective-permute-start.21) | collective-permute-done | bytes 491552 | tf_op jit(solution)/shard_map/ppermute | solution.py:389
  406.2 3.3 pad_maximum_fusion.1
  409.5 18.9 %shard_map.393 = (bf16[1536,512]{1,0:T(8,128)(2,1)}, bf16[1536,1024]{1,0:T(8,128)(2,1)}) custom-call(s32[1]{0:T(128)S(6)} %mul.366.at_ref, bf16[1536,2560]{1,0:T(8,128)(2,1)} %copy-done.8, bf16[1536,2560]{1,0:T(8,128)(2,1)} %constant_dynamic-update-slice_fusion.13.d_ref, bf16[2560,1536]{1,0:T(8,128)(2,1)} %all-gather.8.cloned.1.call-done.w_ref.refs_2_, ...), custom_call_target="tpu_custom_call" | custom-call | flops 1 | bytes 1 | tf_op jit(solution)/shard_map/pallas_call | solution.py:228
  428.5 18.4 %shard_map.394 = (bf16[2560,1536]{1,0:T(8,128)(2,1)}, f32[8,1024]{1,0:T(8,128)}) custom-call(bf16[1536,2560]{1,0:T(8,128)(2,1)} %copy-done.8, bf16[1536,2560]{1,0:T(8,128)(2,1)} %constant_dynamic-update-slice_fusion.13.d_ref, bf16[1536,1024]{1,0:T(8,128)(2,1)} %get-tuple-element.115.g_ref.refs_0_, bf16[1536,512]{1,0:T(8,128)(2,1)} %get-tuple-element.133.h_ref.refs_0_), custom_call_target="tpu_custom_call" | custom-call | flops 1 | bytes 1 | tf_op jit(solution)/shard_map/pallas_call | solution.py:267
  446.8 18.9 %shard_map.395 = (bf16[1536,512]{1,0:T(8,128)(2,1)}, bf16[1536,1024]{1,0:T(8,128)(2,1)}) custom-call(s32[1]{0:T(128)S(6)} %mul.366.at_ref, bf16[1536,2560]{1,0:T(8,128)(2,1)} %copy-done.8, bf16[1536,2560]{1,0:T(8,128)(2,1)} %constant_dynamic-update-slice_fusion.13.d_ref, bf16[2560,1536]{1,0:T(8,128)(2,1)} %all-gather.10.cloned.1.call-done.w_ref.refs_3_, ...), custom_call_target="tpu_custom_call" | custom-call | flops 1 | bytes 1 | tf_op jit(solution)/shard_map/pallas_call | solution.py:228
  465.8 12.6 %shard_map.396 = bf16[768,2560]{1,0:T(8,128)(2,1)} custom-call(bf16[1536,1024]{1,0:T(8,128)(2,1)} %get-tuple-element.115.g_ref.refs_0_, bf16[1536,1024]{1,0:T(8,128)(2,1)} %get-tuple-element.122.refs_1_.g_ref, bf16[2560,1536]{1,0:T(8,128)(2,1)} %all-gather.8.cloned.1.call-done.w_ref.refs_2_, bf16[2560,1536]{1,0:T(8,128)(2,1)} %all-gather.10.cloned.1.call-done.w_ref.refs_3_), custom_call_target="tpu_custom_call" | custom-call | flops 1 | bytes 1 | tf_op jit(solution)/shard_map/pallas_call | solution.py:296
  479.5 13.7 %shard_map.397 = bf16[768,2560]{1,0:T(8,128)(2,1)} custom-call(bf16[1536,1024]{1,0:T(8,128)(2,1)} %get-tuple-element.115.g_ref.refs_0_, bf16[1536,1024]{1,0:T(8,128)(2,1)} %get-tuple-element.122.refs_1_.g_ref, bf16[2560,1536]{1,0:T(8,128)(2,1)} %all-gather.8.cloned.1.call-done.w_ref.refs_2_, bf16[2560,1536]{1,0:T(8,128)(2,1)} %all-gather.10.cloned.1.call-done.w_ref.refs_3_), custom_call_target="tpu_custom_call" | custom-call | flops 1 | bytes 1 | tf_op jit(solution)/shard_map/pallas_call | solution.py:296
  493.2 4.3 add_convert_fusion.1
  501.8 18.4 %shard_map.398 = (bf16[2560,1536]{1,0:T(8,128)(2,1)}, f32[8,1024]{1,0:T(8,128)}) custom-call(bf16[1536,2560]{1,0:T(8,128)(2,1)} %copy-done.8, bf16[1536,2560]{1,0:T(8,128)(2,1)} %constant_dynamic-update-slice_fusion.13.d_ref, bf16[1536,1024]{1,0:T(8,128)(2,1)} %get-tuple-element.122.refs_1_.g_ref, bf16[1536,512]{1,0:T(8,128)(2,1)} %get-tuple-element.134.h_ref.refs_1_), custom_call_target="tpu_custom_call" | custom-call | flops 1 | bytes 1 | tf_op jit(solution)/shard_map/pallas_call | solution.py:267
  526.1 9.9 %collective-permute-done.29 = bf16[96,2560]{1,0:T(8,128)(2,1)S(1)} collective-permute-done((bf16[96,2560]{1,0:T(8,128)(2,1)S(1)}, bf16[96,2560]{1,0:T(8,128)(2,1)S(1)}, u32[]{:S(2)}, u32[]{:S(2)}) %collective-permute-start.29) | collective-permute-done | bytes 491552 | tf_op jit(solution)/shard_map/ppermute | solution.py:309
  538.3 9.2 %shard_map.399 = bf16[768,2560]{1,0:T(8,128)(2,1)} custom-call(bf16[1536,512]{1,0:T(8,128)(2,1)} %get-tuple-element.133.h_ref.refs_0_, bf16[1536,512]{1,0:T(8,128)(2,1)} %get-tuple-element.134.h_ref.refs_1_, bf16[2560,1536]{1,0:T(8,128)(2,1)} %all-gather.8.cloned.1.call-done.w_ref.refs_2_, bf16[2560,1536]{1,0:T(8,128)(2,1)} %all-gather.10.cloned.1.call-done.w_ref.refs_3_), custom_call_target="tpu_custom_call" | custom-call | flops 1 | bytes 1 | tf_op jit(solution)/shard_map/pallas_call | solution.py:296
  551.1 8.9 shard_map.400
  560.0 6.4 add_convert_fusion
  566.4 7.1 collective-permute-done.31
  575.0 5.5 fusion.dm_ref
  580.6 5.2 shard_map.401
  588.2 7.5 fusion.6
  595.7 4.0 copy.136
  607.3 15.3 %collective-permute-done.35 = bf16[4,160,384]{2,1,0:T(8,128)(2,1)S(1)} collective-permute-done((bf16[4,160,384]{2,1,0:T(8,128)(2,1)S(1)}, bf16[4,160,384]{2,1,0:T(8,128)(2,1)S(1)}, u32[]{:S(2)}, u32[]{:S(2)}) %collective-permute-start.35) | collective-permute-done | bytes 491552 | tf_op jit(solution)/shard_map/ppermute | solution.py:389
  622.5 8.3 collective-permute-done.33
  633.0 3.8 convolution_convert_fusion.1
  643.8 3.2 collective-permute-start.38
  647.0 10.2 %collective-permute-done.39 = bf16[2,32,1280]{2,1,0:T(8,128)(2,1)S(1)} collective-permute-done((bf16[2,32,1280]{2,1,0:T(8,128)(2,1)S(1)}, bf16[2,32,1280]{2,1,0:T(8,128)(2,1)S(1)}, u32[]{:S(2)}, u32[]{:S(2)}) %collective-permute-start.39) | collective-permute-done | bytes 163872 | tf_op jit(solution)/shard_map/ppermute | solution.py:487
  657.2 20.1 %collective-permute-done.38 = bf16[2,32,1280]{2,1,0:T(8,128)(2,1)S(1)} collective-permute-done((bf16[2,32,1280]{2,1,0:T(8,128)(2,1)S(1)}, bf16[2,32,1280]{2,1,0:T(8,128)(2,1)S(1)}, u32[]{:S(2)}, u32[]{:S(2)}) %collective-permute-start.38) | collective-permute-done | bytes 163872 | tf_op jit(solution)/shard_map/ppermute | solution.py:487
  677.4 8.6 shard_map.402
  693.2 6.9 collective-permute-done.44
  700.7 9.8 %collective-permute-start.45 = (bf16[384,1280]{1,0:T(8,128)(2,1)S(1)}, bf16[384,1280]{1,0:T(8,128)(2,1)S(1)}, u32[]{:S(2)}, u32[]{:S(2)}) collective-permute-start(bf16[384,1280]{1,0:T(8,128)(2,1)S(1)} %fusion.51), channel_id=1, source_target_pairs={{0,4},{4,0},{1,5},{5,1},{2,6},{6,2},{3,7},{7,3},{8,12},{12,8},{9,1... | collective-permute-start | bytes 2949128 | tf_op jit(solution)/shard_map/ppermute | solution.py:309
  713.3 14.1 %collective-permute-done.45 = bf16[384,1280]{1,0:T(8,128)(2,1)S(1)} collective-permute-done((bf16[384,1280]{1,0:T(8,128)(2,1)S(1)}, bf16[384,1280]{1,0:T(8,128)(2,1)S(1)}, u32[]{:S(2)}, u32[]{:S(2)}) %collective-permute-start.45) | collective-permute-done | bytes 983072 | tf_op jit(solution)/shard_map/ppermute | solution.py:309
  734.9 5.2 fusion.41
  740.1 7.6 pad_maximum_fusion
  747.7 5.1 fusion.10
  761.3 19.9 %collective-permute-done.49 = bf16[192,2560]{1,0:T(8,128)(2,1)} collective-permute-done((bf16[192,2560]{1,0:T(8,128)(2,1)}, bf16[192,2560]{1,0:T(8,128)(2,1)}, u32[]{:S(2)}, u32[]{:S(2)}) %collective-permute-start.49) | collective-permute-done | bytes 983072 | tf_op jit(solution)/shard_map/ppermute | solution.py:309
  792.2 5.2 collective-permute-done.52
  807.0 5.3 collective-permute-done.58
  812.3 2.9 collective-permute-start.59
  815.2 4.7 collective-permute-done.56
  822.9 4.9 fusion.61
  830.6 34.2 %collective-permute-done.60 = bf16[1,2,160,1536]{3,2,1,0:T(8,128)(2,1)} collective-permute-done((bf16[1,2,160,1536]{3,2,1,0:T(8,128)(2,1)}, bf16[1,2,160,1536]{3,2,1,0:T(8,128)(2,1)}, u32[]{:S(2)}, u32[]{:S(2)}) %collective-permute-start.60) | collective-permute-done | bytes 983072 | tf_op jit(solution)/shard_map/ppermute | solution.py:434
  875.4 13.5 %reduce-scatter.8.cloned.1.call-done = bf16[1,512,1280]{2,1,0:T(8,128)(2,1)} async-done(((bf16[4,512,1280]{2,1,0:T(8,128)(2,1)}), bf16[1,512,1280]{2,1,0:T(8,128)(2,1)}) %reduce-scatter.8.cloned.1.call-update) | async-done | bytes 1310736 | tf_op jit(solution)/shard_map/reduce_scatter | solution.py:413
  (560 shorter events, 193.4 us)
Async XLA Ops:
  7.2 146.9 %all-gather.6.cloned.1.call-start = ((), (), s32[]{:S(2)}) async-start(), calls=%async_computation.3 | async-start | bytes 20889600 | tf_op jit(solution)/shard_map/all_gather | solution.py:530
  9.8 399.7 %all-gather.8.cloned.1.call-start = ((), (), s32[]{:S(2)}) async-start(), calls=%async_computation.4 | async-start | bytes 9830400 | tf_op jit(solution)/shard_map/all_gather | solution.py:597
  10.7 133.1 %collective-permute-start = (bf16[96,2560]{1,0:T(8,128)(2,1)}, bf16[96,2560]{1,0:T(8,128)(2,1)}, u32[]{:S(2)}, u32[]{:S(2)}) collective-permute-start(bf16[96,2560]{1,0:T(8,128)(2,1)} %bitcast.6), channel_id=1, source_target_pairs={{0,2},{2,4},{4,6},{6,8},{8,10},{10,12},{12,14},{14,16},{16,18},{18... | collective-permute-start | bytes 1474568 | tf_op jit(solution)/shard_map/ppermute | solution.py:528
  20.5 128.7 %collective-permute-start.3 = (bf16[1,1,160,1536]{3,2,0,1:T(8,128)(2,1)}, bf16[1,1,160,1536]{3,2,0,1:T(8,128)(2,1)}, u32[]{:S(2)}, u32[]{:S(2)}) collective-permute-start(bf16[1,1,160,1536]{3,2,0,1:T(8,128)(2,1)} %get-tuple-element.346), channel_id=1, source_target_pairs={{0,6},{2,4},{4,2},{6,0},{1,7},{3,5},{5,3},{7,1},{8,14},{10,12},{12... | collective-permute-start | bytes 1474568 | tf_op jit(solution)/shard_map/ppermute | solution.py:434
  20.5 126.8 %collective-permute-start.2 = (bf16[1,1,160,1536]{3,2,0,1:T(8,128)(2,1)}, bf16[1,1,160,1536]{3,2,0,1:T(8,128)(2,1)}, u32[]{:S(2)}, u32[]{:S(2)}) collective-permute-start(bf16[1,1,160,1536]{3,2,0,1:T(8,128)(2,1)} %get-tuple-element.347), channel_id=1, source_target_pairs={{0,4},{2,6},{4,0},{6,2},{1,5},{3,7},{5,1},{7,3},{8,12},{10,14},{12... | collective-permute-start | bytes 1474568 | tf_op jit(solution)/shard_map/ppermute | solution.py:434
  21.8 123.6 %collective-permute-start.1 = (bf16[1,1,160,1536]{3,2,0,1:T(8,128)(2,1)}, bf16[1,1,160,1536]{3,2,0,1:T(8,128)(2,1)}, u32[]{:S(2)}, u32[]{:S(2)}) collective-permute-start(bf16[1,1,160,1536]{3,2,0,1:T(8,128)(2,1)} %get-tuple-element.348), channel_id=1, source_target_pairs={{0,2},{2,0},{4,6},{6,4},{1,3},{3,1},{5,7},{7,5},{8,10},{10,8},{12,... | collective-permute-start | bytes 1474568 | tf_op jit(solution)/shard_map/ppermute | solution.py:434
  154.2 292.7 %all-gather.10.cloned.1.call-start = ((), (), s32[]{:S(2)}) async-start(), calls=%async_computation.5 | async-start | bytes 9830400 | tf_op jit(solution)/shard_map/all_gather | solution.py:597
  155.8 87.7 %collective-permute-start.15 = (bf16[192,2560]{1,0:T(8,128)(2,1)S(1)}, bf16[192,2560]{1,0:T(8,128)(2,1)}, u32[]{:S(2)}, u32[]{:S(2)}) collective-permute-start(bf16[192,2560]{1,0:T(8,128)(2,1)S(1)} %copy-done.14), channel_id=1, source_target_pairs={{0,4},{4,0},{1,5},{5,1},{2,6},{6,2},{3,7},{7,3},{8,12},{12,8},{9,1... | collective-permute-start | bytes 2949128 | tf_op jit(solution)/shard_map/ppermute | solution.py:309
  158.9 83.6 %collective-permute-start.20 = (bf16[1,1,160,1536]{3,2,0,1:T(8,128)(2,1)S(1)}, bf16[1,1,160,1536]{3,2,0,1:T(8,128)(2,1)S(1)}, u32[]{:S(2)}, u32[]{:S(2)}) collective-permute-start(bf16[1,1,160,1536]{3,2,0,1:T(8,128)(2,1)S(1)} %get-tuple-element.342), channel_id=1, source_target_pairs={{0,6},{2,4},{4,2},{6,0},{1,7},{3,5},{5,3},{7,1},{8,14},{10,12},{12... | collective-permute-start | bytes 1474568 | tf_op jit(solution)/shard_map/ppermute | solution.py:434
  174.3 8.3 collective-permute-start.4
  182.8 10.4 %collective-permute-start.5 = (bf16[2,32,1280]{2,1,0:T(8,128)(2,1)S(1)}, bf16[2,32,1280]{2,1,0:T(8,128)(2,1)S(1)}, u32[]{:S(2)}, u32[]{:S(2)}) collective-permute-start(bf16[2,32,1280]{2,1,0:T(8,128)(2,1)S(1)} %pad_maximum_fusion.24), channel_id=1, source_target_pairs={{0,4},{4,0},{1,5},{5,1},{2,6},{6,2},{3,7},{7,3},{8,12},{12,8},{9,1... | collective-permute-start | bytes 491528 | tf_op jit(solution)/shard_map/ppermute | solution.py:309
  193.3 32.7 %collective-permute-start.8 = (bf16[1,32,1280]{2,1,0:T(8,128)(2,1)S(1)}, bf16[1,32,1280]{2,1,0:T(8,128)(2,1)S(1)}, u32[]{:S(2)}, u32[]{:S(2)}) collective-permute-start(bf16[1,32,1280]{2,1,0:T(8,128)(2,1)S(1)} %get-tuple-element.269), channel_id=1, source_target_pairs={{0,24},{1,25},{2,26},{3,27},{4,28},{5,29},{6,30},{7,31}} | collective-permute-start | bytes 245768 | tf_op jit(solution)/shard_map/ppermute | solution.py:487
  194.0 19.2 %collective-permute-start.7 = (bf16[2,32,1280]{2,1,0:T(8,128)(2,1)S(1)}, bf16[2,32,1280]{2,1,0:T(8,128)(2,1)S(1)}, u32[]{:S(2)}, u32[]{:S(2)}) collective-permute-start(bf16[2,32,1280]{2,1,0:T(8,128)(2,1)S(1)} %pad_maximum_fusion.25), channel_id=1, source_target_pairs={{0,16},{8,24},{1,17},{9,25},{2,18},{10,26},{3,19},{11,27},{4,20},{... | collective-permute-start | bytes 491528 | tf_op jit(solution)/shard_map/ppermute | solution.py:487
  197.4 28.1 %collective-permute-start.6 = (bf16[2,32,1280]{2,1,0:T(8,128)(2,1)S(1)}, bf16[2,32,1280]{2,1,0:T(8,128)(2,1)S(1)}, u32[]{:S(2)}, u32[]{:S(2)}) collective-permute-start(bf16[2,32,1280]{2,1,0:T(8,128)(2,1)S(1)} %pad_maximum_fusion.25), channel_id=1, source_target_pairs={{0,8},{8,16},{16,24},{1,9},{9,17},{17,25},{2,10},{10,18},{18,26},{... | collective-permute-start | bytes 491528 | tf_op jit(solution)/shard_map/ppermute | solution.py:487
  213.2 28.6 %collective-permute-start.19 = (bf16[1,1,160,1536]{3,2,0,1:T(8,128)(2,1)S(1)}, bf16[1,1,160,1536]{3,2,0,1:T(8,128)(2,1)S(1)}, u32[]{:S(2)}, u32[]{:S(2)}) collective-permute-start(bf16[1,1,160,1536]{3,2,0,1:T(8,128)(2,1)S(1)} %get-tuple-element.343), channel_id=1, source_target_pairs={{0,4},{2,6},{4,0},{6,2},{1,5},{3,7},{5,1},{7,3},{8,12},{10,14},{12... | collective-permute-start | bytes 1474568 | tf_op jit(solution)/shard_map/ppermute | solution.py:434
  225.5 15.5 %collective-permute-start.18 = (bf16[1,1,160,1536]{3,2,0,1:T(8,128)(2,1)S(1)}, bf16[1,1,160,1536]{3,2,0,1:T(8,128)(2,1)S(1)}, u32[]{:S(2)}, u32[]{:S(2)}) collective-permute-start(bf16[1,1,160,1536]{3,2,0,1:T(8,128)(2,1)S(1)} %get-tuple-element.344), channel_id=1, source_target_pairs={{0,2},{2,0},{4,6},{6,4},{1,3},{3,1},{5,7},{7,5},{8,10},{10,8},{12,... | collective-permute-start | bytes 1474568 | tf_op jit(solution)/shard_map/ppermute | solution.py:434
  238.9 23.7 %collective-permute-start.9 = (bf16[192,2560]{1,0:T(8,128)(2,1)}, bf16[192,2560]{1,0:T(8,128)(2,1)}, u32[]{:S(2)}, u32[]{:S(2)}) collective-permute-start(bf16[192,2560]{1,0:T(8,128)(2,1)} %fusion.32), channel_id=1, source_target_pairs={{0,1},{1,0},{2,3},{3,2},{4,5},{5,4},{6,7},{7,6},{8,9},{9,8},{10,11... | collective-permute-start | bytes 2949128 | tf_op jit(solution)/shard_map/ppermute | solution.py:309
  243.5 517.8 %reduce-scatter.4.cloned.1.call-start = ((), (), s32[]{:S(2)}) async-start(), calls=%async_computation.6 | async-start | bytes 9830400 | tf_op jit(solution)/shard_map/reduce_scatter | solution.py:649
  243.5 93.5 %collective-permute-start.16 = (bf16[192,2560]{1,0:T(8,128)(2,1)}, bf16[192,2560]{1,0:T(8,128)(2,1)S(1)}, u32[]{:S(2)}, u32[]{:S(2)}) collective-permute-start(bf16[192,2560]{1,0:T(8,128)(2,1)} %collective-permute-done.15), channel_id=1, source_target_pairs={{0,1},{1,0},{2,3},{3,2},{4,5},{5,4},{6,7},{7,6},{8,9},{9,8},{10,11... | collective-permute-start | bytes 2949128 | tf_op jit(solution)/shard_map/ppermute | solution.py:309
  269.7 11.5 %collective-permute-start.10 = (bf16[96,2560]{1,0:T(8,128)(2,1)S(1)}, bf16[96,2560]{1,0:T(8,128)(2,1)S(1)}, u32[]{:S(2)}, u32[]{:S(2)}) collective-permute-start(bf16[96,2560]{1,0:T(8,128)(2,1)S(1)} %get-tuple-element.375), channel_id=1, source_target_pairs={{0,4},{4,0},{1,5},{5,1},{2,6},{6,2},{3,7},{7,3},{8,12},{12,8},{9,1... | collective-permute-start | bytes 1474568 | tf_op jit(solution)/shard_map/ppermute | solution.py:309
  281.3 21.2 %collective-permute-start.11 = (bf16[192,2560]{1,0:T(8,128)(2,1)S(1)}, bf16[192,2560]{1,0:T(8,128)(2,1)S(1)}, u32[]{:S(2)}, u32[]{:S(2)}) collective-permute-start(bf16[192,2560]{1,0:T(8,128)(2,1)S(1)} %pad_maximum_fusion.20), channel_id=1, source_target_pairs={{0,1},{1,0},{2,3},{3,2},{4,5},{5,4},{6,7},{7,6},{8,9},{9,8},{10,11... | collective-permute-start | bytes 2949128 | tf_op jit(solution)/shard_map/ppermute | solution.py:309
  302.7 9.8 %collective-permute-start.12 = (bf16[96,2560]{1,0:T(8,128)(2,1)S(1)}, bf16[96,2560]{1,0:T(8,128)(2,1)S(1)}, u32[]{:S(2)}, u32[]{:S(2)}) collective-permute-start(bf16[96,2560]{1,0:T(8,128)(2,1)S(1)} %get-tuple-element.373), channel_id=1, source_target_pairs={{0,1},{1,0},{2,3},{3,2},{4,5},{5,4},{6,7},{7,6},{8,9},{9,8},{10,11... | collective-permute-start | bytes 1474568 | tf_op jit(solution)/shard_map/ppermute | solution.py:309
  312.5 19.5 %collective-permute-start.13 = (bf16[192,2560]{1,0:T(8,128)(2,1)S(1)}, bf16[192,2560]{1,0:T(8,128)(2,1)S(1)}, u32[]{:S(2)}, u32[]{:S(2)}) collective-permute-start(bf16[192,2560]{1,0:T(8,128)(2,1)S(1)} %pad_maximum_fusion.21), channel_id=1, source_target_pairs={{0,4},{4,0},{1,5},{5,1},{2,6},{6,2},{3,7},{7,3},{8,12},{12,8},{9,1... | collective-permute-start | bytes 2949128 | tf_op jit(solution)/shard_map/ppermute | solution.py:309
  332.2 15.5 %collective-permute-start.14 = (bf16[768,2560]{1,0:T(8,128)(2,1)S(1)}, bf16[768,2560]{1,0:T(8,128)(2,1)S(1)}, u32[]{:S(2)}, u32[]{:S(2)}) collective-permute-start(bf16[768,2560]{1,0:T(8,128)(2,1)S(1)} %get-tuple-element.369), channel_id=1, source_target_pairs={{0,2},{2,0},{1,3},{3,1},{4,6},{6,4},{5,7},{7,5},{8,10},{10,8},{9,1... | collective-permute-start | bytes 11796488 | tf_op jit(solution)/shard_map/ppermute | solution.py:309
  343.8 40.6 %collective-permute-start.17 = (bf16[768,2560]{1,0:T(8,128)(2,1)}, bf16[768,2560]{1,0:T(8,128)(2,1)}, u32[]{:S(2)}, u32[]{:S(2)}) collective-permute-start(bf16[768,2560]{1,0:T(8,128)(2,1)} %get-tuple-element.363), channel_id=1, source_target_pairs={{0,2},{2,0},{1,3},{3,1},{4,6},{6,4},{5,7},{7,5},{8,10},{10,8},{9,1... | collective-permute-start | bytes 11796488 | tf_op jit(solution)/shard_map/ppermute | solution.py:309
  348.0 23.0 %collective-permute-start.24 = (bf16[384,1280]{1,0:T(8,128)(2,1)S(1)}, bf16[384,1280]{1,0:T(8,128)(2,1)S(1)}, u32[]{:S(2)}, u32[]{:S(2)}) collective-permute-start(bf16[384,1280]{1,0:T(8,128)(2,1)S(1)} %copy-done.4), channel_id=1, source_target_pairs={{0,4},{4,0},{1,5},{5,1},{2,6},{6,2},{3,7},{7,3},{8,12},{12,8},{9,1... | collective-permute-start | bytes 2949128 | tf_op jit(solution)/shard_map/ppermute | solution.py:309
  372.5 33.7 %collective-permute-start.25 = (bf16[768,1280]{1,0:T(8,128)(2,1)}, bf16[768,1280]{1,0:T(8,128)(2,1)}, u32[]{:S(2)}, u32[]{:S(2)}) collective-permute-start(bf16[768,1280]{1,0:T(8,128)(2,1)} %pad_maximum_fusion.8), channel_id=1, source_target_pairs={{0,2},{2,0},{1,3},{3,1},{4,6},{6,4},{5,7},{7,5},{8,10},{10,8},{9,1... | collective-permute-start | bytes 5898248 | tf_op jit(solution)/shard_map/ppermute | solution.py:309
  381.6 13.9 %collective-permute-start.23 = (bf16[4,160,384]{2,1,0:T(8,128)(2,1)S(1)}, bf16[4,160,384]{2,1,0:T(8,128)(2,1)S(1)}, u32[]{:S(2)}, u32[]{:S(2)}) collective-permute-start(bf16[4,160,384]{2,1,0:T(8,128)(2,1)S(1)} %get-tuple-element.339), channel_id=1, source_target_pairs={{0,6},{2,4},{4,2},{6,0},{1,7},{3,5},{5,3},{7,1},{8,14},{10,12},{12... | collective-permute-start | bytes 1474568 | tf_op jit(solution)/shard_map/ppermute | solution.py:389
  382.6 12.9 %collective-permute-start.22 = (bf16[4,160,384]{2,1,0:T(8,128)(2,1)S(1)}, bf16[4,160,384]{2,1,0:T(8,128)(2,1)S(1)}, u32[]{:S(2)}, u32[]{:S(2)}) collective-permute-start(bf16[4,160,384]{2,1,0:T(8,128)(2,1)S(1)} %get-tuple-element.340), channel_id=1, source_target_pairs={{0,2},{2,0},{4,6},{6,4},{1,3},{3,1},{5,7},{7,5},{8,10},{10,8},{12,... | collective-permute-start | bytes 1474568 | tf_op jit(solution)/shard_map/ppermute | solution.py:389
  383.1 21.6 %collective-permute-start.21 = (bf16[4,160,384]{2,1,0:T(8,128)(2,1)S(1)}, bf16[4,160,384]{2,1,0:T(8,128)(2,1)S(1)}, u32[]{:S(2)}, u32[]{:S(2)}) collective-permute-start(bf16[4,160,384]{2,1,0:T(8,128)(2,1)S(1)} %get-tuple-element.341), channel_id=1, source_target_pairs={{0,4},{2,6},{4,0},{6,2},{1,5},{3,7},{5,1},{7,3},{8,12},{10,14},{12... | collective-permute-start | bytes 1474568 | tf_op jit(solution)/shard_map/ppermute | solution.py:389
  478.4 14.8 %collective-permute-start.26 = (bf16[768,2560]{1,0:T(8,128)(2,1)}, bf16[768,2560]{1,0:T(8,128)(2,1)}, u32[]{:S(2)}, u32[]{:S(2)}) collective-permute-start(bf16[768,2560]{1,0:T(8,128)(2,1)} %shard_map.396), channel_id=1, source_target_pairs={{0,2},{2,0},{1,3},{3,1},{4,6},{6,4},{5,7},{7,5},{8,10},{10,8},{9,1... | collective-permute-start | bytes 11796488 | tf_op jit(solution)/shard_map/ppermute | solution.py:309
  479.4 301.7 %reduce-scatter.6.cloned.1.call-start = ((), (), s32[]{:S(2)}) async-start(), calls=%async_computation.7 | async-start | bytes 9830400 | tf_op jit(solution)/shard_map/reduce_scatter | solution.py:649
  498.2 23.6 %collective-permute-start.28 = (bf16[192,2560]{1,0:T(8,128)(2,1)S(1)}, bf16[192,2560]{1,0:T(8,128)(2,1)S(1)}, u32[]{:S(2)}, u32[]{:S(2)}) collective-permute-start(bf16[192,2560]{1,0:T(8,128)(2,1)S(1)} %bitcast.373), channel_id=1, source_target_pairs={{0,1},{1,0},{2,3},{3,2},{4,5},{5,4},{6,7},{7,6},{8,9},{9,8},{10,11... | collective-permute-start | bytes 2949128 | tf_op jit(solution)/shard_map/ppermute | solution.py:309
  500.4 23.4 %collective-permute-start.27 = (bf16[192,2560]{1,0:T(8,128)(2,1)}, bf16[192,2560]{1,0:T(8,128)(2,1)S(1)}, u32[]{:S(2)}, u32[]{:S(2)}) collective-permute-start(bf16[192,2560]{1,0:T(8,128)(2,1)} %bitcast.70), channel_id=1, source_target_pairs={{0,4},{4,0},{1,5},{5,1},{2,6},{6,2},{3,7},{7,3},{8,12},{12,8},{9,1... | collective-permute-start | bytes 2949128 | tf_op jit(solution)/shard_map/ppermute | solution.py:309
  524.2 11.9 %collective-permute-start.29 = (bf16[96,2560]{1,0:T(8,128)(2,1)S(1)}, bf16[96,2560]{1,0:T(8,128)(2,1)S(1)}, u32[]{:S(2)}, u32[]{:S(2)}) collective-permute-start(bf16[96,2560]{1,0:T(8,128)(2,1)S(1)} %slice.761), channel_id=1, source_target_pairs={{0,1},{1,0},{2,3},{3,2},{4,5},{5,4},{6,7},{7,6},{8,9},{9,8},{10,11... | collective-permute-start | bytes 1474568 | tf_op jit(solution)/shard_map/ppermute | solution.py:309
  525.0 11.6 %collective-permute-start.30 = (bf16[96,2560]{1,0:T(8,128)(2,1)S(1)}, bf16[96,2560]{1,0:T(8,128)(2,1)S(1)}, u32[]{:S(2)}, u32[]{:S(2)}) collective-permute-start(bf16[96,2560]{1,0:T(8,128)(2,1)S(1)} %slice.764), channel_id=1, source_target_pairs={{0,4},{4,0},{1,5},{5,1},{2,6},{6,2},{3,7},{7,3},{8,12},{12,8},{9,1... | collective-permute-start | bytes 1474568 | tf_op jit(solution)/shard_map/ppermute | solution.py:309
  547.4 12.6 %collective-permute-start.32 = (bf16[768,2560]{1,0:T(8,128)(2,1)}, bf16[768,2560]{1,0:T(8,128)(2,1)}, u32[]{:S(2)}, u32[]{:S(2)}) collective-permute-start(bf16[768,2560]{1,0:T(8,128)(2,1)} %shard_map.399), channel_id=1, source_target_pairs={{0,2},{2,0},{1,3},{3,1},{4,6},{6,4},{5,7},{7,5},{8,10},{10,8},{9,1... | collective-permute-start | bytes 11796488 | tf_op jit(solution)/shard_map/ppermute | solution.py:309
  549.9 339.0 %reduce-scatter.8.cloned.1.call-start = ((), (), s32[]{:S(2)}) async-start(), calls=%async_computation.8 | async-start | bytes 6553600 | tf_op jit(solution)/shard_map/reduce_scatter | solution.py:413
  549.9 23.6 %collective-permute-start.31 = (bf16[192,2560]{1,0:T(8,128)(2,1)S(1)}, bf16[192,2560]{1,0:T(8,128)(2,1)S(1)}, u32[]{:S(2)}, u32[]{:S(2)}) collective-permute-start(bf16[192,2560]{1,0:T(8,128)(2,1)S(1)} %fusion.135), channel_id=1, source_target_pairs={{0,1},{1,0},{2,3},{3,2},{4,5},{5,4},{6,7},{7,6},{8,9},{9,8},{10,11... | collective-permute-start | bytes 2949128 | tf_op jit(solution)/shard_map/ppermute | solution.py:309
  587.1 51.0 %collective-permute-start.42 = (bf16[384,1280]{1,0:T(8,128)(2,1)S(1)}, bf16[384,1280]{1,0:T(8,128)(2,1)}, u32[]{:S(2)}, u32[]{:S(2)}) collective-permute-start(bf16[384,1280]{1,0:T(8,128)(2,1)S(1)} %get-tuple-element.143), channel_id=1, source_target_pairs={{0,4},{4,0},{1,5},{5,1},{2,6},{6,2},{3,7},{7,3},{8,12},{12,8},{9,1... | collective-permute-start | bytes 2949128 | tf_op jit(solution)/shard_map/ppermute | solution.py:309
  601.5 21.0 %collective-permute-start.35 = (bf16[4,160,384]{2,1,0:T(8,128)(2,1)S(1)}, bf16[4,160,384]{2,1,0:T(8,128)(2,1)S(1)}, u32[]{:S(2)}, u32[]{:S(2)}) collective-permute-start(bf16[4,160,384]{2,1,0:T(8,128)(2,1)S(1)} %get-tuple-element.329), channel_id=1, source_target_pairs={{0,6},{2,4},{4,2},{6,0},{1,7},{3,5},{5,3},{7,1},{8,14},{10,12},{12... | collective-permute-start | bytes 1474568 | tf_op jit(solution)/shard_map/ppermute | solution.py:389
  602.8 19.7 %collective-permute-start.34 = (bf16[4,160,384]{2,1,0:T(8,128)(2,1)S(1)}, bf16[4,160,384]{2,1,0:T(8,128)(2,1)S(1)}, u32[]{:S(2)}, u32[]{:S(2)}) collective-permute-start(bf16[4,160,384]{2,1,0:T(8,128)(2,1)S(1)} %get-tuple-element.330), channel_id=1, source_target_pairs={{0,2},{2,0},{4,6},{6,4},{1,3},{3,1},{5,7},{7,5},{8,10},{10,8},{12,... | collective-permute-start | bytes 1474568 | tf_op jit(solution)/shard_map/ppermute | solution.py:389
  602.8 28.0 %collective-permute-start.33 = (bf16[4,160,384]{2,1,0:T(8,128)(2,1)S(1)}, bf16[4,160,384]{2,1,0:T(8,128)(2,1)S(1)}, u32[]{:S(2)}, u32[]{:S(2)}) collective-permute-start(bf16[4,160,384]{2,1,0:T(8,128)(2,1)S(1)} %get-tuple-element.331), channel_id=1, source_target_pairs={{0,4},{2,6},{4,0},{6,2},{1,5},{3,7},{5,1},{7,3},{8,12},{10,14},{12... | collective-permute-start | bytes 1474568 | tf_op jit(solution)/shard_map/ppermute | solution.py:389
  604.5 73.0 %collective-permute-start.41 = (bf16[384,2560]{1,0:T(8,128)(2,1)S(1)}, bf16[384,2560]{1,0:T(8,128)(2,1)S(1)}, u32[]{:S(2)}, u32[]{:S(2)}) collective-permute-start(bf16[384,2560]{1,0:T(8,128)(2,1)S(1)} %pad_maximum_fusion.13), channel_id=1, source_target_pairs={{0,1},{1,0},{2,3},{3,2},{4,5},{5,4},{6,7},{7,6},{8,9},{9,8},{10,11... | collective-permute-start | bytes 5898248 | tf_op jit(solution)/shard_map/ppermute | solution.py:309
  631.1 5.7 collective-permute-start.36
  639.4 48.7 %collective-permute-start.43 = (bf16[768,1280]{1,0:T(8,128)(2,1)S(1)}, bf16[768,1280]{1,0:T(8,128)(2,1)S(1)}, u32[]{:S(2)}, u32[]{:S(2)}) collective-permute-start(bf16[768,1280]{1,0:T(8,128)(2,1)S(1)} %pad_maximum_fusion.14), channel_id=1, source_target_pairs={{0,2},{2,0},{1,3},{3,1},{4,6},{6,4},{5,7},{7,5},{8,10},{10,8},{9,1... | collective-permute-start | bytes 5898248 | tf_op jit(solution)/shard_map/ppermute | solution.py:309
  641.6 35.7 %collective-permute-start.40 = (bf16[1,32,1280]{2,1,0:T(8,128)(2,1)S(1)}, bf16[1,32,1280]{2,1,0:T(8,128)(2,1)S(1)}, u32[]{:S(2)}, u32[]{:S(2)}) collective-permute-start(bf16[1,32,1280]{2,1,0:T(8,128)(2,1)S(1)} %get-tuple-element.265), channel_id=1, source_target_pairs={{24,0},{25,1},{26,2},{27,3},{28,4},{29,5},{30,6},{31,7}} | collective-permute-start | bytes 245768 | tf_op jit(solution)/shard_map/ppermute | solution.py:487
  642.5 14.7 %collective-permute-start.39 = (bf16[2,32,1280]{2,1,0:T(8,128)(2,1)S(1)}, bf16[2,32,1280]{2,1,0:T(8,128)(2,1)S(1)}, u32[]{:S(2)}, u32[]{:S(2)}) collective-permute-start(bf16[2,32,1280]{2,1,0:T(8,128)(2,1)S(1)} %pad_maximum_fusion.27), channel_id=1, source_target_pairs={{16,0},{24,8},{17,1},{25,9},{18,2},{26,10},{19,3},{27,11},{20,4},{... | collective-permute-start | bytes 491528 | tf_op jit(solution)/shard_map/ppermute | solution.py:487
  643.8 33.5 %collective-permute-start.38 = (bf16[2,32,1280]{2,1,0:T(8,128)(2,1)S(1)}, bf16[2,32,1280]{2,1,0:T(8,128)(2,1)S(1)}, u32[]{:S(2)}, u32[]{:S(2)}) collective-permute-start(bf16[2,32,1280]{2,1,0:T(8,128)(2,1)S(1)} %pad_maximum_fusion.27), channel_id=1, source_target_pairs={{8,0},{16,8},{24,16},{9,1},{17,9},{25,17},{10,2},{18,10},{26,18},{... | collective-permute-start | bytes 491528 | tf_op jit(solution)/shard_map/ppermute | solution.py:487
  686.3 5.5 collective-permute-start.46
  689.6 10.5 %collective-permute-start.44 = (bf16[96,1280]{1,0:T(8,128)(2,1)S(1)}, bf16[96,1280]{1,0:T(8,128)(2,1)S(1)}, u32[]{:S(2)}, u32[]{:S(2)}) collective-permute-start(bf16[96,1280]{1,0:T(8,128)(2,1)S(1)} %slice.1094), channel_id=1, source_target_pairs={{2,0},{4,2},{6,4},{8,6},{10,8},{12,10},{14,12},{16,14},{18,16},{20... | collective-permute-start | bytes 737288 | tf_op jit(solution)/shard_map/ppermute | solution.py:680
  692.0 18.6 %collective-permute-start.47 = (bf16[4,32,1280]{2,1,0:T(8,128)(2,1)S(1)}, bf16[4,32,1280]{2,1,0:T(8,128)(2,1)S(1)}, u32[]{:S(2)}, u32[]{:S(2)}) collective-permute-start(bf16[4,32,1280]{2,1,0:T(8,128)(2,1)S(1)} %dynamic-slice_bitcast_fusion.9), channel_id=1, source_target_pairs={{0,4},{4,0},{1,5},{5,1},{2,6},{6,2},{3,7},{7,3},{8,12},{12,8},{9,1... | collective-permute-start | bytes 983048 | tf_op jit(solution)/shard_map/ppermute | solution.py:309
  700.7 26.7 %collective-permute-start.45 = (bf16[384,1280]{1,0:T(8,128)(2,1)S(1)}, bf16[384,1280]{1,0:T(8,128)(2,1)S(1)}, u32[]{:S(2)}, u32[]{:S(2)}) collective-permute-start(bf16[384,1280]{1,0:T(8,128)(2,1)S(1)} %fusion.51), channel_id=1, source_target_pairs={{0,4},{4,0},{1,5},{5,1},{2,6},{6,2},{3,7},{7,3},{8,12},{12,8},{9,1... | collective-permute-start | bytes 2949128 | tf_op jit(solution)/shard_map/ppermute | solution.py:309
  729.0 5.8 collective-permute-start.48
  758.0 23.1 %collective-permute-start.49 = (bf16[192,2560]{1,0:T(8,128)(2,1)}, bf16[192,2560]{1,0:T(8,128)(2,1)}, u32[]{:S(2)}, u32[]{:S(2)}) collective-permute-start(bf16[192,2560]{1,0:T(8,128)(2,1)} %dynamic-slice_convert_fusion), channel_id=1, source_target_pairs={{0,1},{1,0},{2,3},{3,2},{4,5},{5,4},{6,7},{7,6},{8,9},{9,8},{10,11... | collective-permute-start | bytes 2949128 | tf_op jit(solution)/shard_map/ppermute | solution.py:309
  797.4 14.9 %collective-permute-start.58 = (f32[24,1280]{1,0:T(8,128)S(1)}, f32[24,1280]{1,0:T(8,128)S(1)}, u32[]{:S(2)}, u32[]{:S(2)}) collective-permute-start(f32[24,1280]{1,0:T(8,128)S(1)} %add.440), channel_id=1, source_target_pairs={{0,24},{8,0},{16,8},{24,16},{1,25},{9,1},{17,9},{25,17},{2,26},{10... | collective-permute-start | bytes 368648 | tf_op jit(solution)/shard_map/ppermute | solution.py:423
  797.5 14.8 %collective-permute-start.57 = (f32[24,1280]{1,0:T(8,128)S(1)}, f32[24,1280]{1,0:T(8,128)S(1)}, u32[]{:S(2)}, u32[]{:S(2)}) collective-permute-start(f32[24,1280]{1,0:T(8,128)S(1)} %add.440), channel_id=1, source_target_pairs={{0,16},{8,24},{16,0},{24,8},{1,17},{9,25},{17,1},{25,9},{2,18},{10... | collective-permute-start | bytes 368648 | tf_op jit(solution)/shard_map/ppermute | solution.py:423
  798.1 21.9 %collective-permute-start.56 = (f32[24,1280]{1,0:T(8,128)S(1)}, f32[24,1280]{1,0:T(8,128)S(1)}, u32[]{:S(2)}, u32[]{:S(2)}) collective-permute-start(f32[24,1280]{1,0:T(8,128)S(1)} %add.440), channel_id=1, source_target_pairs={{0,8},{8,16},{16,24},{24,0},{1,9},{9,17},{17,25},{25,1},{2,10},{10... | collective-permute-start | bytes 368648 | tf_op jit(solution)/shard_map/ppermute | solution.py:423
  800.2 22.6 %collective-permute-start.53 = (bf16[192,2560]{1,0:T(8,128)(2,1)}, bf16[192,2560]{1,0:T(8,128)(2,1)}, u32[]{:S(2)}, u32[]{:S(2)}) collective-permute-start(bf16[192,2560]{1,0:T(8,128)(2,1)} %slice.677), channel_id=1, source_target_pairs={{0,4},{4,0},{1,5},{5,1},{2,6},{6,2},{3,7},{7,3},{8,12},{12,8},{9,1... | collective-permute-start | bytes 2949128 | tf_op jit(solution)/shard_map/ppermute | solution.py:309
  804.8 61.3 %collective-permute-start.61 = (bf16[1,2,160,1536]{3,2,1,0:T(8,128)(2,1)}, bf16[1,2,160,1536]{3,2,1,0:T(8,128)(2,1)}, u32[]{:S(2)}, u32[]{:S(2)}) collective-permute-start(bf16[1,2,160,1536]{3,2,1,0:T(8,128)(2,1)} %get-tuple-element.289), channel_id=1, source_target_pairs={{0,6},{2,4},{4,2},{6,0},{1,7},{3,5},{5,3},{7,1},{8,14},{10,12},{12... | collective-permute-start | bytes 2949128 | tf_op jit(solution)/shard_map/ppermute | solution.py:434
  812.3 52.5 %collective-permute-start.60 = (bf16[1,2,160,1536]{3,2,1,0:T(8,128)(2,1)}, bf16[1,2,160,1536]{3,2,1,0:T(8,128)(2,1)}, u32[]{:S(2)}, u32[]{:S(2)}) collective-permute-start(bf16[1,2,160,1536]{3,2,1,0:T(8,128)(2,1)} %get-tuple-element.290), channel_id=1, source_target_pairs={{0,4},{2,6},{4,0},{6,2},{1,5},{3,7},{5,1},{7,3},{8,12},{10,14},{12... | collective-permute-start | bytes 2949128 | tf_op jit(solution)/shard_map/ppermute | solution.py:434
  812.3 17.0 %collective-permute-start.59 = (bf16[1,2,160,1536]{3,2,1,0:T(8,128)(2,1)}, bf16[1,2,160,1536]{3,2,1,0:T(8,128)(2,1)}, u32[]{:S(2)}, u32[]{:S(2)}) collective-permute-start(bf16[1,2,160,1536]{3,2,1,0:T(8,128)(2,1)} %get-tuple-element.291), channel_id=1, source_target_pairs={{0,2},{2,0},{4,6},{6,4},{1,3},{3,1},{5,7},{7,5},{8,10},{10,8},{12,... | collective-permute-start | bytes 2949128 | tf_op jit(solution)/shard_map/ppermute | solution.py:434
  827.8 44.3 %collective-permute-start.55 = (bf16[192,2560]{1,0:T(8,128)(2,1)S(1)}, bf16[192,2560]{1,0:T(8,128)(2,1)S(1)}, u32[]{:S(2)}, u32[]{:S(2)}) collective-permute-start(bf16[192,2560]{1,0:T(8,128)(2,1)S(1)} %get-tuple-element.324), channel_id=1, source_target_pairs={{0,1},{1,0},{2,3},{3,2},{4,5},{5,4},{6,7},{7,6},{8,9},{9,8},{10,11... | collective-permute-start | bytes 2949128 | tf_op jit(solution)/shard_map/ppermute | solution.py:309
  829.2 44.5 %collective-permute-start.54 = (bf16[192,2560]{1,0:T(8,128)(2,1)S(1)}, bf16[192,2560]{1,0:T(8,128)(2,1)S(1)}, u32[]{:S(2)}, u32[]{:S(2)}) collective-permute-start(bf16[192,2560]{1,0:T(8,128)(2,1)S(1)} %get-tuple-element.325), channel_id=1, source_target_pairs={{0,1},{1,0},{2,3},{3,2},{4,5},{5,4},{6,7},{7,6},{8,9},{9,8},{10,11... | collective-permute-start | bytes 2949128 | tf_op jit(solution)/shard_map/ppermute | solution.py:309
  (102 other events, 867.9 us)
Sparse Core Ops, SparseCore 0:
  10.2 129.8 all-gather.5
  154.3 148.6 all-gather.7
  304.6 140.3 all-gather.9
  479.6 136.8 reduce-scatter.3
  618.6 151.6 reduce-scatter.5
  785.6 103.2 reduce-scatter.7

commit v3 on v2

--- a/solution.py
+++ b/solution.py
@@ -414,13 +414,19 @@
 
 
 def sum_plane(v):
-    v = v + swap(v, "c")
-    return v + swap(v, "x") if lax.axis_size("x") == 2 else lax.psum(v, "x")
+    if lax.axis_size("x") != 2:
+        v = v + swap(v, "c")
+        return lax.psum(v, "x")
+    return sum([lax.ppermute(v, ("x", "c"), [(j, j ^ flip) for j in range(4)]) for flip in (1, 2, 3)], v)
 
 
 def sum_planes(v):
     count = lax.axis_size("z")
     return sum([lax.ppermute(v, "z", [(j, (j + far) % count) for j in range(count)]) for far in range(1, count)], v)
+
+
+def sum_line(v):
+    return lax.psum_scatter(v, "z", scatter_dimension=0, tiled=True)
 
 
 def to_slices(v):
@@ -449,47 +455,47 @@
     return jnp.concatenate([jnp.where(low, own, other), jnp.where(low, other, own)], axis=0)
 
 
-def ranks(value, axis):
+def ranks(value, axis, beside):
     count = lax.axis_size(axis)
     if count == 2:
-        other = swap(value, axis)
+        other, *beside = tie(swap(value, axis), *beside)
         low = lax.axis_index(axis) == 0
-        return [jnp.where(low, value, other), jnp.where(low, other, value)]
-    every = lax.all_gather(value, axis)
-    return [every[j] for j in range(count)]
-
-
-def carry_in(state, total, backward):
-    pair = jnp.stack([state, total])
-    inner = []
-    for axis, kind in (("c", F32), ("x", BF16)):
-        parts = [part.astype(F32) for part in ranks(pair.astype(kind), axis)]
-        order = range(len(parts))
-        at = lax.axis_index(axis)
+        return [jnp.where(low, value, other), jnp.where(low, other, value)], beside
+    every, *beside = tie(lax.all_gather(value, axis), *beside)
+    return [every[j] for j in range(count)], beside
+
+
+def carry_axis(pair, axis, kind, backward, beside=()):
+    parts, beside = ranks(pair.astype(kind), axis, beside)
+    parts = [part.astype(F32) for part in parts]
+    order, at = range(len(parts)), lax.axis_index(axis)
+    if backward:
+        order, at = [len(parts) - 1 - j for j in order], len(parts) - 1 - at
+    gone = jnp.stack([jnp.zeros_like(pair[0]), jnp.ones_like(pair[1])])
+    mine = gone
+    for place, j in enumerate(order):
+        mine = jnp.where(at == place, gone, mine)
+        gone = jnp.stack([parts[j][0] + parts[j][1] * gone[0], parts[j][1] * gone[1]])
+    return (gone, mine, *beside)
+
+
+def carry_planes(pair, inner, backward, beside=()):
+    sent = pair.astype(BF16)
+    steps = []
+    for far in range(1, PLANES):
         if backward:
-            order, at = [len(parts) - 1 - j for j in order], len(parts) - 1 - at
-        gone = jnp.stack([jnp.zeros_like(state), jnp.ones_like(total)])
-        mine = gone
-        for place, j in enumerate(order):
-            mine = jnp.where(at == place, gone, mine)
-            gone = jnp.stack([parts[j][0] + parts[j][1] * gone[0], parts[j][1] * gone[1]])
-        inner.append(mine)
-        pair = gone
-    planes = lax.axis_size("z")
-    sent = pair.astype(BF16)
-    entering = jnp.zeros_like(state)
-    steps = []
-    for far in range(1, planes):
-        if backward:
-            route = [(j + far, j) for j in range(planes - far)]
+            route = [(j + far, j) for j in range(PLANES - far)]
         else:
-            route = [(j, j + far) for j in range(planes - far)]
-        steps.append(lax.ppermute(sent if far < planes - 1 else sent[:1], "z", route).astype(F32))
+            route = [(j, j + far) for j in range(PLANES - far)]
+        steps.append(lax.ppermute(sent if far < PLANES - 1 else sent[:1], "z", route))
+    values = tie(*steps, *beside)
+    steps, beside = [step.astype(F32) for step in values[: len(steps)]], values[len(steps) :]
+    entering = jnp.zeros_like(pair[0])
     for step in reversed(steps):
         entering = step[0] + (step[1] * entering if step.shape[0] == 2 else 0.0)
     for mine in reversed(inner):
         entering = mine[0] + mine[1] * entering
-    return entering
+    return (entering, *beside)
 
 
 def norm(v, gain):
@@ -604,7 +610,9 @@
     ext_row = lax.broadcasted_iota(jnp.int32, (rows + halo, 1), 0)
     recur = jnp.where(jnp.logical_and(ext_row < halo, place == 0), 0.0, recur)
     conv, sig_in, sig_dec, end, total = gates(first, recur, coefs, inlet_full, decay_full)
-    carry = carry_in(end, total, False)
+    ends, by_core = carry_axis(jnp.stack([end, total]), "c", F32, False)
+    ends, by_mid = carry_axis(ends, "x", BF16, False)
+    (carry,) = carry_planes(ends, (by_core, by_mid), False)
     branch = dot(normed, branch_full) + vec_branch
     state, mixed = states(first, conv, sig_in, sig_dec, branch, coefs, carry)
     mixed_own, mixed_other = halves(mixed, "y")
@@ -646,20 +654,17 @@
     last_grads, last_sums = feed_grads(plane, d_plane, d_pre[-1], hidden[-1])
     d_second_own, last_sums = scatter_plane(d_pair, last_sums)
     bias_grads = [sums[0].reshape(2, step) for sums in [*bias_grads, last_sums]]
-    ffn_grads = [lax.psum_scatter(grad, "z", scatter_dimension=0, tiled=True) for grad in ffn_grads + [last_grads]]
+    ffn_grads = [sum_line(grad) for grad in ffn_grads]
     d_middle, grad_gain_two = norm_back(middle, scale_two, gain_two, d_second_own)
     d_middle = d_middle + d_own.astype(F32)
     d_low_own = d_middle.astype(BF16)
-    d_low_own, *hidden = tie(d_low_own, *hidden)
-    low_other, out_pair = tie(swap(d_low_own, "y"), pair_sum(hidden, 2))
-    out_side = scatter_side(out_pair)
+    dealt_own = deal_group(d_low_own.T)
+    low_other, dealt_own = tie(swap(d_low_own, "y"), dealt_own)
     is_low = side == 0
     d_low = jnp.concatenate([jnp.where(is_low, d_low_own, low_other), jnp.where(is_low, low_other, d_low_own)], axis=0)
     d_mixed = dot(d_low, output_full)
     pulled, d_branch, end_back, branch_sum = branch_back(d_mixed, branch, state, sig_dec, coefs)
-    low_dealt = deal_group(d_low.T)
-    end_back, low_dealt = tie(end_back, low_dealt)
-    late = carry_in(end_back, total, True)
+    dealt_other = swap(dealt_own, "y")
 
     def by_plane(grad):
         return grad.astype(BF16).reshape(PLANES, part, channels)
@@ -667,11 +672,14 @@
     def by_owner(grad):
         return grad.reshape(groups, -1, channels)
 
-    d_normed_first = dot(d_branch, branch_full, ((1,), (1,)))
-    late, d_normed_first, *out_side = tie(late, d_normed_first, *(out_side if mid == 2 else [out_side]))
-    if mid == 2:
-        out_side = ((out_side[0].astype(F32) + out_side[1].astype(F32)).astype(BF16),)
-    out_side = out_side[0]
+    end_back, last_grads, *ffn_grads = tie(end_back, last_grads, *ffn_grads)
+    ffn_grads.append(sum_line(last_grads))
+    ends, by_core, *hidden = carry_axis(jnp.stack([end_back, total]), "c", F32, True, hidden)
+    out_far, out_near = [feed_back(hidden, ffn_full, j, 2, CORES) for j in (1, 0)]
+    ends, by_mid, out_far, d_branch = carry_axis(ends, "x", BF16, True, (out_far, d_branch))
+    late, out_near, mixed_group = carry_planes(ends, (by_core, by_mid), True, (out_near, mixed_group))
+    out_pair = (out_near.astype(F32) + swap(out_far, "c").astype(F32)).astype(BF16)
+    out_side = scatter_side(out_pair) if mid == 2 else (scatter_side(out_pair),)
     d_conv, grad_inlet, grad_decay, core_sums = core_back(
         first, pulled, conv, sig_in, sig_dec, state, recur, coefs, carry, late, inlet_full, decay_full
     )
@@ -685,19 +693,24 @@
     d_recur = d_recur.astype(BF16)
     recur_near = swap(d_recur, "x") if mid == 2 else lax.all_gather(d_recur, "x", axis=0, tiled=True)
     gates_b = fold_mid(fold_cores(jnp.concatenate([by_owner(grad_inlet), by_owner(grad_decay)], axis=1)))
-    grad_output, grad_branch = dot(low_dealt, mixed_group), dot(normed_dealt, branch_group)
+    recur_near, dealt_other, *out_side = tie(recur_near, dealt_other, *out_side)
+    mixed_sides = [lax.dynamic_index_in_dim(mixed_group.reshape(mid * CORES, 2, -1, channels), j, 1, keepdims=False)
+                   .reshape(-1, channels) for j in (side, 1 - side)]
+    grad_output = dot(dealt_own, mixed_sides[0]) + dot(dealt_other, mixed_sides[1])
+    grad_branch = dot(normed_dealt, branch_group)
     packed = [by_plane(grad_output), by_plane(grad_branch)]
-    recur_near, gates_b, *packed = tie(recur_near, gates_b, *packed)
     recur_near = jnp.concatenate([d_recur, recur_near], axis=0) if mid == 2 else recur_near
     packed += [by_plane(dot(normed_dealt, gather_rows(recur_near, "c"))), gates_b]
     packed = jnp.concatenate(packed, axis=1)
-    packed, d_recur = tie(packed, d_recur)
-    d_normed = d_normed_first + dot(d_recur, recur_full, ((1,), (1,)))
+    packed, d_recur, *ffn_grads = tie(packed, d_recur, *ffn_grads)
+    sums = fold_planes(packed)
+    d_normed = dot(d_branch, branch_full, ((1,), (1,))) + dot(d_recur, recur_full, ((1,), (1,)))
     dn_own, dn_other = halves(d_normed, "y")
     dn_got = swap(dn_other.astype(BF16), "y")
-    packed, dn_got, out_side, *ffn_grads = tie(packed, dn_got, out_side, *ffn_grads)
-    sums = fold_planes(packed)
     dn_own = dn_own + dn_got.astype(F32)
+    if mid == 2:
+        out_side = [(out_side[0].astype(F32) + out_side[1].astype(F32)).astype(BF16)]
+    out_side = out_side[0]
     scale_one = lax.rsqrt(jnp.mean(x_own * x_own, axis=-1, keepdims=True) + 1e-6)
     d_input, grad_gain_one = norm_back(x_own, scale_one, gain_one, dn_own)
     d_input = whole_rows((d_middle + d_input).astype(BF16), "y")
@@ -717,7 +730,7 @@
     )
     small = sum_plane(small)
     returned = jnp.stack([grad.reshape(slices, part, 3 * step) for grad in ffn_grads], axis=1)
-    small, out_side, returned = tie(small, out_side, returned)
+    small, returned = tie(small, returned)
 
     mask_own, _ = halves(mask, "y")
     result = jnp.where(mask_own, middle + scatter_rows(out_side, "x").astype(F32) + vec_shrink, 0.0).astype(BF16)

time: 909 us -> 887 us (0.976)
  waiting for transfers between devices: 325 us -> 292 us
    ppermute x6, waiting for transfers between devices: 39.6 us -> 15.6 us  [deal_group(): lax.ppermute(part, ('x', 'c'), [(j, j ^ flip) for j in range(4)])]
    ppermute x9, waiting for transfers between devices: 34.2 us -> 14.7 us  [to_slices(): lax.ppermute(pick(v, other), ('x', 'c'), [(j, j ^ flip) for j in range(4)])]
    ppermute x36 -> x35, waiting for transfers between devices: 165 us -> 180 us  [swap(): return lax.ppermute(v, axis, [(0, 1), (1, 0)])]
    reduce_scatter x1, waiting for transfers between devices: 13.5 us -> 0.01 us  [fold_planes(): lax.psum_scatter(v, 'z', scatter_dimension=0, tiled=False).astype(F32)]
    all_gather x2, waiting for transfers between devices: 0.01 us -> 10 us  [body(): lax.all_gather(weights, 'z', axis=0, tiled=True)]
    reduce_scatter x2, waiting for transfers between devices: 0.01 us -> 9.3 us  [sum_line(): return lax.psum_scatter(v, 'z', scatter_dimension=0, tiled=True)]
    unnamed x241 -> x253, local copies, waits for them, and re-layouts: 29 us -> 35.6 us
    dot_general x10 -> x11, matrix products: 59.5 us -> 54.6 us  [dot(): return lax.dot_general(a, b, (dims, ((), ())), preferred_element_type=F32)]
  transfers between devices with their start and end apart: 68 -> 70, of which waited for: 30 -> 27; matrix products, arithmetic and copies ran while one was open for 23% -> 23% of each run, Pallas kernels for 12% -> 16%
where the time goes in v3:
time: 887 us; the launch traced here: 879 us
  waiting for transfers between devices  292 us (33%)
  Pallas kernels  142 us (16%)
  local copies, waits for them, and re-layouts  105 us (12%)
  blocking collectives  100 us (11%)
  starting transfers between devices  90.2 us (10%)
  other arithmetic  75.9 us (9%)
  matrix products  54.6 us (6%)
  between operations  18.1 us (2%)
    ppermute x35, waiting for transfers between devices, swap(): return lax.ppermute(v, axis, [(0, 1), (1, 0)])  180 us
    ppermute x6, waiting for transfers between devices, carry_planes(): lax.ppermute(sent if far < PLANES - 1 else sent[:1], 'z', route)  55.6 us
    dot_general x11, matrix products, dot(): return lax.dot_general(a, b, (dims, ((), ())), preferred_element_type=F32)  54.6 us
    all_gather x1, blocking collectives, body(): every = lax.all_gather(flat, DP, axis=0, tiled=False).astype(F32)  54.1 us
    ppermute x35, starting transfers between devices, swap(): return lax.ppermute(v, axis, [(0, 1), (1, 0)])  48.7 us
    pallas_call x4, Pallas kernels, feed_back(): pl.pallas_call(back_kernel, grid=(width // tile,), in_specs=[pl.BlockSpec...  43.3 us
    pallas_call x2, Pallas kernels, feed(): pl.pallas_call(functools.partial(feed_kernel, first_unit=first_unit), gri...  37.9 us
    pallas_call x2, Pallas kernels, feed_grads(): pl.pallas_call(grad_kernel, grid=(width // tile,), in_specs=[pl.BlockSpec...  36.8 us
  transfers between devices with their start and end apart: 70, of which 27 were waited for; matrix products, arithmetic and copies ran while one was open for 23% of the time, Pallas kernels for 16%

profile of v3, /device:TPU:9, one launch (start us, length us, event | category | flops | bytes accessed | tf_op | source)
XLA Modules:
  0.0 879.2 jit_solution(12963247143063727595)
XLA Ops:
  10.7 3.7 collective-permute-start
  24.8 54.1 %all-gather.1 = bf16[16,1,1920]{2,1,0:T(2,128)(2,1)S(1)} all-gather(bf16[1,1,1920]{2,1,0:T(2,128)(2,1)S(1)} %reshape.697), channel_id=2, replica_groups=mesh['z'=4,'x'=2,'c'=2,'y'=2] {'z','x','c'}, dimensions={0}, use_global_device_ids=true | all-gather | bytes 65280 | tf_op jit(solution)/shard_map/all_gather | solution.py:542
  88.0 21.9 %all_gather.25.wd_ref = bf16[256,1280]{1,0:T(8,128)(2,1)S(1)} all-gather(bf16[16,1280]{1,0:T(8,128)(2,1)S(1)} %bitcast.394), channel_id=1, replica_groups=mesh['z'=4,'x'=2,'c'=2,'y'=2] {'z','x','c'}, dimensions={0}, use_global_device_ids=true | all-gather | bytes 696320 | tf_op jit(solution)/shard_map/all_gather | solution.py:538
  109.9 24.4 %all_gather.24.wi_ref = bf16[256,1280]{1,0:T(8,128)(2,1)S(1)} all-gather(bf16[16,1280]{1,0:T(8,128)(2,1)S(1)} %bitcast.393), channel_id=1, replica_groups=mesh['z'=4,'x'=2,'c'=2,'y'=2] {'z','x','c'}, dimensions={0}, use_global_device_ids=true | all-gather | bytes 696320 | tf_op jit(solution)/shard_map/all_gather | solution.py:537
  149.7 3.1 fusion.23
  158.3 8.4 fusion.41.r_ref
  166.7 5.7 shard_map.391
  172.5 8.3 fusion.48.b_ref
  181.3 10.2 %collective-permute-done.5 = bf16[2,32,1280]{2,1,0:T(8,128)(2,1)S(1)} collective-permute-done((bf16[2,32,1280]{2,1,0:T(8,128)(2,1)S(1)}, bf16[2,32,1280]{2,1,0:T(8,128)(2,1)S(1)}, u32[]{:S(2)}, u32[]{:S(2)}) %collective-permute-start.5) | collective-permute-done | bytes 163872 | tf_op jit(solution)/shard_map/ppermute | solution.py:309
  192.3 3.2 collective-permute-start.7
  197.5 14.4 %collective-permute-done.7 = bf16[2,32,1280]{2,1,0:T(8,128)(2,1)S(1)} collective-permute-done((bf16[2,32,1280]{2,1,0:T(8,128)(2,1)S(1)}, bf16[2,32,1280]{2,1,0:T(8,128)(2,1)S(1)}, u32[]{:S(2)}, u32[]{:S(2)}) %collective-permute-start.7) | collective-permute-done | bytes 163872 | tf_op jit(solution)/shard_map/ppermute | solution.py:490
  212.3 11.9 %collective-permute-done.6 = bf16[2,32,1280]{2,1,0:T(8,128)(2,1)S(1)} collective-permute-done((bf16[2,32,1280]{2,1,0:T(8,128)(2,1)S(1)}, bf16[2,32,1280]{2,1,0:T(8,128)(2,1)S(1)}, u32[]{:S(2)}, u32[]{:S(2)}) %collective-permute-start.6) | collective-permute-done | bytes 163872 | tf_op jit(solution)/shard_map/ppermute | solution.py:490
  224.3 5.5 shard_map.392
  229.9 7.1 fusion.35
  242.1 18.0 %collective-permute-done.9 = bf16[192,2560]{1,0:T(8,128)(2,1)} collective-permute-done((bf16[192,2560]{1,0:T(8,128)(2,1)}, bf16[192,2560]{1,0:T(8,128)(2,1)}, u32[]{:S(2)}, u32[]{:S(2)}) %collective-permute-start.9) | collective-permute-done | bytes 983072 | tf_op jit(solution)/shard_map/ppermute | solution.py:309
  260.1 5.8 multiply_reduce_fusion.2
  270.2 7.4 collective-permute-done.10
  280.4 20.5 %collective-permute-done.11 = bf16[192,2560]{1,0:T(8,128)(2,1)S(1)} collective-permute-done((bf16[192,2560]{1,0:T(8,128)(2,1)S(1)}, bf16[192,2560]{1,0:T(8,128)(2,1)S(1)}, u32[]{:S(2)}, u32[]{:S(2)}) %collective-permute-start.11) | collective-permute-done | bytes 983072 | tf_op jit(solution)/shard_map/ppermute | solution.py:309
  302.6 8.8 collective-permute-done.12
  313.0 18.3 %collective-permute-done.13 = bf16[192,2560]{1,0:T(8,128)(2,1)S(1)} collective-permute-done((bf16[192,2560]{1,0:T(8,128)(2,1)S(1)}, bf16[192,2560]{1,0:T(8,128)(2,1)S(1)}, u32[]{:S(2)}, u32[]{:S(2)}) %collective-permute-start.13) | collective-permute-done | bytes 983072 | tf_op jit(solution)/shard_map/ppermute | solution.py:309
  331.5 4.4 collective-permute-start.14
  350.4 19.2 %collective-permute-done.24 = bf16[384,1280]{1,0:T(8,128)(2,1)S(1)} collective-permute-done((bf16[384,1280]{1,0:T(8,128)(2,1)S(1)}, bf16[384,1280]{1,0:T(8,128)(2,1)S(1)}, u32[]{:S(2)}, u32[]{:S(2)}) %collective-permute-start.24) | collective-permute-done | bytes 983072 | tf_op jit(solution)/shard_map/ppermute | solution.py:309
  375.1 4.0 copy.133
  379.2 2.8 constant_dynamic-slice_fusion.15
  383.8 4.3 constant_dynamic-update-slice_fusion.13.d_ref
  388.1 19.0 %shard_map.393 = (bf16[1536,512]{1,0:T(8,128)(2,1)}, bf16[1536,1024]{1,0:T(8,128)(2,1)}) custom-call(s32[1]{0:T(128)S(6)} %mul.368.at_ref, bf16[1536,2560]{1,0:T(8,128)(2,1)} %copy-done.8, bf16[1536,2560]{1,0:T(8,128)(2,1)} %constant_dynamic-update-slice_fusion.13.d_ref, bf16[2560,1536]{1,0:T(8,128)(2,1)} %all-gather.8.cloned.1.call-done.w_ref.refs_2_, ...), custom_call_target="tpu_custom_call" | custom-call | flops 1 | bytes 1 | tf_op jit(solution)/shard_map/pallas_call | solution.py:228
  407.1 18.3 %shard_map.394 = (bf16[2560,1536]{1,0:T(8,128)(2,1)}, f32[8,1024]{1,0:T(8,128)}) custom-call(bf16[1536,2560]{1,0:T(8,128)(2,1)} %copy-done.8, bf16[1536,2560]{1,0:T(8,128)(2,1)} %constant_dynamic-update-slice_fusion.13.d_ref, bf16[1536,1024]{1,0:T(8,128)(2,1)} %get-tuple-element.120.g_ref.refs_0_, bf16[1536,512]{1,0:T(8,128)(2,1)} %get-tuple-element.145.h_ref.refs_0_), custom_call_target="tpu_custom_call" | custom-call | flops 1 | bytes 1 | tf_op jit(solution)/shard_map/pallas_call | solution.py:267
  427.2 3.1 pad_maximum_fusion.7
  430.3 3.4 pad_maximum_fusion.1
  433.6 10.0 %all-gather.10.cloned.1.call-done.w_ref.refs_3_ = bf16[2560,1536]{1,0:T(8,128)(2,1)} async-done(((bf16[640,1536]{1,0:T(8,128)(2,1)}), bf16[2560,1536]{1,0:T(8,128)(2,1)}) %all-gather.10.cloned.1.call-update) | async-done | bytes 7864336 | tf_op jit(solution)/shard_map/all_gather | solution.py:603
  443.6 18.9 %shard_map.395 = (bf16[1536,512]{1,0:T(8,128)(2,1)}, bf16[1536,1024]{1,0:T(8,128)(2,1)}) custom-call(s32[1]{0:T(128)S(6)} %mul.368.at_ref, bf16[1536,2560]{1,0:T(8,128)(2,1)} %copy-done.8, bf16[1536,2560]{1,0:T(8,128)(2,1)} %constant_dynamic-update-slice_fusion.13.d_ref, bf16[2560,1536]{1,0:T(8,128)(2,1)} %all-gather.10.cloned.1.call-done.w_ref.refs_3_, ...), custom_call_target="tpu_custom_call" | custom-call | flops 1 | bytes 1 | tf_op jit(solution)/shard_map/pallas_call | solution.py:228
  462.6 12.6 %shard_map.396 = bf16[768,2560]{1,0:T(8,128)(2,1)} custom-call(bf16[1536,1024]{1,0:T(8,128)(2,1)} %get-tuple-element.120.g_ref.refs_0_, bf16[1536,1024]{1,0:T(8,128)(2,1)} %get-tuple-element.127.refs_1_.g_ref, bf16[2560,1536]{1,0:T(8,128)(2,1)} %all-gather.8.cloned.1.call-done.w_ref.refs_2_, bf16[2560,1536]{1,0:T(8,128)(2,1)} %all-gather.10.cloned.1.call-done.w_ref.refs_3_), custom_call_target="tpu_custom_call" | custom-call | flops 1 | bytes 1 | tf_op jit(solution)/shard_map/pallas_call | solution.py:296
  475.7 12.8 %shard_map.397 = bf16[768,2560]{1,0:T(8,128)(2,1)} custom-call(bf16[1536,1024]{1,0:T(8,128)(2,1)} %get-tuple-element.120.g_ref.refs_0_, bf16[1536,1024]{1,0:T(8,128)(2,1)} %get-tuple-element.127.refs_1_.g_ref, bf16[2560,1536]{1,0:T(8,128)(2,1)} %all-gather.8.cloned.1.call-done.w_ref.refs_2_, bf16[2560,1536]{1,0:T(8,128)(2,1)} %all-gather.10.cloned.1.call-done.w_ref.refs_3_), custom_call_target="tpu_custom_call" | custom-call | flops 1 | bytes 1 | tf_op jit(solution)/shard_map/pallas_call | solution.py:296
  488.6 3.1 add_convert_fusion.1
  496.2 18.5 %shard_map.398 = (bf16[2560,1536]{1,0:T(8,128)(2,1)}, f32[8,1024]{1,0:T(8,128)}) custom-call(bf16[1536,2560]{1,0:T(8,128)(2,1)} %copy-done.8, bf16[1536,2560]{1,0:T(8,128)(2,1)} %constant_dynamic-update-slice_fusion.13.d_ref, bf16[1536,1024]{1,0:T(8,128)(2,1)} %get-tuple-element.127.refs_1_.g_ref, bf16[1536,512]{1,0:T(8,128)(2,1)} %get-tuple-element.146.h_ref.refs_1_), custom_call_target="tpu_custom_call" | custom-call | flops 1 | bytes 1 | tf_op jit(solution)/shard_map/pallas_call | solution.py:267
  520.8 10.0 %collective-permute-done.29 = bf16[96,2560]{1,0:T(8,128)(2,1)S(1)} collective-permute-done((bf16[96,2560]{1,0:T(8,128)(2,1)S(1)}, bf16[96,2560]{1,0:T(8,128)(2,1)S(1)}, u32[]{:S(2)}, u32[]{:S(2)}) %collective-permute-start.29) | collective-permute-done | bytes 491552 | tf_op jit(solution)/shard_map/ppermute | solution.py:309
  538.8 3.4 collective-permute-start.34
  542.5 8.6 collective-permute-done.34
  551.1 7.0 collective-permute-done.32
  561.9 5.6 fusion.dm_ref
  567.4 5.2 shard_map.399
  573.9 9.3 %reduce-scatter.4.cloned.1.call-done = bf16[640,1536]{1,0:T(8,128)(2,1)} async-done(((bf16[2560,1536]{1,0:T(8,128)(2,1)}), bf16[640,1536]{1,0:T(8,128)(2,1)}) %reduce-scatter.4.cloned.1.call-update) | async-done | bytes 1966096 | tf_op jit(solution)/shard_map/reduce_scatter | solution.py:429
  593.4 9.1 %shard_map.400 = bf16[768,2560]{1,0:T(8,128)(2,1)} custom-call(bf16[1536,512]{1,0:T(8,128)(2,1)} %get-tuple-element.145.h_ref.refs_0_, bf16[1536,512]{1,0:T(8,128)(2,1)} %get-tuple-element.146.h_ref.refs_1_, bf16[2560,1536]{1,0:T(8,128)(2,1)} %all-gather.8.cloned.1.call-done.w_ref.refs_2_, bf16[2560,1536]{1,0:T(8,128)(2,1)} %all-gather.10.cloned.1.call-done.w_ref.refs_3_), custom_call_target="tpu_custom_call" | custom-call | flops 1 | bytes 1 | tf_op jit(solution)/shard_map/pallas_call | solution.py:296
  608.9 8.7 shard_map.401
  617.7 7.8 collective-permute-done.40
  634.7 9.6 %collective-permute-done.38 = bf16[2,32,1280]{2,1,0:T(8,128)(2,1)S(1)} collective-permute-done((bf16[2,32,1280]{2,1,0:T(8,128)(2,1)S(1)}, bf16[2,32,1280]{2,1,0:T(8,128)(2,1)S(1)}, u32[]{:S(2)}, u32[]{:S(2)}) %collective-permute-start.38) | collective-permute-done | bytes 163872 | tf_op jit(solution)/shard_map/ppermute | solution.py:490
  644.3 19.8 %collective-permute-done.37 = bf16[2,32,1280]{2,1,0:T(8,128)(2,1)S(1)} collective-permute-done((bf16[2,32,1280]{2,1,0:T(8,128)(2,1)S(1)}, bf16[2,32,1280]{2,1,0:T(8,128)(2,1)S(1)}, u32[]{:S(2)}, u32[]{:S(2)}) %collective-permute-start.37) | collective-permute-done | bytes 163872 | tf_op jit(solution)/shard_map/ppermute | solution.py:490
  664.2 8.0 shard_map.402
  677.4 3.1 add_convert_fusion
  684.4 13.8 %collective-permute-start.43 = (bf16[384,1280]{1,0:T(8,128)(2,1)S(1)}, bf16[384,1280]{1,0:T(8,128)(2,1)S(1)}, u32[]{:S(2)}, u32[]{:S(2)}) collective-permute-start(bf16[384,1280]{1,0:T(8,128)(2,1)S(1)} %fusion.55), channel_id=1, source_target_pairs={{0,4},{4,0},{1,5},{5,1},{2,6},{6,2},{3,7},{7,3},{8,12},{12,8},{9,1... | collective-permute-start | bytes 2949128 | tf_op jit(solution)/shard_map/ppermute | solution.py:309
  701.0 17.8 %collective-permute-done.43 = bf16[384,1280]{1,0:T(8,128)(2,1)S(1)} collective-permute-done((bf16[384,1280]{1,0:T(8,128)(2,1)S(1)}, bf16[384,1280]{1,0:T(8,128)(2,1)S(1)}, u32[]{:S(2)}, u32[]{:S(2)}) %collective-permute-start.43) | collective-permute-done | bytes 983072 | tf_op jit(solution)/shard_map/ppermute | solution.py:309
  718.8 6.8 collective-permute-done.46
  727.7 2.7 convolution_convert_fusion
  734.5 2.7 fusion.45
  737.2 7.6 pad_maximum_fusion
  744.8 4.9 fusion.10
  749.8 5.1 fusion.24
  762.2 4.0 pad_maximum_fusion.3
  766.3 13.3 %collective-permute-done.52 = bf16[192,2560]{1,0:T(8,128)(2,1)} collective-permute-done((bf16[192,2560]{1,0:T(8,128)(2,1)}, bf16[192,2560]{1,0:T(8,128)(2,1)}, u32[]{:S(2)}, u32[]{:S(2)}) %collective-permute-start.52) | collective-permute-done | bytes 983072 | tf_op jit(solution)/shard_map/ppermute | solution.py:309
  788.5 6.1 fusion.63
  802.0 7.1 collective-permute-done.60
  809.0 8.2 collective-permute-start.63
  823.7 15.2 %collective-permute-done.48 = bf16[192,2560]{1,0:T(8,128)(2,1)} collective-permute-done((bf16[192,2560]{1,0:T(8,128)(2,1)}, bf16[192,2560]{1,0:T(8,128)(2,1)}, u32[]{:S(2)}, u32[]{:S(2)}) %collective-permute-start.48) | collective-permute-done | bytes 983072 | tf_op jit(solution)/shard_map/ppermute | solution.py:309
  846.0 14.6 %collective-permute-done.62 = bf16[1,2,160,1536]{3,2,1,0:T(8,128)(2,1)} collective-permute-done((bf16[1,2,160,1536]{3,2,1,0:T(8,128)(2,1)}, bf16[1,2,160,1536]{3,2,1,0:T(8,128)(2,1)}, u32[]{:S(2)}, u32[]{:S(2)}) %collective-permute-start.62) | collective-permute-done | bytes 983072 | tf_op jit(solution)/shard_map/ppermute | solution.py:440
  (574 shorter events, 200.8 us)
Async XLA Ops:
  7.2 145.6 %all-gather.6.cloned.1.call-start = ((), (), s32[]{:S(2)}) async-start(), calls=%async_computation.3 | async-start | bytes 20889600 | tf_op jit(solution)/shard_map/all_gather | solution.py:536
  9.8 378.2 %all-gather.8.cloned.1.call-start = ((), (), s32[]{:S(2)}) async-start(), calls=%async_computation.4 | async-start | bytes 9830400 | tf_op jit(solution)/shard_map/all_gather | solution.py:603
  10.7 131.8 %collective-permute-start = (bf16[96,2560]{1,0:T(8,128)(2,1)}, bf16[96,2560]{1,0:T(8,128)(2,1)}, u32[]{:S(2)}, u32[]{:S(2)}) collective-permute-start(bf16[96,2560]{1,0:T(8,128)(2,1)} %bitcast.6), channel_id=1, source_target_pairs={{0,2},{2,4},{4,6},{6,8},{8,10},{10,12},{12,14},{14,16},{16,18},{18... | collective-permute-start | bytes 1474568 | tf_op jit(solution)/shard_map/ppermute | solution.py:534
  20.4 127.5 %collective-permute-start.3 = (bf16[1,1,160,1536]{3,2,0,1:T(8,128)(2,1)}, bf16[1,1,160,1536]{3,2,0,1:T(8,128)(2,1)}, u32[]{:S(2)}, u32[]{:S(2)}) collective-permute-start(bf16[1,1,160,1536]{3,2,0,1:T(8,128)(2,1)} %get-tuple-element.350), channel_id=1, source_target_pairs={{0,6},{2,4},{4,2},{6,0},{1,7},{3,5},{5,3},{7,1},{8,14},{10,12},{12... | collective-permute-start | bytes 1474568 | tf_op jit(solution)/shard_map/ppermute | solution.py:440
  20.4 125.6 %collective-permute-start.2 = (bf16[1,1,160,1536]{3,2,0,1:T(8,128)(2,1)}, bf16[1,1,160,1536]{3,2,0,1:T(8,128)(2,1)}, u32[]{:S(2)}, u32[]{:S(2)}) collective-permute-start(bf16[1,1,160,1536]{3,2,0,1:T(8,128)(2,1)} %get-tuple-element.351), channel_id=1, source_target_pairs={{0,4},{2,6},{4,0},{6,2},{1,5},{3,7},{5,1},{7,3},{8,12},{10,14},{12... | collective-permute-start | bytes 1474568 | tf_op jit(solution)/shard_map/ppermute | solution.py:440
  21.7 122.5 %collective-permute-start.1 = (bf16[1,1,160,1536]{3,2,0,1:T(8,128)(2,1)}, bf16[1,1,160,1536]{3,2,0,1:T(8,128)(2,1)}, u32[]{:S(2)}, u32[]{:S(2)}) collective-permute-start(bf16[1,1,160,1536]{3,2,0,1:T(8,128)(2,1)} %get-tuple-element.352), channel_id=1, source_target_pairs={{0,2},{2,0},{4,6},{6,4},{1,3},{3,1},{5,7},{7,5},{8,10},{10,8},{12,... | collective-permute-start | bytes 1474568 | tf_op jit(solution)/shard_map/ppermute | solution.py:440
  152.9 290.8 %all-gather.10.cloned.1.call-start = ((), (), s32[]{:S(2)}) async-start(), calls=%async_computation.5 | async-start | bytes 9830400 | tf_op jit(solution)/shard_map/all_gather | solution.py:603
  154.1 87.9 %collective-permute-start.15 = (bf16[192,2560]{1,0:T(8,128)(2,1)S(1)}, bf16[192,2560]{1,0:T(8,128)(2,1)}, u32[]{:S(2)}, u32[]{:S(2)}) collective-permute-start(bf16[192,2560]{1,0:T(8,128)(2,1)S(1)} %copy-done.14), channel_id=1, source_target_pairs={{0,4},{4,0},{1,5},{5,1},{2,6},{6,2},{3,7},{7,3},{8,12},{12,8},{9,1... | collective-permute-start | bytes 2949128 | tf_op jit(solution)/shard_map/ppermute | solution.py:309
  157.2 83.7 %collective-permute-start.20 = (bf16[1,1,160,1536]{3,2,0,1:T(8,128)(2,1)S(1)}, bf16[1,1,160,1536]{3,2,0,1:T(8,128)(2,1)S(1)}, u32[]{:S(2)}, u32[]{:S(2)}) collective-permute-start(bf16[1,1,160,1536]{3,2,0,1:T(8,128)(2,1)S(1)} %get-tuple-element.346), channel_id=1, source_target_pairs={{0,6},{2,4},{4,2},{6,0},{1,7},{3,5},{5,3},{7,1},{8,14},{10,12},{12... | collective-permute-start | bytes 1474568 | tf_op jit(solution)/shard_map/ppermute | solution.py:440
  172.4 8.3 collective-permute-start.4
  180.9 10.6 %collective-permute-start.5 = (bf16[2,32,1280]{2,1,0:T(8,128)(2,1)S(1)}, bf16[2,32,1280]{2,1,0:T(8,128)(2,1)S(1)}, u32[]{:S(2)}, u32[]{:S(2)}) collective-permute-start(bf16[2,32,1280]{2,1,0:T(8,128)(2,1)S(1)} %pad_maximum_fusion.22), channel_id=1, source_target_pairs={{0,4},{4,0},{1,5},{5,1},{2,6},{6,2},{3,7},{7,3},{8,12},{12,8},{9,1... | collective-permute-start | bytes 491528 | tf_op jit(solution)/shard_map/ppermute | solution.py:309
  192.3 19.6 %collective-permute-start.7 = (bf16[2,32,1280]{2,1,0:T(8,128)(2,1)S(1)}, bf16[2,32,1280]{2,1,0:T(8,128)(2,1)S(1)}, u32[]{:S(2)}, u32[]{:S(2)}) collective-permute-start(bf16[2,32,1280]{2,1,0:T(8,128)(2,1)S(1)} %pad_maximum_fusion.23), channel_id=1, source_target_pairs={{0,16},{8,24},{1,17},{9,25},{2,18},{10,26},{3,19},{11,27},{4,20},{... | collective-permute-start | bytes 491528 | tf_op jit(solution)/shard_map/ppermute | solution.py:490
  195.5 28.7 %collective-permute-start.6 = (bf16[2,32,1280]{2,1,0:T(8,128)(2,1)S(1)}, bf16[2,32,1280]{2,1,0:T(8,128)(2,1)S(1)}, u32[]{:S(2)}, u32[]{:S(2)}) collective-permute-start(bf16[2,32,1280]{2,1,0:T(8,128)(2,1)S(1)} %pad_maximum_fusion.23), channel_id=1, source_target_pairs={{0,8},{8,16},{16,24},{1,9},{9,17},{17,25},{2,10},{10,18},{18,26},{... | collective-permute-start | bytes 491528 | tf_op jit(solution)/shard_map/ppermute | solution.py:490
  197.4 42.6 %collective-permute-start.19 = (bf16[1,1,160,1536]{3,2,0,1:T(8,128)(2,1)S(1)}, bf16[1,1,160,1536]{3,2,0,1:T(8,128)(2,1)S(1)}, u32[]{:S(2)}, u32[]{:S(2)}) collective-permute-start(bf16[1,1,160,1536]{3,2,0,1:T(8,128)(2,1)S(1)} %get-tuple-element.347), channel_id=1, source_target_pairs={{0,4},{2,6},{4,0},{6,2},{1,5},{3,7},{5,1},{7,3},{8,12},{10,14},{12... | collective-permute-start | bytes 1474568 | tf_op jit(solution)/shard_map/ppermute | solution.py:440
  211.9 27.3 %collective-permute-start.18 = (bf16[1,1,160,1536]{3,2,0,1:T(8,128)(2,1)S(1)}, bf16[1,1,160,1536]{3,2,0,1:T(8,128)(2,1)S(1)}, u32[]{:S(2)}, u32[]{:S(2)}) collective-permute-start(bf16[1,1,160,1536]{3,2,0,1:T(8,128)(2,1)S(1)} %get-tuple-element.348), channel_id=1, source_target_pairs={{0,2},{2,0},{4,6},{6,4},{1,3},{3,1},{5,7},{7,5},{8,10},{10,8},{12,... | collective-permute-start | bytes 1474568 | tf_op jit(solution)/shard_map/ppermute | solution.py:440
  237.0 23.1 %collective-permute-start.9 = (bf16[192,2560]{1,0:T(8,128)(2,1)}, bf16[192,2560]{1,0:T(8,128)(2,1)}, u32[]{:S(2)}, u32[]{:S(2)}) collective-permute-start(bf16[192,2560]{1,0:T(8,128)(2,1)} %fusion.35), channel_id=1, source_target_pairs={{0,1},{1,0},{2,3},{3,2},{4,5},{5,4},{6,7},{7,6},{8,9},{9,8},{10,11... | collective-permute-start | bytes 2949128 | tf_op jit(solution)/shard_map/ppermute | solution.py:309
  241.7 341.5 %reduce-scatter.4.cloned.1.call-start = ((), (), s32[]{:S(2)}) async-start(), calls=%async_computation.6 | async-start | bytes 9830400 | tf_op jit(solution)/shard_map/reduce_scatter | solution.py:429
  242.0 93.9 %collective-permute-start.16 = (bf16[192,2560]{1,0:T(8,128)(2,1)}, bf16[192,2560]{1,0:T(8,128)(2,1)S(1)}, u32[]{:S(2)}, u32[]{:S(2)}) collective-permute-start(bf16[192,2560]{1,0:T(8,128)(2,1)} %collective-permute-done.15), channel_id=1, source_target_pairs={{0,1},{1,0},{2,3},{3,2},{4,5},{5,4},{6,7},{7,6},{8,9},{9,8},{10,11... | collective-permute-start | bytes 2949128 | tf_op jit(solution)/shard_map/ppermute | solution.py:309
  267.2 10.5 %collective-permute-start.10 = (bf16[96,2560]{1,0:T(8,128)(2,1)S(1)}, bf16[96,2560]{1,0:T(8,128)(2,1)S(1)}, u32[]{:S(2)}, u32[]{:S(2)}) collective-permute-start(bf16[96,2560]{1,0:T(8,128)(2,1)S(1)} %get-tuple-element.383), channel_id=1, source_target_pairs={{0,4},{4,0},{1,5},{5,1},{2,6},{6,2},{3,7},{7,3},{8,12},{12,8},{9,1... | collective-permute-start | bytes 1474568 | tf_op jit(solution)/shard_map/ppermute | solution.py:309
  277.7 23.2 %collective-permute-start.11 = (bf16[192,2560]{1,0:T(8,128)(2,1)S(1)}, bf16[192,2560]{1,0:T(8,128)(2,1)S(1)}, u32[]{:S(2)}, u32[]{:S(2)}) collective-permute-start(bf16[192,2560]{1,0:T(8,128)(2,1)S(1)} %pad_maximum_fusion.17), channel_id=1, source_target_pairs={{0,1},{1,0},{2,3},{3,2},{4,5},{5,4},{6,7},{7,6},{8,9},{9,8},{10,11... | collective-permute-start | bytes 2949128 | tf_op jit(solution)/shard_map/ppermute | solution.py:309
  301.1 10.2 %collective-permute-start.12 = (bf16[96,2560]{1,0:T(8,128)(2,1)S(1)}, bf16[96,2560]{1,0:T(8,128)(2,1)S(1)}, u32[]{:S(2)}, u32[]{:S(2)}) collective-permute-start(bf16[96,2560]{1,0:T(8,128)(2,1)S(1)} %get-tuple-element.381), channel_id=1, source_target_pairs={{0,1},{1,0},{2,3},{3,2},{4,5},{5,4},{6,7},{7,6},{8,9},{9,8},{10,11... | collective-permute-start | bytes 1474568 | tf_op jit(solution)/shard_map/ppermute | solution.py:309
  311.4 19.9 %collective-permute-start.13 = (bf16[192,2560]{1,0:T(8,128)(2,1)S(1)}, bf16[192,2560]{1,0:T(8,128)(2,1)S(1)}, u32[]{:S(2)}, u32[]{:S(2)}) collective-permute-start(bf16[192,2560]{1,0:T(8,128)(2,1)S(1)} %pad_maximum_fusion.18), channel_id=1, source_target_pairs={{0,4},{4,0},{1,5},{5,1},{2,6},{6,2},{3,7},{7,3},{8,12},{12,8},{9,1... | collective-permute-start | bytes 2949128 | tf_op jit(solution)/shard_map/ppermute | solution.py:309
  331.5 14.9 %collective-permute-start.14 = (bf16[768,2560]{1,0:T(8,128)(2,1)S(1)}, bf16[768,2560]{1,0:T(8,128)(2,1)S(1)}, u32[]{:S(2)}, u32[]{:S(2)}) collective-permute-start(bf16[768,2560]{1,0:T(8,128)(2,1)S(1)} %get-tuple-element.377), channel_id=1, source_target_pairs={{0,2},{2,0},{1,3},{3,1},{4,6},{6,4},{5,7},{7,5},{8,10},{10,8},{9,1... | collective-permute-start | bytes 11796488 | tf_op jit(solution)/shard_map/ppermute | solution.py:309
  342.5 41.3 %collective-permute-start.17 = (bf16[768,2560]{1,0:T(8,128)(2,1)}, bf16[768,2560]{1,0:T(8,128)(2,1)}, u32[]{:S(2)}, u32[]{:S(2)}) collective-permute-start(bf16[768,2560]{1,0:T(8,128)(2,1)} %get-tuple-element.371), channel_id=1, source_target_pairs={{0,2},{2,0},{1,3},{3,1},{4,6},{6,4},{5,7},{7,5},{8,10},{10,8},{9,1... | collective-permute-start | bytes 11796488 | tf_op jit(solution)/shard_map/ppermute | solution.py:309
  346.7 22.9 %collective-permute-start.24 = (bf16[384,1280]{1,0:T(8,128)(2,1)S(1)}, bf16[384,1280]{1,0:T(8,128)(2,1)S(1)}, u32[]{:S(2)}, u32[]{:S(2)}) collective-permute-start(bf16[384,1280]{1,0:T(8,128)(2,1)S(1)} %copy-done.4), channel_id=1, source_target_pairs={{0,4},{4,0},{1,5},{5,1},{2,6},{6,2},{3,7},{7,3},{8,12},{12,8},{9,1... | collective-permute-start | bytes 2949128 | tf_op jit(solution)/shard_map/ppermute | solution.py:309
  371.1 59.1 %collective-permute-start.25 = (bf16[768,1280]{1,0:T(8,128)(2,1)}, bf16[768,1280]{1,0:T(8,128)(2,1)}, u32[]{:S(2)}, u32[]{:S(2)}) collective-permute-start(bf16[768,1280]{1,0:T(8,128)(2,1)} %pad_maximum_fusion.8), channel_id=1, source_target_pairs={{0,2},{2,0},{1,3},{3,1},{4,6},{6,4},{5,7},{7,5},{8,10},{10,8},{9,1... | collective-permute-start | bytes 5898248 | tf_op jit(solution)/shard_map/ppermute | solution.py:309
  382.0 45.2 %collective-permute-start.23 = (bf16[4,160,384]{2,1,0:T(8,128)(2,1)}, bf16[4,160,384]{2,1,0:T(8,128)(2,1)}, u32[]{:S(2)}, u32[]{:S(2)}) collective-permute-start(bf16[4,160,384]{2,1,0:T(8,128)(2,1)} %get-tuple-element.343), channel_id=1, source_target_pairs={{0,6},{2,4},{4,2},{6,0},{1,7},{3,5},{5,3},{7,1},{8,14},{10,12},{12... | collective-permute-start | bytes 1474568 | tf_op jit(solution)/shard_map/ppermute | solution.py:389
  383.2 43.9 %collective-permute-start.22 = (bf16[4,160,384]{2,1,0:T(8,128)(2,1)}, bf16[4,160,384]{2,1,0:T(8,128)(2,1)}, u32[]{:S(2)}, u32[]{:S(2)}) collective-permute-start(bf16[4,160,384]{2,1,0:T(8,128)(2,1)} %get-tuple-element.344), channel_id=1, source_target_pairs={{0,2},{2,0},{4,6},{6,4},{1,3},{3,1},{5,7},{7,5},{8,10},{10,8},{12,... | collective-permute-start | bytes 1474568 | tf_op jit(solution)/shard_map/ppermute | solution.py:389
  383.8 43.4 %collective-permute-start.21 = (bf16[4,160,384]{2,1,0:T(8,128)(2,1)}, bf16[4,160,384]{2,1,0:T(8,128)(2,1)}, u32[]{:S(2)}, u32[]{:S(2)}) collective-permute-start(bf16[4,160,384]{2,1,0:T(8,128)(2,1)} %get-tuple-element.345), channel_id=1, source_target_pairs={{0,4},{2,6},{4,0},{6,2},{1,5},{3,7},{5,1},{7,3},{8,12},{10,14},{12... | collective-permute-start | bytes 1474568 | tf_op jit(solution)/shard_map/ppermute | solution.py:389
  425.4 319.4 %reduce-scatter.6.cloned.1.call-start = ((), (), s32[]{:S(2)}) async-start(), calls=%async_computation.7 | async-start | bytes 9830400 | tf_op jit(solution)/shard_map/reduce_scatter | solution.py:429
  475.2 13.4 %collective-permute-start.26 = (bf16[768,2560]{1,0:T(8,128)(2,1)}, bf16[768,2560]{1,0:T(8,128)(2,1)S(1)}, u32[]{:S(2)}, u32[]{:S(2)}) collective-permute-start(bf16[768,2560]{1,0:T(8,128)(2,1)} %shard_map.396), channel_id=1, source_target_pairs={{0,2},{2,0},{1,3},{3,1},{4,6},{6,4},{5,7},{7,5},{8,10},{10,8},{9,1... | collective-permute-start | bytes 11796488 | tf_op jit(solution)/shard_map/ppermute | solution.py:309
  492.4 23.5 %collective-permute-start.28 = (bf16[192,2560]{1,0:T(8,128)(2,1)S(1)}, bf16[192,2560]{1,0:T(8,128)(2,1)S(1)}, u32[]{:S(2)}, u32[]{:S(2)}) collective-permute-start(bf16[192,2560]{1,0:T(8,128)(2,1)S(1)} %bitcast.383), channel_id=1, source_target_pairs={{0,1},{1,0},{2,3},{3,2},{4,5},{5,4},{6,7},{7,6},{8,9},{9,8},{10,11... | collective-permute-start | bytes 2949128 | tf_op jit(solution)/shard_map/ppermute | solution.py:309
  495.0 23.4 %collective-permute-start.27 = (bf16[192,2560]{1,0:T(8,128)(2,1)}, bf16[192,2560]{1,0:T(8,128)(2,1)S(1)}, u32[]{:S(2)}, u32[]{:S(2)}) collective-permute-start(bf16[192,2560]{1,0:T(8,128)(2,1)} %bitcast.70), channel_id=1, source_target_pairs={{0,4},{4,0},{1,5},{5,1},{2,6},{6,2},{3,7},{7,3},{8,12},{12,8},{9,1... | collective-permute-start | bytes 2949128 | tf_op jit(solution)/shard_map/ppermute | solution.py:309
  518.8 11.9 %collective-permute-start.29 = (bf16[96,2560]{1,0:T(8,128)(2,1)S(1)}, bf16[96,2560]{1,0:T(8,128)(2,1)S(1)}, u32[]{:S(2)}, u32[]{:S(2)}) collective-permute-start(bf16[96,2560]{1,0:T(8,128)(2,1)S(1)} %slice.762), channel_id=1, source_target_pairs={{0,1},{1,0},{2,3},{3,2},{4,5},{5,4},{6,7},{7,6},{8,9},{9,8},{10,11... | collective-permute-start | bytes 1474568 | tf_op jit(solution)/shard_map/ppermute | solution.py:309
  519.2 11.7 %collective-permute-start.30 = (bf16[96,2560]{1,0:T(8,128)(2,1)S(1)}, bf16[96,2560]{1,0:T(8,128)(2,1)S(1)}, u32[]{:S(2)}, u32[]{:S(2)}) collective-permute-start(bf16[96,2560]{1,0:T(8,128)(2,1)S(1)} %slice.765), channel_id=1, source_target_pairs={{0,4},{4,0},{1,5},{5,1},{2,6},{6,2},{3,7},{7,3},{8,12},{12,8},{9,1... | collective-permute-start | bytes 1474568 | tf_op jit(solution)/shard_map/ppermute | solution.py:309
  533.8 26.8 %collective-permute-start.31 = (bf16[192,2560]{1,0:T(8,128)(2,1)S(1)}, bf16[192,2560]{1,0:T(8,128)(2,1)}, u32[]{:S(2)}, u32[]{:S(2)}) collective-permute-start(bf16[192,2560]{1,0:T(8,128)(2,1)S(1)} %get-tuple-element.270), channel_id=1, source_target_pairs={{0,1},{1,0},{2,3},{3,2},{4,5},{5,4},{6,7},{7,6},{8,9},{9,8},{10,11... | collective-permute-start | bytes 2949128 | tf_op jit(solution)/shard_map/ppermute | solution.py:309
  538.8 12.3 %collective-permute-start.34 = (bf16[4,160,192]{2,1,0:T(8,128)(2,1)}, bf16[4,160,192]{2,1,0:T(8,128)(2,1)S(1)}, u32[]{:S(2)}, u32[]{:S(2)}) collective-permute-start(bf16[4,160,192]{2,1,0:T(8,128)(2,1)} %get-tuple-element.360), channel_id=1, source_target_pairs={{0,6},{2,4},{4,2},{6,0},{1,7},{3,5},{5,3},{7,1},{8,14},{10,12},{12... | collective-permute-start | bytes 737288 | tf_op jit(solution)/shard_map/ppermute | solution.py:389
  542.2 8.9 %collective-permute-start.33 = (bf16[4,160,192]{2,1,0:T(8,128)(2,1)}, bf16[4,160,192]{2,1,0:T(8,128)(2,1)}, u32[]{:S(2)}, u32[]{:S(2)}) collective-permute-start(bf16[4,160,192]{2,1,0:T(8,128)(2,1)} %get-tuple-element.361), channel_id=1, source_target_pairs={{0,2},{2,0},{4,6},{6,4},{1,3},{3,1},{5,7},{7,5},{8,10},{10,8},{12,... | collective-permute-start | bytes 737288 | tf_op jit(solution)/shard_map/ppermute | solution.py:389
  542.2 15.9 %collective-permute-start.32 = (bf16[4,160,192]{2,1,0:T(8,128)(2,1)S(1)}, bf16[4,160,192]{2,1,0:T(8,128)(2,1)}, u32[]{:S(2)}, u32[]{:S(2)}) collective-permute-start(bf16[4,160,192]{2,1,0:T(8,128)(2,1)S(1)} %get-tuple-element.362), channel_id=1, source_target_pairs={{0,4},{2,6},{4,0},{6,2},{1,5},{3,7},{5,1},{7,3},{8,12},{10,14},{12... | collective-permute-start | bytes 737288 | tf_op jit(solution)/shard_map/ppermute | solution.py:389
  583.3 283.4 %reduce-scatter.8.cloned.1.call-start = ((), (), s32[]{:S(2)}) async-start(), calls=%async_computation.8 | async-start | bytes 6553600 | tf_op jit(solution)/shard_map/reduce_scatter | solution.py:413
  585.4 17.1 %collective-permute-start.36 = (bf16[2,32,1280]{2,1,0:T(8,128)(2,1)S(1)}, bf16[2,32,1280]{2,1,0:T(8,128)(2,1)S(1)}, u32[]{:S(2)}, u32[]{:S(2)}) collective-permute-start(bf16[2,32,1280]{2,1,0:T(8,128)(2,1)S(1)} %pad_maximum_fusion.24), channel_id=1, source_target_pairs={{0,4},{4,0},{1,5},{5,1},{2,6},{6,2},{3,7},{7,3},{8,12},{12,8},{9,1... | collective-permute-start | bytes 491528 | tf_op jit(solution)/shard_map/ppermute | solution.py:309
  602.5 23.0 %collective-permute-start.40 = (bf16[384,1280]{1,0:T(8,128)(2,1)S(1)}, bf16[384,1280]{1,0:T(8,128)(2,1)}, u32[]{:S(2)}, u32[]{:S(2)}) collective-permute-start(bf16[384,1280]{1,0:T(8,128)(2,1)S(1)} %get-tuple-element.154), channel_id=1, source_target_pairs={{0,4},{4,0},{1,5},{5,1},{2,6},{6,2},{3,7},{7,3},{8,12},{12,8},{9,1... | collective-permute-start | bytes 2949128 | tf_op jit(solution)/shard_map/ppermute | solution.py:309
  603.6 73.8 %collective-permute-start.45 = (bf16[768,2560]{1,0:T(8,128)(2,1)}, bf16[768,2560]{1,0:T(8,128)(2,1)}, u32[]{:S(2)}, u32[]{:S(2)}) collective-permute-start(bf16[768,2560]{1,0:T(8,128)(2,1)} %shard_map.400), channel_id=1, source_target_pairs={{0,2},{2,0},{1,3},{3,1},{4,6},{6,4},{5,7},{7,5},{8,10},{10,8},{9,1... | collective-permute-start | bytes 11796488 | tf_op jit(solution)/shard_map/ppermute | solution.py:309
  626.8 46.8 %collective-permute-start.41 = (bf16[768,1280]{1,0:T(8,128)(2,1)S(1)}, bf16[768,1280]{1,0:T(8,128)(2,1)S(1)}, u32[]{:S(2)}, u32[]{:S(2)}) collective-permute-start(bf16[768,1280]{1,0:T(8,128)(2,1)S(1)} %pad_maximum_fusion.10), channel_id=1, source_target_pairs={{0,2},{2,0},{1,3},{3,1},{4,6},{6,4},{5,7},{7,5},{8,10},{10,8},{9,1... | collective-permute-start | bytes 5898248 | tf_op jit(solution)/shard_map/ppermute | solution.py:309
  629.2 15.0 %collective-permute-start.38 = (bf16[2,32,1280]{2,1,0:T(8,128)(2,1)S(1)}, bf16[2,32,1280]{2,1,0:T(8,128)(2,1)S(1)}, u32[]{:S(2)}, u32[]{:S(2)}) collective-permute-start(bf16[2,32,1280]{2,1,0:T(8,128)(2,1)S(1)} %pad_maximum_fusion.25), channel_id=1, source_target_pairs={{16,0},{24,8},{17,1},{25,9},{18,2},{26,10},{19,3},{27,11},{20,4},{... | collective-permute-start | bytes 491528 | tf_op jit(solution)/shard_map/ppermute | solution.py:490
  630.5 33.5 %collective-permute-start.37 = (bf16[2,32,1280]{2,1,0:T(8,128)(2,1)S(1)}, bf16[2,32,1280]{2,1,0:T(8,128)(2,1)S(1)}, u32[]{:S(2)}, u32[]{:S(2)}) collective-permute-start(bf16[2,32,1280]{2,1,0:T(8,128)(2,1)S(1)} %pad_maximum_fusion.25), channel_id=1, source_target_pairs={{8,0},{16,8},{24,16},{9,1},{17,9},{25,17},{10,2},{18,10},{26,18},{... | collective-permute-start | bytes 491528 | tf_op jit(solution)/shard_map/ppermute | solution.py:490
  633.3 67.7 %collective-permute-start.44 = (bf16[640,768]{1,0:T(8,128)(2,1)S(1)}, bf16[640,768]{1,0:T(8,128)(2,1)}, u32[]{:S(2)}, u32[]{:S(2)}) collective-permute-start(bf16[640,768]{1,0:T(8,128)(2,1)S(1)} %copy-done.43), channel_id=1, source_target_pairs={{0,1},{1,0},{2,3},{3,2},{4,5},{5,4},{6,7},{7,6},{8,9},{9,8},{10,11... | collective-permute-start | bytes 2949128 | tf_op jit(solution)/shard_map/ppermute | solution.py:309
  673.2 25.0 %collective-permute-start.50 = (bf16[4,2,32,1280]{3,2,0,1:T(8,128)(2,1)}, bf16[4,2,32,1280]{3,2,0,1:T(8,128)(2,1)}, u32[]{:S(2)}, u32[]{:S(2)}) collective-permute-start(bf16[4,2,32,1280]{3,2,0,1:T(8,128)(2,1)} %bitcast.341), channel_id=1, source_target_pairs={{0,2},{2,0},{1,3},{3,1},{4,6},{6,4},{5,7},{7,5},{8,10},{10,8},{9,1... | collective-permute-start | bytes 1966088 | tf_op jit(solution)/shard_map/ppermute | solution.py:309
  675.3 8.6 collective-permute-start.42
  681.0 44.6 %collective-permute-start.46 = (bf16[384,2560]{1,0:T(8,128)(2,1)S(1)}, bf16[384,2560]{1,0:T(8,128)(2,1)S(1)}, u32[]{:S(2)}, u32[]{:S(2)}) collective-permute-start(bf16[384,2560]{1,0:T(8,128)(2,1)S(1)} %pad_maximum_fusion.12), channel_id=1, source_target_pairs={{0,1},{1,0},{2,3},{3,2},{4,5},{5,4},{6,7},{7,6},{8,9},{9,8},{10,11... | collective-permute-start | bytes 5898248 | tf_op jit(solution)/shard_map/ppermute | solution.py:309
  684.4 34.4 %collective-permute-start.43 = (bf16[384,1280]{1,0:T(8,128)(2,1)S(1)}, bf16[384,1280]{1,0:T(8,128)(2,1)S(1)}, u32[]{:S(2)}, u32[]{:S(2)}) collective-permute-start(bf16[384,1280]{1,0:T(8,128)(2,1)S(1)} %fusion.55), channel_id=1, source_target_pairs={{0,4},{4,0},{1,5},{5,1},{2,6},{6,2},{3,7},{7,3},{8,12},{12,8},{9,1... | collective-permute-start | bytes 2949128 | tf_op jit(solution)/shard_map/ppermute | solution.py:309
  699.5 28.1 %collective-permute-start.51 = (bf16[4,32,1280]{2,1,0:T(8,128)(2,1)S(1)}, bf16[4,32,1280]{2,1,0:T(8,128)(2,1)S(1)}, u32[]{:S(2)}, u32[]{:S(2)}) collective-permute-start(bf16[4,32,1280]{2,1,0:T(8,128)(2,1)S(1)} %dynamic-slice_bitcast_fusion.6), channel_id=1, source_target_pairs={{0,4},{4,0},{1,5},{5,1},{2,6},{6,2},{3,7},{7,3},{8,12},{12,8},{9,1... | collective-permute-start | bytes 983048 | tf_op jit(solution)/shard_map/ppermute | solution.py:309
  756.0 23.7 %collective-permute-start.52 = (bf16[192,2560]{1,0:T(8,128)(2,1)}, bf16[192,2560]{1,0:T(8,128)(2,1)}, u32[]{:S(2)}, u32[]{:S(2)}) collective-permute-start(bf16[192,2560]{1,0:T(8,128)(2,1)} %dynamic-slice_convert_fusion), channel_id=1, source_target_pairs={{0,1},{1,0},{2,3},{3,2},{4,5},{5,4},{6,7},{7,6},{8,9},{9,8},{10,11... | collective-permute-start | bytes 2949128 | tf_op jit(solution)/shard_map/ppermute | solution.py:309
  760.7 27.8 %collective-permute-start.47 = (bf16[192,2560]{1,0:T(8,128)(2,1)}, bf16[192,2560]{1,0:T(8,128)(2,1)}, u32[]{:S(2)}, u32[]{:S(2)}) collective-permute-start(bf16[192,2560]{1,0:T(8,128)(2,1)} %slice.799), channel_id=1, source_target_pairs={{0,4},{4,0},{1,5},{5,1},{2,6},{6,2},{3,7},{7,3},{8,12},{12,8},{9,1... | collective-permute-start | bytes 2949128 | tf_op jit(solution)/shard_map/ppermute | solution.py:309
  785.5 10.6 %collective-permute-start.57 = (f32[24,1280]{1,0:T(8,128)S(1)}, f32[24,1280]{1,0:T(8,128)S(1)}, u32[]{:S(2)}, u32[]{:S(2)}) collective-permute-start(f32[24,1280]{1,0:T(8,128)S(1)} %concatenate.237), channel_id=1, source_target_pairs={{0,6},{2,4},{4,2},{6,0},{1,7},{3,5},{5,3},{7,1},{8,14},{10,12},{12... | collective-permute-start | bytes 368648 | tf_op jit(solution)/shard_map/ppermute | solution.py:420
  787.5 8.6 collective-permute-start.56
  794.6 27.4 %collective-permute-start.53 = (bf16[192,2560]{1,0:T(8,128)(2,1)}, bf16[192,2560]{1,0:T(8,128)(2,1)}, u32[]{:S(2)}, u32[]{:S(2)}) collective-permute-start(bf16[192,2560]{1,0:T(8,128)(2,1)} %get-tuple-element.332), channel_id=1, source_target_pairs={{0,1},{1,0},{2,3},{3,2},{4,5},{5,4},{6,7},{7,6},{8,9},{9,8},{10,11... | collective-permute-start | bytes 2949128 | tf_op jit(solution)/shard_map/ppermute | solution.py:309
  796.0 42.8 %collective-permute-start.48 = (bf16[192,2560]{1,0:T(8,128)(2,1)}, bf16[192,2560]{1,0:T(8,128)(2,1)}, u32[]{:S(2)}, u32[]{:S(2)}) collective-permute-start(bf16[192,2560]{1,0:T(8,128)(2,1)} %get-tuple-element.333), channel_id=1, source_target_pairs={{0,1},{1,0},{2,3},{3,2},{4,5},{5,4},{6,7},{7,6},{8,9},{9,8},{10,11... | collective-permute-start | bytes 2949128 | tf_op jit(solution)/shard_map/ppermute | solution.py:309
  796.2 12.9 %collective-permute-start.60 = (f32[24,1280]{1,0:T(8,128)S(1)}, f32[24,1280]{1,0:T(8,128)S(1)}, u32[]{:S(2)}, u32[]{:S(2)}) collective-permute-start(f32[24,1280]{1,0:T(8,128)S(1)} %add_add_fusion.2), channel_id=1, source_target_pairs={{0,24},{8,0},{16,8},{24,16},{1,25},{9,1},{17,9},{25,17},{2,26},{10... | collective-permute-start | bytes 368648 | tf_op jit(solution)/shard_map/ppermute | solution.py:425
  796.2 21.0 %collective-permute-start.59 = (f32[24,1280]{1,0:T(8,128)S(1)}, f32[24,1280]{1,0:T(8,128)S(1)}, u32[]{:S(2)}, u32[]{:S(2)}) collective-permute-start(f32[24,1280]{1,0:T(8,128)S(1)} %add_add_fusion.2), channel_id=1, source_target_pairs={{0,16},{8,24},{16,0},{24,8},{1,17},{9,25},{17,1},{25,9},{2,18},{10... | collective-permute-start | bytes 368648 | tf_op jit(solution)/shard_map/ppermute | solution.py:425
  796.7 20.6 %collective-permute-start.58 = (f32[24,1280]{1,0:T(8,128)S(1)}, f32[24,1280]{1,0:T(8,128)S(1)}, u32[]{:S(2)}, u32[]{:S(2)}) collective-permute-start(f32[24,1280]{1,0:T(8,128)S(1)} %add_add_fusion.2), channel_id=1, source_target_pairs={{0,8},{8,16},{16,24},{24,0},{1,9},{9,17},{17,25},{25,1},{2,10},{10... | collective-permute-start | bytes 368648 | tf_op jit(solution)/shard_map/ppermute | solution.py:425
  809.0 52.9 %collective-permute-start.63 = (bf16[1,2,160,1536]{3,2,1,0:T(8,128)(2,1)S(1)}, bf16[1,2,160,1536]{3,2,1,0:T(8,128)(2,1)S(1)}, u32[]{:S(2)}, u32[]{:S(2)}) collective-permute-start(bf16[1,2,160,1536]{3,2,1,0:T(8,128)(2,1)S(1)} %get-tuple-element.295), channel_id=1, source_target_pairs={{0,6},{2,4},{4,2},{6,0},{1,7},{3,5},{5,3},{7,1},{8,14},{10,12},{12... | collective-permute-start | bytes 2949128 | tf_op jit(solution)/shard_map/ppermute | solution.py:440
  817.2 43.4 %collective-permute-start.62 = (bf16[1,2,160,1536]{3,2,1,0:T(8,128)(2,1)}, bf16[1,2,160,1536]{3,2,1,0:T(8,128)(2,1)}, u32[]{:S(2)}, u32[]{:S(2)}) collective-permute-start(bf16[1,2,160,1536]{3,2,1,0:T(8,128)(2,1)} %get-tuple-element.296), channel_id=1, source_target_pairs={{0,4},{2,6},{4,0},{6,2},{1,5},{3,7},{5,1},{7,3},{8,12},{10,14},{12... | collective-permute-start | bytes 2949128 | tf_op jit(solution)/shard_map/ppermute | solution.py:440
  817.4 25.9 %collective-permute-start.61 = (bf16[1,2,160,1536]{3,2,1,0:T(8,128)(2,1)}, bf16[1,2,160,1536]{3,2,1,0:T(8,128)(2,1)}, u32[]{:S(2)}, u32[]{:S(2)}) collective-permute-start(bf16[1,2,160,1536]{3,2,1,0:T(8,128)(2,1)} %get-tuple-element.297), channel_id=1, source_target_pairs={{0,2},{2,0},{4,6},{6,4},{1,3},{3,1},{5,7},{7,5},{8,10},{10,8},{12,... | collective-permute-start | bytes 2949128 | tf_op jit(solution)/shard_map/ppermute | solution.py:440
  (110 other events, 1137.8 us)
Sparse Core Ops, SparseCore 0:
  10.2 129.7 all-gather.5
  153.0 148.6 all-gather.7
  303.3 140.3 all-gather.9
  445.8 137.3 reduce-scatter.3
  585.3 151.6 reduce-scatter.5
  761.3 102.8 reduce-scatter.7

commit v4 on v3

--- a/solution.py
+++ b/solution.py
@@ -698,10 +698,11 @@
                    .reshape(-1, channels) for j in (side, 1 - side)]
     grad_output = dot(dealt_own, mixed_sides[0]) + dot(dealt_other, mixed_sides[1])
     grad_branch = dot(normed_dealt, branch_group)
-    packed = [by_plane(grad_output), by_plane(grad_branch)]
+    packed = [by_plane(grad_output), by_plane(grad_branch), jnp.zeros((PLANES, part, channels), BF16), gates_b]
+    recur_near, packed = tie(recur_near, jnp.concatenate(packed, axis=1))
     recur_near = jnp.concatenate([d_recur, recur_near], axis=0) if mid == 2 else recur_near
-    packed += [by_plane(dot(normed_dealt, gather_rows(recur_near, "c"))), gates_b]
-    packed = jnp.concatenate(packed, axis=1)
+    grad_recur = by_plane(dot(normed_dealt, gather_rows(recur_near, "c")))
+    packed = lax.dynamic_update_slice_in_dim(packed, grad_recur, 2 * part, 1)
     packed, d_recur, *ffn_grads = tie(packed, d_recur, *ffn_grads)
     sums = fold_planes(packed)
     d_normed = dot(d_branch, branch_full, ((1,), (1,))) + dot(d_recur, recur_full, ((1,), (1,)))

time: 887 us -> 887 us (level)
  waiting for transfers between devices: 292 us -> 301 us
    unnamed x253 -> x229, local copies, waits for them, and re-layouts: 35.6 us -> 33.1 us
  transfers between devices with their start and end apart: 70 -> 70, of which waited for: 27 -> 27; matrix products, arithmetic and copies ran while one was open for 23% -> 22% of each run, Pallas kernels for 16% -> 16%
where the time goes in v4:
time: 887 us; the launch traced here: 879 us
  waiting for transfers between devices  301 us (34%)
  Pallas kernels  143 us (16%)
  blocking collectives  101 us (11%)
  local copies, waits for them, and re-layouts  97.6 us (11%)
  starting transfers between devices  86.4 us (10%)
  other arithmetic  75.1 us (8%)
  matrix products  57.6 us (6%)
  between operations  17.7 us (2%)
    ppermute x35, waiting for transfers between devices, swap(): return lax.ppermute(v, axis, [(0, 1), (1, 0)])  183 us
    dot_general x11, matrix products, dot(): return lax.dot_general(a, b, (dims, ((), ())), preferred_element_type=F32)  57.6 us
    ppermute x6, waiting for transfers between devices, carry_planes(): lax.ppermute(sent if far < PLANES - 1 else sent[:1], 'z', route)  57.3 us
    all_gather x1, blocking collectives, body(): every = lax.all_gather(flat, DP, axis=0, tiled=False).astype(F32)  54.8 us
    ppermute x35, starting transfers between devices, swap(): return lax.ppermute(v, axis, [(0, 1), (1, 0)])  44.4 us
    pallas_call x4, Pallas kernels, feed_back(): pl.pallas_call(back_kernel, grid=(width // tile,), in_specs=[pl.BlockSpec...  43.1 us
    pallas_call x2, Pallas kernels, feed(): pl.pallas_call(functools.partial(feed_kernel, first_unit=first_unit), gri...  37.9 us
    pallas_call x2, Pallas kernels, feed_grads(): pl.pallas_call(grad_kernel, grid=(width // tile,), in_specs=[pl.BlockSpec...  37.1 us
  transfers between devices with their start and end apart: 70, of which 27 were waited for; matrix products, arithmetic and copies ran while one was open for 22% of the time, Pallas kernels for 16%

profile of v4, /device:TPU:9, one launch (start us, length us, event | category | flops | bytes accessed | tf_op | source)
XLA Modules:
  0.0 879.4 jit_solution(16992358531867383211)
XLA Ops:
  10.7 3.7 collective-permute-start
  24.2 54.8 %all-gather.1 = bf16[16,1,1920]{2,1,0:T(2,128)(2,1)S(1)} all-gather(bf16[1,1,1920]{2,1,0:T(2,128)(2,1)S(1)} %reshape.697), channel_id=2, replica_groups=mesh['z'=4,'x'=2,'c'=2,'y'=2] {'z','x','c'}, dimensions={0}, use_global_device_ids=true | all-gather | bytes 65280 | tf_op jit(solution)/shard_map/all_gather | solution.py:542
  87.7 22.1 %all_gather.25.wd_ref = bf16[256,1280]{1,0:T(8,128)(2,1)S(1)} all-gather(bf16[16,1280]{1,0:T(8,128)(2,1)S(1)} %bitcast.395), channel_id=1, replica_groups=mesh['z'=4,'x'=2,'c'=2,'y'=2] {'z','x','c'}, dimensions={0}, use_global_device_ids=true | all-gather | bytes 696320 | tf_op jit(solution)/shard_map/all_gather | solution.py:538
  109.8 24.3 %all_gather.24.wi_ref = bf16[256,1280]{1,0:T(8,128)(2,1)S(1)} all-gather(bf16[16,1280]{1,0:T(8,128)(2,1)S(1)} %bitcast.394), channel_id=1, replica_groups=mesh['z'=4,'x'=2,'c'=2,'y'=2] {'z','x','c'}, dimensions={0}, use_global_device_ids=true | all-gather | bytes 696320 | tf_op jit(solution)/shard_map/all_gather | solution.py:537
  149.5 3.1 fusion.23
  158.0 8.2 fusion.41.r_ref
  166.2 5.7 shard_map.391
  172.1 8.2 fusion.48.b_ref
  180.9 10.3 %collective-permute-done.5 = bf16[2,32,1280]{2,1,0:T(8,128)(2,1)S(1)} collective-permute-done((bf16[2,32,1280]{2,1,0:T(8,128)(2,1)S(1)}, bf16[2,32,1280]{2,1,0:T(8,128)(2,1)S(1)}, u32[]{:S(2)}, u32[]{:S(2)}) %collective-permute-start.5) | collective-permute-done | bytes 163872 | tf_op jit(solution)/shard_map/ppermute | solution.py:309
  197.3 14.6 %collective-permute-done.7 = bf16[2,32,1280]{2,1,0:T(8,128)(2,1)S(1)} collective-permute-done((bf16[2,32,1280]{2,1,0:T(8,128)(2,1)S(1)}, bf16[2,32,1280]{2,1,0:T(8,128)(2,1)S(1)}, u32[]{:S(2)}, u32[]{:S(2)}) %collective-permute-start.7) | collective-permute-done | bytes 163872 | tf_op jit(solution)/shard_map/ppermute | solution.py:490
  212.3 11.9 %collective-permute-done.6 = bf16[2,32,1280]{2,1,0:T(8,128)(2,1)S(1)} collective-permute-done((bf16[2,32,1280]{2,1,0:T(8,128)(2,1)S(1)}, bf16[2,32,1280]{2,1,0:T(8,128)(2,1)S(1)}, u32[]{:S(2)}, u32[]{:S(2)}) %collective-permute-start.6) | collective-permute-done | bytes 163872 | tf_op jit(solution)/shard_map/ppermute | solution.py:490
  224.3 5.5 shard_map.392
  229.9 7.2 fusion.35
  242.4 17.9 %collective-permute-done.9 = bf16[192,2560]{1,0:T(8,128)(2,1)} collective-permute-done((bf16[192,2560]{1,0:T(8,128)(2,1)}, bf16[192,2560]{1,0:T(8,128)(2,1)}, u32[]{:S(2)}, u32[]{:S(2)}) %collective-permute-start.9) | collective-permute-done | bytes 983072 | tf_op jit(solution)/shard_map/ppermute | solution.py:309
  260.3 5.8 multiply_reduce_fusion.2
  270.2 7.9 collective-permute-done.10
  280.5 20.4 %collective-permute-done.11 = bf16[192,2560]{1,0:T(8,128)(2,1)S(1)} collective-permute-done((bf16[192,2560]{1,0:T(8,128)(2,1)S(1)}, bf16[192,2560]{1,0:T(8,128)(2,1)S(1)}, u32[]{:S(2)}, u32[]{:S(2)}) %collective-permute-start.11) | collective-permute-done | bytes 983072 | tf_op jit(solution)/shard_map/ppermute | solution.py:309
  302.6 8.5 collective-permute-done.12
  313.0 18.3 %collective-permute-done.13 = bf16[192,2560]{1,0:T(8,128)(2,1)S(1)} collective-permute-done((bf16[192,2560]{1,0:T(8,128)(2,1)S(1)}, bf16[192,2560]{1,0:T(8,128)(2,1)S(1)}, u32[]{:S(2)}, u32[]{:S(2)}) %collective-permute-start.13) | collective-permute-done | bytes 983072 | tf_op jit(solution)/shard_map/ppermute | solution.py:309
  331.5 4.3 collective-permute-start.14
  349.8 19.3 %collective-permute-done.24 = bf16[384,1280]{1,0:T(8,128)(2,1)S(1)} collective-permute-done((bf16[384,1280]{1,0:T(8,128)(2,1)S(1)}, bf16[384,1280]{1,0:T(8,128)(2,1)S(1)}, u32[]{:S(2)}, u32[]{:S(2)}) %collective-permute-start.24) | collective-permute-done | bytes 983072 | tf_op jit(solution)/shard_map/ppermute | solution.py:309
  374.6 4.0 copy.133
  378.6 2.8 constant_dynamic-slice_fusion.15
  383.3 4.3 constant_dynamic-update-slice_fusion.13.d_ref
  387.6 19.0 %shard_map.393 = (bf16[1536,512]{1,0:T(8,128)(2,1)}, bf16[1536,1024]{1,0:T(8,128)(2,1)}) custom-call(s32[1]{0:T(128)S(6)} %mul.368.at_ref, bf16[1536,2560]{1,0:T(8,128)(2,1)} %copy-done.10, bf16[1536,2560]{1,0:T(8,128)(2,1)} %constant_dynamic-update-slice_fusion.13.d_ref, bf16[2560,1536]{1,0:T(8,128)(2,1)} %all-gather.8.cloned.1.call-done.w_ref.refs_2_, ...), custom_call_target="tpu_custom_call" | custom-call | flops 1 | bytes 1 | tf_op jit(solution)/shard_map/pallas_call | solution.py:228
  406.5 18.3 %shard_map.394 = (bf16[2560,1536]{1,0:T(8,128)(2,1)}, f32[8,1024]{1,0:T(8,128)}) custom-call(bf16[1536,2560]{1,0:T(8,128)(2,1)} %copy-done.10, bf16[1536,2560]{1,0:T(8,128)(2,1)} %constant_dynamic-update-slice_fusion.13.d_ref, bf16[1536,1024]{1,0:T(8,128)(2,1)} %get-tuple-element.122.g_ref.refs_0_, bf16[1536,512]{1,0:T(8,128)(2,1)} %get-tuple-element.147.h_ref.refs_0_), custom_call_target="tpu_custom_call" | custom-call | flops 1 | bytes 1 | tf_op jit(solution)/shard_map/pallas_call | solution.py:267
  425.7 3.1 pad_maximum_fusion.7
  428.8 3.4 pad_maximum_fusion.1
  432.2 11.5 %all-gather.10.cloned.1.call-done.w_ref.refs_3_ = bf16[2560,1536]{1,0:T(8,128)(2,1)} async-done(((bf16[640,1536]{1,0:T(8,128)(2,1)}), bf16[2560,1536]{1,0:T(8,128)(2,1)}) %all-gather.10.cloned.1.call-update) | async-done | bytes 7864336 | tf_op jit(solution)/shard_map/all_gather | solution.py:603
  443.7 19.0 %shard_map.395 = (bf16[1536,512]{1,0:T(8,128)(2,1)}, bf16[1536,1024]{1,0:T(8,128)(2,1)}) custom-call(s32[1]{0:T(128)S(6)} %mul.368.at_ref, bf16[1536,2560]{1,0:T(8,128)(2,1)} %copy-done.10, bf16[1536,2560]{1,0:T(8,128)(2,1)} %constant_dynamic-update-slice_fusion.13.d_ref, bf16[2560,1536]{1,0:T(8,128)(2,1)} %all-gather.10.cloned.1.call-done.w_ref.refs_3_, ...), custom_call_target="tpu_custom_call" | custom-call | flops 1 | bytes 1 | tf_op jit(solution)/shard_map/pallas_call | solution.py:228
  462.6 12.6 %shard_map.396 = bf16[768,2560]{1,0:T(8,128)(2,1)} custom-call(bf16[1536,1024]{1,0:T(8,128)(2,1)} %get-tuple-element.122.g_ref.refs_0_, bf16[1536,1024]{1,0:T(8,128)(2,1)} %get-tuple-element.129.refs_1_.g_ref, bf16[2560,1536]{1,0:T(8,128)(2,1)} %all-gather.8.cloned.1.call-done.w_ref.refs_2_, bf16[2560,1536]{1,0:T(8,128)(2,1)} %all-gather.10.cloned.1.call-done.w_ref.refs_3_), custom_call_target="tpu_custom_call" | custom-call | flops 1 | bytes 1 | tf_op jit(solution)/shard_map/pallas_call | solution.py:296
  475.8 12.8 %shard_map.397 = bf16[768,2560]{1,0:T(8,128)(2,1)} custom-call(bf16[1536,1024]{1,0:T(8,128)(2,1)} %get-tuple-element.122.g_ref.refs_0_, bf16[1536,1024]{1,0:T(8,128)(2,1)} %get-tuple-element.129.refs_1_.g_ref, bf16[2560,1536]{1,0:T(8,128)(2,1)} %all-gather.8.cloned.1.call-done.w_ref.refs_2_, bf16[2560,1536]{1,0:T(8,128)(2,1)} %all-gather.10.cloned.1.call-done.w_ref.refs_3_), custom_call_target="tpu_custom_call" | custom-call | flops 1 | bytes 1 | tf_op jit(solution)/shard_map/pallas_call | solution.py:296
  488.6 3.1 add_convert_fusion.1
  496.3 18.7 %shard_map.398 = (bf16[2560,1536]{1,0:T(8,128)(2,1)}, f32[8,1024]{1,0:T(8,128)}) custom-call(bf16[1536,2560]{1,0:T(8,128)(2,1)} %copy-done.10, bf16[1536,2560]{1,0:T(8,128)(2,1)} %constant_dynamic-update-slice_fusion.13.d_ref, bf16[1536,1024]{1,0:T(8,128)(2,1)} %get-tuple-element.129.refs_1_.g_ref, bf16[1536,512]{1,0:T(8,128)(2,1)} %get-tuple-element.148.h_ref.refs_1_), custom_call_target="tpu_custom_call" | custom-call | flops 1 | bytes 1 | tf_op jit(solution)/shard_map/pallas_call | solution.py:267
  520.8 10.0 %collective-permute-done.29 = bf16[96,2560]{1,0:T(8,128)(2,1)S(1)} collective-permute-done((bf16[96,2560]{1,0:T(8,128)(2,1)S(1)}, bf16[96,2560]{1,0:T(8,128)(2,1)S(1)}, u32[]{:S(2)}, u32[]{:S(2)}) %collective-permute-start.29) | collective-permute-done | bytes 491552 | tf_op jit(solution)/shard_map/ppermute | solution.py:309
  538.5 3.4 collective-permute-start.34
  542.3 8.6 collective-permute-done.34
  550.8 7.0 collective-permute-done.32
  561.6 5.6 fusion.dm_ref
  567.2 5.2 shard_map.399
  573.6 9.6 %reduce-scatter.4.cloned.1.call-done = bf16[640,1536]{1,0:T(8,128)(2,1)} async-done(((bf16[2560,1536]{1,0:T(8,128)(2,1)}), bf16[640,1536]{1,0:T(8,128)(2,1)}) %reduce-scatter.4.cloned.1.call-update) | async-done | bytes 1966096 | tf_op jit(solution)/shard_map/reduce_scatter | solution.py:429
  586.6 8.9 %shard_map.401 = bf16[768,2560]{1,0:T(8,128)(2,1)} custom-call(bf16[1536,512]{1,0:T(8,128)(2,1)} %get-tuple-element.147.h_ref.refs_0_, bf16[1536,512]{1,0:T(8,128)(2,1)} %get-tuple-element.148.h_ref.refs_1_, bf16[2560,1536]{1,0:T(8,128)(2,1)} %all-gather.8.cloned.1.call-done.w_ref.refs_2_, bf16[2560,1536]{1,0:T(8,128)(2,1)} %all-gather.10.cloned.1.call-done.w_ref.refs_3_), custom_call_target="tpu_custom_call" | custom-call | flops 1 | bytes 1 | tf_op jit(solution)/shard_map/pallas_call | solution.py:296
  595.6 8.7 shard_map.400
  607.7 2.8 collective-permute-start.37
  610.6 11.0 %collective-permute-done.38 = bf16[2,32,1280]{2,1,0:T(8,128)(2,1)S(1)} collective-permute-done((bf16[2,32,1280]{2,1,0:T(8,128)(2,1)S(1)}, bf16[2,32,1280]{2,1,0:T(8,128)(2,1)S(1)}, u32[]{:S(2)}, u32[]{:S(2)}) %collective-permute-start.38) | collective-permute-done | bytes 163872 | tf_op jit(solution)/shard_map/ppermute | solution.py:490
  621.5 19.8 %collective-permute-done.37 = bf16[2,32,1280]{2,1,0:T(8,128)(2,1)S(1)} collective-permute-done((bf16[2,32,1280]{2,1,0:T(8,128)(2,1)S(1)}, bf16[2,32,1280]{2,1,0:T(8,128)(2,1)S(1)}, u32[]{:S(2)}, u32[]{:S(2)}) %collective-permute-start.37) | collective-permute-done | bytes 163872 | tf_op jit(solution)/shard_map/ppermute | solution.py:490
  643.6 8.1 shard_map.402
  660.6 3.2 collective-permute-start.42
  663.8 3.1 add_convert_fusion
  670.5 10.7 %collective-permute-start.43 = (bf16[384,1280]{1,0:T(8,128)(2,1)S(1)}, bf16[384,1280]{1,0:T(8,128)(2,1)S(1)}, u32[]{:S(2)}, u32[]{:S(2)}) collective-permute-start(bf16[384,1280]{1,0:T(8,128)(2,1)S(1)} %fusion.55), channel_id=1, source_target_pairs={{0,4},{4,0},{1,5},{5,1},{2,6},{6,2},{3,7},{7,3},{8,12},{12,8},{9,1... | collective-permute-start | bytes 2949128 | tf_op jit(solution)/shard_map/ppermute | solution.py:309
  685.3 17.6 %collective-permute-done.43 = bf16[384,1280]{1,0:T(8,128)(2,1)S(1)} collective-permute-done((bf16[384,1280]{1,0:T(8,128)(2,1)S(1)}, bf16[384,1280]{1,0:T(8,128)(2,1)S(1)}, u32[]{:S(2)}, u32[]{:S(2)}) %collective-permute-start.43) | collective-permute-done | bytes 983072 | tf_op jit(solution)/shard_map/ppermute | solution.py:309
  702.9 15.8 %collective-permute-done.46 = bf16[384,2560]{1,0:T(8,128)(2,1)S(1)} collective-permute-done((bf16[384,2560]{1,0:T(8,128)(2,1)S(1)}, bf16[384,2560]{1,0:T(8,128)(2,1)S(1)}, u32[]{:S(2)}, u32[]{:S(2)}) %collective-permute-start.46) | collective-permute-done | bytes 1966112 | tf_op jit(solution)/shard_map/ppermute | solution.py:309
  718.7 3.4 fusion.152
  723.6 6.4 pad_maximum_fusion
  738.5 5.1 fusion.45
  744.9 4.9 fusion.10
  749.9 5.1 fusion.24
  762.3 4.1 pad_maximum_fusion.3
  766.4 13.3 %collective-permute-done.52 = bf16[192,2560]{1,0:T(8,128)(2,1)} collective-permute-done((bf16[192,2560]{1,0:T(8,128)(2,1)}, bf16[192,2560]{1,0:T(8,128)(2,1)}, u32[]{:S(2)}, u32[]{:S(2)}) %collective-permute-start.52) | collective-permute-done | bytes 983072 | tf_op jit(solution)/shard_map/ppermute | solution.py:309
  788.8 6.2 fusion.63
  801.8 8.0 collective-permute-done.60
  809.8 7.8 collective-permute-start.63
  823.3 16.2 %collective-permute-done.48 = bf16[192,2560]{1,0:T(8,128)(2,1)} collective-permute-done((bf16[192,2560]{1,0:T(8,128)(2,1)}, bf16[192,2560]{1,0:T(8,128)(2,1)}, u32[]{:S(2)}, u32[]{:S(2)}) %collective-permute-start.48) | collective-permute-done | bytes 983072 | tf_op jit(solution)/shard_map/ppermute | solution.py:309
  846.6 14.5 %collective-permute-done.62 = bf16[1,2,160,1536]{3,2,1,0:T(8,128)(2,1)} collective-permute-done((bf16[1,2,160,1536]{3,2,1,0:T(8,128)(2,1)S(1)}, bf16[1,2,160,1536]{3,2,1,0:T(8,128)(2,1)}, u32[]{:S(2)}, u32[]{:S(2)}) %collective-permute-start.62) | collective-permute-done | bytes 983072 | tf_op jit(solution)/shard_map/ppermute | solution.py:440
  (553 shorter events, 193.0 us)
Async XLA Ops:
  7.2 145.4 %all-gather.6.cloned.1.call-start = ((), (), s32[]{:S(2)}) async-start(), calls=%async_computation.3 | async-start | bytes 20889600 | tf_op jit(solution)/shard_map/all_gather | solution.py:536
  9.8 377.7 %all-gather.8.cloned.1.call-start = ((), (), s32[]{:S(2)}) async-start(), calls=%async_computation.4 | async-start | bytes 9830400 | tf_op jit(solution)/shard_map/all_gather | solution.py:603
  10.7 131.6 %collective-permute-start = (bf16[96,2560]{1,0:T(8,128)(2,1)}, bf16[96,2560]{1,0:T(8,128)(2,1)}, u32[]{:S(2)}, u32[]{:S(2)}) collective-permute-start(bf16[96,2560]{1,0:T(8,128)(2,1)} %bitcast.6), channel_id=1, source_target_pairs={{0,2},{2,4},{4,6},{6,8},{8,10},{10,12},{12,14},{14,16},{16,18},{18... | collective-permute-start | bytes 1474568 | tf_op jit(solution)/shard_map/ppermute | solution.py:534
  20.4 127.2 %collective-permute-start.3 = (bf16[1,1,160,1536]{3,2,0,1:T(8,128)(2,1)}, bf16[1,1,160,1536]{3,2,0,1:T(8,128)(2,1)}, u32[]{:S(2)}, u32[]{:S(2)}) collective-permute-start(bf16[1,1,160,1536]{3,2,0,1:T(8,128)(2,1)} %get-tuple-element.354), channel_id=1, source_target_pairs={{0,6},{2,4},{4,2},{6,0},{1,7},{3,5},{5,3},{7,1},{8,14},{10,12},{12... | collective-permute-start | bytes 1474568 | tf_op jit(solution)/shard_map/ppermute | solution.py:440
  20.4 125.4 %collective-permute-start.2 = (bf16[1,1,160,1536]{3,2,0,1:T(8,128)(2,1)}, bf16[1,1,160,1536]{3,2,0,1:T(8,128)(2,1)}, u32[]{:S(2)}, u32[]{:S(2)}) collective-permute-start(bf16[1,1,160,1536]{3,2,0,1:T(8,128)(2,1)} %get-tuple-element.355), channel_id=1, source_target_pairs={{0,4},{2,6},{4,0},{6,2},{1,5},{3,7},{5,1},{7,3},{8,12},{10,14},{12... | collective-permute-start | bytes 1474568 | tf_op jit(solution)/shard_map/ppermute | solution.py:440
  21.7 122.3 %collective-permute-start.1 = (bf16[1,1,160,1536]{3,2,0,1:T(8,128)(2,1)}, bf16[1,1,160,1536]{3,2,0,1:T(8,128)(2,1)}, u32[]{:S(2)}, u32[]{:S(2)}) collective-permute-start(bf16[1,1,160,1536]{3,2,0,1:T(8,128)(2,1)} %get-tuple-element.356), channel_id=1, source_target_pairs={{0,2},{2,0},{4,6},{6,4},{1,3},{3,1},{5,7},{7,5},{8,10},{10,8},{12,... | collective-permute-start | bytes 1474568 | tf_op jit(solution)/shard_map/ppermute | solution.py:440
  152.6 291.0 %all-gather.10.cloned.1.call-start = ((), (), s32[]{:S(2)}) async-start(), calls=%async_computation.5 | async-start | bytes 9830400 | tf_op jit(solution)/shard_map/all_gather | solution.py:603
  153.9 88.3 %collective-permute-start.15 = (bf16[192,2560]{1,0:T(8,128)(2,1)S(1)}, bf16[192,2560]{1,0:T(8,128)(2,1)}, u32[]{:S(2)}, u32[]{:S(2)}) collective-permute-start(bf16[192,2560]{1,0:T(8,128)(2,1)S(1)} %copy-done.16), channel_id=1, source_target_pairs={{0,4},{4,0},{1,5},{5,1},{2,6},{6,2},{3,7},{7,3},{8,12},{12,8},{9,1... | collective-permute-start | bytes 2949128 | tf_op jit(solution)/shard_map/ppermute | solution.py:309
  156.6 84.3 %collective-permute-start.20 = (bf16[1,1,160,1536]{3,2,0,1:T(8,128)(2,1)S(1)}, bf16[1,1,160,1536]{3,2,0,1:T(8,128)(2,1)S(1)}, u32[]{:S(2)}, u32[]{:S(2)}) collective-permute-start(bf16[1,1,160,1536]{3,2,0,1:T(8,128)(2,1)S(1)} %get-tuple-element.350), channel_id=1, source_target_pairs={{0,6},{2,4},{4,2},{6,0},{1,7},{3,5},{5,3},{7,1},{8,14},{10,12},{12... | collective-permute-start | bytes 1474568 | tf_op jit(solution)/shard_map/ppermute | solution.py:440
  172.0 8.3 collective-permute-start.4
  180.5 10.8 %collective-permute-start.5 = (bf16[2,32,1280]{2,1,0:T(8,128)(2,1)S(1)}, bf16[2,32,1280]{2,1,0:T(8,128)(2,1)S(1)}, u32[]{:S(2)}, u32[]{:S(2)}) collective-permute-start(bf16[2,32,1280]{2,1,0:T(8,128)(2,1)S(1)} %pad_maximum_fusion.22), channel_id=1, source_target_pairs={{0,4},{4,0},{1,5},{5,1},{2,6},{6,2},{3,7},{7,3},{8,12},{12,8},{9,1... | collective-permute-start | bytes 491528 | tf_op jit(solution)/shard_map/ppermute | solution.py:309
  192.0 19.9 %collective-permute-start.7 = (bf16[2,32,1280]{2,1,0:T(8,128)(2,1)S(1)}, bf16[2,32,1280]{2,1,0:T(8,128)(2,1)S(1)}, u32[]{:S(2)}, u32[]{:S(2)}) collective-permute-start(bf16[2,32,1280]{2,1,0:T(8,128)(2,1)S(1)} %pad_maximum_fusion.23), channel_id=1, source_target_pairs={{0,16},{8,24},{1,17},{9,25},{2,18},{10,26},{3,19},{11,27},{4,20},{... | collective-permute-start | bytes 491528 | tf_op jit(solution)/shard_map/ppermute | solution.py:490
  194.7 29.5 %collective-permute-start.6 = (bf16[2,32,1280]{2,1,0:T(8,128)(2,1)S(1)}, bf16[2,32,1280]{2,1,0:T(8,128)(2,1)S(1)}, u32[]{:S(2)}, u32[]{:S(2)}) collective-permute-start(bf16[2,32,1280]{2,1,0:T(8,128)(2,1)S(1)} %pad_maximum_fusion.23), channel_id=1, source_target_pairs={{0,8},{8,16},{16,24},{1,9},{9,17},{17,25},{2,10},{10,18},{18,26},{... | collective-permute-start | bytes 491528 | tf_op jit(solution)/shard_map/ppermute | solution.py:490
  196.7 43.4 %collective-permute-start.19 = (bf16[1,1,160,1536]{3,2,0,1:T(8,128)(2,1)S(1)}, bf16[1,1,160,1536]{3,2,0,1:T(8,128)(2,1)S(1)}, u32[]{:S(2)}, u32[]{:S(2)}) collective-permute-start(bf16[1,1,160,1536]{3,2,0,1:T(8,128)(2,1)S(1)} %get-tuple-element.351), channel_id=1, source_target_pairs={{0,4},{2,6},{4,0},{6,2},{1,5},{3,7},{5,1},{7,3},{8,12},{10,14},{12... | collective-permute-start | bytes 1474568 | tf_op jit(solution)/shard_map/ppermute | solution.py:440
  211.9 27.4 %collective-permute-start.18 = (bf16[1,1,160,1536]{3,2,0,1:T(8,128)(2,1)S(1)}, bf16[1,1,160,1536]{3,2,0,1:T(8,128)(2,1)S(1)}, u32[]{:S(2)}, u32[]{:S(2)}) collective-permute-start(bf16[1,1,160,1536]{3,2,0,1:T(8,128)(2,1)S(1)} %get-tuple-element.352), channel_id=1, source_target_pairs={{0,2},{2,0},{4,6},{6,4},{1,3},{3,1},{5,7},{7,5},{8,10},{10,8},{12,... | collective-permute-start | bytes 1474568 | tf_op jit(solution)/shard_map/ppermute | solution.py:440
  237.0 23.3 %collective-permute-start.9 = (bf16[192,2560]{1,0:T(8,128)(2,1)}, bf16[192,2560]{1,0:T(8,128)(2,1)}, u32[]{:S(2)}, u32[]{:S(2)}) collective-permute-start(bf16[192,2560]{1,0:T(8,128)(2,1)} %fusion.35), channel_id=1, source_target_pairs={{0,1},{1,0},{2,3},{3,2},{4,5},{5,4},{6,7},{7,6},{8,9},{9,8},{10,11... | collective-permute-start | bytes 2949128 | tf_op jit(solution)/shard_map/ppermute | solution.py:309
  241.8 341.4 %reduce-scatter.4.cloned.1.call-start = ((), (), s32[]{:S(2)}) async-start(), calls=%async_computation.6 | async-start | bytes 9830400 | tf_op jit(solution)/shard_map/reduce_scatter | solution.py:429
  242.2 93.6 %collective-permute-start.16 = (bf16[192,2560]{1,0:T(8,128)(2,1)}, bf16[192,2560]{1,0:T(8,128)(2,1)S(1)}, u32[]{:S(2)}, u32[]{:S(2)}) collective-permute-start(bf16[192,2560]{1,0:T(8,128)(2,1)} %collective-permute-done.15), channel_id=1, source_target_pairs={{0,1},{1,0},{2,3},{3,2},{4,5},{5,4},{6,7},{7,6},{8,9},{9,8},{10,11... | collective-permute-start | bytes 2949128 | tf_op jit(solution)/shard_map/ppermute | solution.py:309
  267.4 10.8 %collective-permute-start.10 = (bf16[96,2560]{1,0:T(8,128)(2,1)S(1)}, bf16[96,2560]{1,0:T(8,128)(2,1)S(1)}, u32[]{:S(2)}, u32[]{:S(2)}) collective-permute-start(bf16[96,2560]{1,0:T(8,128)(2,1)S(1)} %get-tuple-element.387), channel_id=1, source_target_pairs={{0,4},{4,0},{1,5},{5,1},{2,6},{6,2},{3,7},{7,3},{8,12},{12,8},{9,1... | collective-permute-start | bytes 1474568 | tf_op jit(solution)/shard_map/ppermute | solution.py:309
  278.2 22.7 %collective-permute-start.11 = (bf16[192,2560]{1,0:T(8,128)(2,1)S(1)}, bf16[192,2560]{1,0:T(8,128)(2,1)S(1)}, u32[]{:S(2)}, u32[]{:S(2)}) collective-permute-start(bf16[192,2560]{1,0:T(8,128)(2,1)S(1)} %pad_maximum_fusion.17), channel_id=1, source_target_pairs={{0,1},{1,0},{2,3},{3,2},{4,5},{5,4},{6,7},{7,6},{8,9},{9,8},{10,11... | collective-permute-start | bytes 2949128 | tf_op jit(solution)/shard_map/ppermute | solution.py:309
  301.1 10.1 %collective-permute-start.12 = (bf16[96,2560]{1,0:T(8,128)(2,1)S(1)}, bf16[96,2560]{1,0:T(8,128)(2,1)S(1)}, u32[]{:S(2)}, u32[]{:S(2)}) collective-permute-start(bf16[96,2560]{1,0:T(8,128)(2,1)S(1)} %get-tuple-element.385), channel_id=1, source_target_pairs={{0,1},{1,0},{2,3},{3,2},{4,5},{5,4},{6,7},{7,6},{8,9},{9,8},{10,11... | collective-permute-start | bytes 1474568 | tf_op jit(solution)/shard_map/ppermute | solution.py:309
  311.2 20.2 %collective-permute-start.13 = (bf16[192,2560]{1,0:T(8,128)(2,1)S(1)}, bf16[192,2560]{1,0:T(8,128)(2,1)S(1)}, u32[]{:S(2)}, u32[]{:S(2)}) collective-permute-start(bf16[192,2560]{1,0:T(8,128)(2,1)S(1)} %pad_maximum_fusion.18), channel_id=1, source_target_pairs={{0,4},{4,0},{1,5},{5,1},{2,6},{6,2},{3,7},{7,3},{8,12},{12,8},{9,1... | collective-permute-start | bytes 2949128 | tf_op jit(solution)/shard_map/ppermute | solution.py:309
  331.5 14.3 %collective-permute-start.14 = (bf16[768,2560]{1,0:T(8,128)(2,1)S(1)}, bf16[768,2560]{1,0:T(8,128)(2,1)S(1)}, u32[]{:S(2)}, u32[]{:S(2)}) collective-permute-start(bf16[768,2560]{1,0:T(8,128)(2,1)S(1)} %get-tuple-element.381), channel_id=1, source_target_pairs={{0,2},{2,0},{1,3},{3,1},{4,6},{6,4},{5,7},{7,5},{8,10},{10,8},{9,1... | collective-permute-start | bytes 11796488 | tf_op jit(solution)/shard_map/ppermute | solution.py:309
  342.5 40.7 %collective-permute-start.17 = (bf16[768,2560]{1,0:T(8,128)(2,1)}, bf16[768,2560]{1,0:T(8,128)(2,1)}, u32[]{:S(2)}, u32[]{:S(2)}) collective-permute-start(bf16[768,2560]{1,0:T(8,128)(2,1)} %get-tuple-element.375), channel_id=1, source_target_pairs={{0,2},{2,0},{1,3},{3,1},{4,6},{6,4},{5,7},{7,5},{8,10},{10,8},{9,1... | collective-permute-start | bytes 11796488 | tf_op jit(solution)/shard_map/ppermute | solution.py:309
  346.1 23.0 %collective-permute-start.24 = (bf16[384,1280]{1,0:T(8,128)(2,1)S(1)}, bf16[384,1280]{1,0:T(8,128)(2,1)S(1)}, u32[]{:S(2)}, u32[]{:S(2)}) collective-permute-start(bf16[384,1280]{1,0:T(8,128)(2,1)S(1)} %copy-done.4), channel_id=1, source_target_pairs={{0,4},{4,0},{1,5},{5,1},{2,6},{6,2},{3,7},{7,3},{8,12},{12,8},{9,1... | collective-permute-start | bytes 2949128 | tf_op jit(solution)/shard_map/ppermute | solution.py:309
  370.6 58.2 %collective-permute-start.25 = (bf16[768,1280]{1,0:T(8,128)(2,1)}, bf16[768,1280]{1,0:T(8,128)(2,1)}, u32[]{:S(2)}, u32[]{:S(2)}) collective-permute-start(bf16[768,1280]{1,0:T(8,128)(2,1)} %pad_maximum_fusion.8), channel_id=1, source_target_pairs={{0,2},{2,0},{1,3},{3,1},{4,6},{6,4},{5,7},{7,5},{8,10},{10,8},{9,1... | collective-permute-start | bytes 5898248 | tf_op jit(solution)/shard_map/ppermute | solution.py:309
  381.4 44.3 %collective-permute-start.23 = (bf16[4,160,384]{2,1,0:T(8,128)(2,1)}, bf16[4,160,384]{2,1,0:T(8,128)(2,1)}, u32[]{:S(2)}, u32[]{:S(2)}) collective-permute-start(bf16[4,160,384]{2,1,0:T(8,128)(2,1)} %get-tuple-element.347), channel_id=1, source_target_pairs={{0,6},{2,4},{4,2},{6,0},{1,7},{3,5},{5,3},{7,1},{8,14},{10,12},{12... | collective-permute-start | bytes 1474568 | tf_op jit(solution)/shard_map/ppermute | solution.py:389
  382.7 43.0 %collective-permute-start.22 = (bf16[4,160,384]{2,1,0:T(8,128)(2,1)}, bf16[4,160,384]{2,1,0:T(8,128)(2,1)}, u32[]{:S(2)}, u32[]{:S(2)}) collective-permute-start(bf16[4,160,384]{2,1,0:T(8,128)(2,1)} %get-tuple-element.348), channel_id=1, source_target_pairs={{0,2},{2,0},{4,6},{6,4},{1,3},{3,1},{5,7},{7,5},{8,10},{10,8},{12,... | collective-permute-start | bytes 1474568 | tf_op jit(solution)/shard_map/ppermute | solution.py:389
  383.2 42.5 %collective-permute-start.21 = (bf16[4,160,384]{2,1,0:T(8,128)(2,1)}, bf16[4,160,384]{2,1,0:T(8,128)(2,1)}, u32[]{:S(2)}, u32[]{:S(2)}) collective-permute-start(bf16[4,160,384]{2,1,0:T(8,128)(2,1)} %get-tuple-element.349), channel_id=1, source_target_pairs={{0,4},{2,6},{4,0},{6,2},{1,5},{3,7},{5,1},{7,3},{8,12},{10,14},{12... | collective-permute-start | bytes 1474568 | tf_op jit(solution)/shard_map/ppermute | solution.py:389
  424.9 320.0 %reduce-scatter.6.cloned.1.call-start = ((), (), s32[]{:S(2)}) async-start(), calls=%async_computation.7 | async-start | bytes 9830400 | tf_op jit(solution)/shard_map/reduce_scatter | solution.py:429
  475.3 13.4 %collective-permute-start.26 = (bf16[768,2560]{1,0:T(8,128)(2,1)}, bf16[768,2560]{1,0:T(8,128)(2,1)S(1)}, u32[]{:S(2)}, u32[]{:S(2)}) collective-permute-start(bf16[768,2560]{1,0:T(8,128)(2,1)} %shard_map.396), channel_id=1, source_target_pairs={{0,2},{2,0},{1,3},{3,1},{4,6},{6,4},{5,7},{7,5},{8,10},{10,8},{9,1... | collective-permute-start | bytes 11796488 | tf_op jit(solution)/shard_map/ppermute | solution.py:309
  492.5 23.5 %collective-permute-start.28 = (bf16[192,2560]{1,0:T(8,128)(2,1)S(1)}, bf16[192,2560]{1,0:T(8,128)(2,1)S(1)}, u32[]{:S(2)}, u32[]{:S(2)}) collective-permute-start(bf16[192,2560]{1,0:T(8,128)(2,1)S(1)} %bitcast.383), channel_id=1, source_target_pairs={{0,1},{1,0},{2,3},{3,2},{4,5},{5,4},{6,7},{7,6},{8,9},{9,8},{10,11... | collective-permute-start | bytes 2949128 | tf_op jit(solution)/shard_map/ppermute | solution.py:309
  495.1 23.4 %collective-permute-start.27 = (bf16[192,2560]{1,0:T(8,128)(2,1)}, bf16[192,2560]{1,0:T(8,128)(2,1)S(1)}, u32[]{:S(2)}, u32[]{:S(2)}) collective-permute-start(bf16[192,2560]{1,0:T(8,128)(2,1)} %bitcast.70), channel_id=1, source_target_pairs={{0,4},{4,0},{1,5},{5,1},{2,6},{6,2},{3,7},{7,3},{8,12},{12,8},{9,1... | collective-permute-start | bytes 2949128 | tf_op jit(solution)/shard_map/ppermute | solution.py:309
  518.9 12.0 %collective-permute-start.29 = (bf16[96,2560]{1,0:T(8,128)(2,1)S(1)}, bf16[96,2560]{1,0:T(8,128)(2,1)S(1)}, u32[]{:S(2)}, u32[]{:S(2)}) collective-permute-start(bf16[96,2560]{1,0:T(8,128)(2,1)S(1)} %slice.762), channel_id=1, source_target_pairs={{0,1},{1,0},{2,3},{3,2},{4,5},{5,4},{6,7},{7,6},{8,9},{9,8},{10,11... | collective-permute-start | bytes 1474568 | tf_op jit(solution)/shard_map/ppermute | solution.py:309
  519.3 11.7 %collective-permute-start.30 = (bf16[96,2560]{1,0:T(8,128)(2,1)S(1)}, bf16[96,2560]{1,0:T(8,128)(2,1)S(1)}, u32[]{:S(2)}, u32[]{:S(2)}) collective-permute-start(bf16[96,2560]{1,0:T(8,128)(2,1)S(1)} %slice.765), channel_id=1, source_target_pairs={{0,4},{4,0},{1,5},{5,1},{2,6},{6,2},{3,7},{7,3},{8,12},{12,8},{9,1... | collective-permute-start | bytes 1474568 | tf_op jit(solution)/shard_map/ppermute | solution.py:309
  533.7 26.6 %collective-permute-start.31 = (bf16[192,2560]{1,0:T(8,128)(2,1)S(1)}, bf16[192,2560]{1,0:T(8,128)(2,1)}, u32[]{:S(2)}, u32[]{:S(2)}) collective-permute-start(bf16[192,2560]{1,0:T(8,128)(2,1)S(1)} %get-tuple-element.274), channel_id=1, source_target_pairs={{0,1},{1,0},{2,3},{3,2},{4,5},{5,4},{6,7},{7,6},{8,9},{9,8},{10,11... | collective-permute-start | bytes 2949128 | tf_op jit(solution)/shard_map/ppermute | solution.py:309
  538.5 12.3 %collective-permute-start.34 = (bf16[4,160,192]{2,1,0:T(8,128)(2,1)}, bf16[4,160,192]{2,1,0:T(8,128)(2,1)S(1)}, u32[]{:S(2)}, u32[]{:S(2)}) collective-permute-start(bf16[4,160,192]{2,1,0:T(8,128)(2,1)} %get-tuple-element.364), channel_id=1, source_target_pairs={{0,6},{2,4},{4,2},{6,0},{1,7},{3,5},{5,3},{7,1},{8,14},{10,12},{12... | collective-permute-start | bytes 737288 | tf_op jit(solution)/shard_map/ppermute | solution.py:389
  542.0 8.9 %collective-permute-start.33 = (bf16[4,160,192]{2,1,0:T(8,128)(2,1)}, bf16[4,160,192]{2,1,0:T(8,128)(2,1)}, u32[]{:S(2)}, u32[]{:S(2)}) collective-permute-start(bf16[4,160,192]{2,1,0:T(8,128)(2,1)} %get-tuple-element.365), channel_id=1, source_target_pairs={{0,2},{2,0},{4,6},{6,4},{1,3},{3,1},{5,7},{7,5},{8,10},{10,8},{12,... | collective-permute-start | bytes 737288 | tf_op jit(solution)/shard_map/ppermute | solution.py:389
  542.0 15.9 %collective-permute-start.32 = (bf16[4,160,192]{2,1,0:T(8,128)(2,1)S(1)}, bf16[4,160,192]{2,1,0:T(8,128)(2,1)}, u32[]{:S(2)}, u32[]{:S(2)}) collective-permute-start(bf16[4,160,192]{2,1,0:T(8,128)(2,1)S(1)} %get-tuple-element.366), channel_id=1, source_target_pairs={{0,4},{2,6},{4,0},{6,2},{1,5},{3,7},{5,1},{7,3},{8,12},{10,14},{12... | collective-permute-start | bytes 737288 | tf_op jit(solution)/shard_map/ppermute | solution.py:389
  583.2 283.9 %reduce-scatter.8.cloned.1.call-start = ((), (), s32[]{:S(2)}) async-start(), calls=%async_computation.8 | async-start | bytes 6553600 | tf_op jit(solution)/shard_map/reduce_scatter | solution.py:413
  585.4 18.9 %collective-permute-start.36 = (bf16[2,32,1280]{2,1,0:T(8,128)(2,1)S(1)}, bf16[2,32,1280]{2,1,0:T(8,128)(2,1)S(1)}, u32[]{:S(2)}, u32[]{:S(2)}) collective-permute-start(bf16[2,32,1280]{2,1,0:T(8,128)(2,1)S(1)} %pad_maximum_fusion.24), channel_id=1, source_target_pairs={{0,4},{4,0},{1,5},{5,1},{2,6},{6,2},{3,7},{7,3},{8,12},{12,8},{9,1... | collective-permute-start | bytes 491528 | tf_op jit(solution)/shard_map/ppermute | solution.py:309
  604.3 37.1 %collective-permute-start.40 = (bf16[384,1280]{1,0:T(8,128)(2,1)S(1)}, bf16[384,1280]{1,0:T(8,128)(2,1)S(1)}, u32[]{:S(2)}, u32[]{:S(2)}) collective-permute-start(bf16[384,1280]{1,0:T(8,128)(2,1)S(1)} %get-tuple-element.156), channel_id=1, source_target_pairs={{0,4},{4,0},{1,5},{5,1},{2,6},{6,2},{3,7},{7,3},{8,12},{12,8},{9,1... | collective-permute-start | bytes 2949128 | tf_op jit(solution)/shard_map/ppermute | solution.py:309
  604.5 59.2 %collective-permute-start.45 = (bf16[768,2560]{1,0:T(8,128)(2,1)}, bf16[768,2560]{1,0:T(8,128)(2,1)}, u32[]{:S(2)}, u32[]{:S(2)}) collective-permute-start(bf16[768,2560]{1,0:T(8,128)(2,1)} %shard_map.400), channel_id=1, source_target_pairs={{0,2},{2,0},{1,3},{3,1},{4,6},{6,4},{5,7},{7,5},{8,10},{10,8},{9,1... | collective-permute-start | bytes 11796488 | tf_op jit(solution)/shard_map/ppermute | solution.py:309
  606.4 15.1 %collective-permute-start.38 = (bf16[2,32,1280]{2,1,0:T(8,128)(2,1)S(1)}, bf16[2,32,1280]{2,1,0:T(8,128)(2,1)S(1)}, u32[]{:S(2)}, u32[]{:S(2)}) collective-permute-start(bf16[2,32,1280]{2,1,0:T(8,128)(2,1)S(1)} %pad_maximum_fusion.25), channel_id=1, source_target_pairs={{16,0},{24,8},{17,1},{25,9},{18,2},{26,10},{19,3},{27,11},{20,4},{... | collective-permute-start | bytes 491528 | tf_op jit(solution)/shard_map/ppermute | solution.py:490
  607.7 33.6 %collective-permute-start.37 = (bf16[2,32,1280]{2,1,0:T(8,128)(2,1)S(1)}, bf16[2,32,1280]{2,1,0:T(8,128)(2,1)S(1)}, u32[]{:S(2)}, u32[]{:S(2)}) collective-permute-start(bf16[2,32,1280]{2,1,0:T(8,128)(2,1)S(1)} %pad_maximum_fusion.25), channel_id=1, source_target_pairs={{8,0},{16,8},{24,16},{9,1},{17,9},{25,17},{10,2},{18,10},{26,18},{... | collective-permute-start | bytes 491528 | tf_op jit(solution)/shard_map/ppermute | solution.py:490
  643.0 15.7 %collective-permute-start.41 = (bf16[768,1280]{1,0:T(8,128)(2,1)}, bf16[768,1280]{1,0:T(8,128)(2,1)}, u32[]{:S(2)}, u32[]{:S(2)}) collective-permute-start(bf16[768,1280]{1,0:T(8,128)(2,1)} %pad_maximum_fusion.10), channel_id=1, source_target_pairs={{0,2},{2,0},{1,3},{3,1},{4,6},{6,4},{5,7},{7,5},{8,10},{10,8},{9,1... | collective-permute-start | bytes 5898248 | tf_op jit(solution)/shard_map/ppermute | solution.py:309
  653.4 31.8 %collective-permute-start.44 = (bf16[640,768]{1,0:T(8,128)(2,1)}, bf16[640,768]{1,0:T(8,128)(2,1)}, u32[]{:S(2)}, u32[]{:S(2)}) collective-permute-start(bf16[640,768]{1,0:T(8,128)(2,1)} %pad_maximum_fusion.19), channel_id=1, source_target_pairs={{0,1},{1,0},{2,3},{3,2},{4,5},{5,4},{6,7},{7,6},{8,9},{9,8},{10,11... | collective-permute-start | bytes 2949128 | tf_op jit(solution)/shard_map/ppermute | solution.py:309
  657.4 10.2 %collective-permute-start.50 = (bf16[4,32,1280]{2,1,0:T(8,128)(2,1)S(1)}, bf16[4,32,1280]{2,1,0:T(8,128)(2,1)S(1)}, u32[]{:S(2)}, u32[]{:S(2)}) collective-permute-start(bf16[4,32,1280]{2,1,0:T(8,128)(2,1)S(1)} %dynamic-slice_bitcast_fusion.6), channel_id=1, source_target_pairs={{0,4},{4,0},{1,5},{5,1},{2,6},{6,2},{3,7},{7,3},{8,12},{12,8},{9,1... | collective-permute-start | bytes 983048 | tf_op jit(solution)/shard_map/ppermute | solution.py:309
  660.6 9.4 %collective-permute-start.42 = (bf16[96,1280]{1,0:T(8,128)(2,1)S(1)}, bf16[96,1280]{1,0:T(8,128)(2,1)S(1)}, u32[]{:S(2)}, u32[]{:S(2)}) collective-permute-start(bf16[96,1280]{1,0:T(8,128)(2,1)S(1)} %slice.1106), channel_id=1, source_target_pairs={{2,0},{4,2},{6,4},{8,6},{10,8},{12,10},{14,12},{16,14},{18,16},{20... | collective-permute-start | bytes 737288 | tf_op jit(solution)/shard_map/ppermute | solution.py:688
  667.3 51.4 %collective-permute-start.46 = (bf16[384,2560]{1,0:T(8,128)(2,1)S(1)}, bf16[384,2560]{1,0:T(8,128)(2,1)S(1)}, u32[]{:S(2)}, u32[]{:S(2)}) collective-permute-start(bf16[384,2560]{1,0:T(8,128)(2,1)S(1)} %pad_maximum_fusion.12), channel_id=1, source_target_pairs={{0,1},{1,0},{2,3},{3,2},{4,5},{5,4},{6,7},{7,6},{8,9},{9,8},{10,11... | collective-permute-start | bytes 5898248 | tf_op jit(solution)/shard_map/ppermute | solution.py:309
  670.5 32.4 %collective-permute-start.43 = (bf16[384,1280]{1,0:T(8,128)(2,1)S(1)}, bf16[384,1280]{1,0:T(8,128)(2,1)S(1)}, u32[]{:S(2)}, u32[]{:S(2)}) collective-permute-start(bf16[384,1280]{1,0:T(8,128)(2,1)S(1)} %fusion.55), channel_id=1, source_target_pairs={{0,4},{4,0},{1,5},{5,1},{2,6},{6,2},{3,7},{7,3},{8,12},{12,8},{9,1... | collective-permute-start | bytes 2949128 | tf_op jit(solution)/shard_map/ppermute | solution.py:309
  756.0 23.7 %collective-permute-start.52 = (bf16[192,2560]{1,0:T(8,128)(2,1)}, bf16[192,2560]{1,0:T(8,128)(2,1)}, u32[]{:S(2)}, u32[]{:S(2)}) collective-permute-start(bf16[192,2560]{1,0:T(8,128)(2,1)} %dynamic-slice_convert_fusion), channel_id=1, source_target_pairs={{0,1},{1,0},{2,3},{3,2},{4,5},{5,4},{6,7},{7,6},{8,9},{9,8},{10,11... | collective-permute-start | bytes 2949128 | tf_op jit(solution)/shard_map/ppermute | solution.py:309
  760.8 28.0 %collective-permute-start.47 = (bf16[192,2560]{1,0:T(8,128)(2,1)}, bf16[192,2560]{1,0:T(8,128)(2,1)}, u32[]{:S(2)}, u32[]{:S(2)}) collective-permute-start(bf16[192,2560]{1,0:T(8,128)(2,1)} %slice.799), channel_id=1, source_target_pairs={{0,4},{4,0},{1,5},{5,1},{2,6},{6,2},{3,7},{7,3},{8,12},{12,8},{9,1... | collective-permute-start | bytes 2949128 | tf_op jit(solution)/shard_map/ppermute | solution.py:309
  785.5 10.9 %collective-permute-start.57 = (f32[24,1280]{1,0:T(8,128)S(1)}, f32[24,1280]{1,0:T(8,128)S(1)}, u32[]{:S(2)}, u32[]{:S(2)}) collective-permute-start(f32[24,1280]{1,0:T(8,128)S(1)} %concatenate.237), channel_id=1, source_target_pairs={{0,6},{2,4},{4,2},{6,0},{1,7},{3,5},{5,3},{7,1},{8,14},{10,12},{12... | collective-permute-start | bytes 368648 | tf_op jit(solution)/shard_map/ppermute | solution.py:420
  788.3 8.1 collective-permute-start.56
  788.5 7.9 collective-permute-start.55
  794.9 26.7 %collective-permute-start.53 = (bf16[192,2560]{1,0:T(8,128)(2,1)}, bf16[192,2560]{1,0:T(8,128)(2,1)}, u32[]{:S(2)}, u32[]{:S(2)}) collective-permute-start(bf16[192,2560]{1,0:T(8,128)(2,1)} %get-tuple-element.336), channel_id=1, source_target_pairs={{0,1},{1,0},{2,3},{3,2},{4,5},{5,4},{6,7},{7,6},{8,9},{9,8},{10,11... | collective-permute-start | bytes 2949128 | tf_op jit(solution)/shard_map/ppermute | solution.py:309
  796.1 43.3 %collective-permute-start.48 = (bf16[192,2560]{1,0:T(8,128)(2,1)}, bf16[192,2560]{1,0:T(8,128)(2,1)}, u32[]{:S(2)}, u32[]{:S(2)}) collective-permute-start(bf16[192,2560]{1,0:T(8,128)(2,1)} %get-tuple-element.337), channel_id=1, source_target_pairs={{0,1},{1,0},{2,3},{3,2},{4,5},{5,4},{6,7},{7,6},{8,9},{9,8},{10,11... | collective-permute-start | bytes 2949128 | tf_op jit(solution)/shard_map/ppermute | solution.py:309
  796.5 13.3 %collective-permute-start.60 = (f32[24,1280]{1,0:T(8,128)S(1)}, f32[24,1280]{1,0:T(8,128)S(1)}, u32[]{:S(2)}, u32[]{:S(2)}) collective-permute-start(f32[24,1280]{1,0:T(8,128)S(1)} %add_add_fusion.2), channel_id=1, source_target_pairs={{0,24},{8,0},{16,8},{24,16},{1,25},{9,1},{17,9},{25,17},{2,26},{10... | collective-permute-start | bytes 368648 | tf_op jit(solution)/shard_map/ppermute | solution.py:425
  796.5 21.1 %collective-permute-start.59 = (f32[24,1280]{1,0:T(8,128)S(1)}, f32[24,1280]{1,0:T(8,128)S(1)}, u32[]{:S(2)}, u32[]{:S(2)}) collective-permute-start(f32[24,1280]{1,0:T(8,128)S(1)} %add_add_fusion.2), channel_id=1, source_target_pairs={{0,16},{8,24},{16,0},{24,8},{1,17},{9,25},{17,1},{25,9},{2,18},{10... | collective-permute-start | bytes 368648 | tf_op jit(solution)/shard_map/ppermute | solution.py:425
  796.6 21.1 %collective-permute-start.58 = (f32[24,1280]{1,0:T(8,128)S(1)}, f32[24,1280]{1,0:T(8,128)S(1)}, u32[]{:S(2)}, u32[]{:S(2)}) collective-permute-start(f32[24,1280]{1,0:T(8,128)S(1)} %add_add_fusion.2), channel_id=1, source_target_pairs={{0,8},{8,16},{16,24},{24,0},{1,9},{9,17},{17,25},{25,1},{2,10},{10... | collective-permute-start | bytes 368648 | tf_op jit(solution)/shard_map/ppermute | solution.py:425
  809.8 52.6 %collective-permute-start.63 = (bf16[1,2,160,1536]{3,2,1,0:T(8,128)(2,1)S(1)}, bf16[1,2,160,1536]{3,2,1,0:T(8,128)(2,1)S(1)}, u32[]{:S(2)}, u32[]{:S(2)}) collective-permute-start(bf16[1,2,160,1536]{3,2,1,0:T(8,128)(2,1)S(1)} %get-tuple-element.299), channel_id=1, source_target_pairs={{0,6},{2,4},{4,2},{6,0},{1,7},{3,5},{5,3},{7,1},{8,14},{10,12},{12... | collective-permute-start | bytes 2949128 | tf_op jit(solution)/shard_map/ppermute | solution.py:440
  817.6 43.4 %collective-permute-start.62 = (bf16[1,2,160,1536]{3,2,1,0:T(8,128)(2,1)S(1)}, bf16[1,2,160,1536]{3,2,1,0:T(8,128)(2,1)}, u32[]{:S(2)}, u32[]{:S(2)}) collective-permute-start(bf16[1,2,160,1536]{3,2,1,0:T(8,128)(2,1)S(1)} %get-tuple-element.300), channel_id=1, source_target_pairs={{0,4},{2,6},{4,0},{6,2},{1,5},{3,7},{5,1},{7,3},{8,12},{10,14},{12... | collective-permute-start | bytes 2949128 | tf_op jit(solution)/shard_map/ppermute | solution.py:440
  817.7 26.1 %collective-permute-start.61 = (bf16[1,2,160,1536]{3,2,1,0:T(8,128)(2,1)}, bf16[1,2,160,1536]{3,2,1,0:T(8,128)(2,1)}, u32[]{:S(2)}, u32[]{:S(2)}) collective-permute-start(bf16[1,2,160,1536]{3,2,1,0:T(8,128)(2,1)} %get-tuple-element.301), channel_id=1, source_target_pairs={{0,2},{2,0},{4,6},{6,4},{1,3},{3,1},{5,7},{7,5},{8,10},{10,8},{12,... | collective-permute-start | bytes 2949128 | tf_op jit(solution)/shard_map/ppermute | solution.py:440
  (98 other events, 663.1 us)
Sparse Core Ops, SparseCore 0:
  10.2 129.8 all-gather.5
  152.8 148.8 all-gather.7
  303.3 140.3 all-gather.9
  445.8 137.3 reduce-scatter.3
  585.4 151.6 reduce-scatter.5
  762.2 102.0 reduce-scatter.7
